TPU v7x, 256 devices: a whole 4x4x8 slice. The times are simulated.
256 devices in a mesh: role: 2 (over z_hi), dp: 8 (over x, core), fsdp: 16 (over y, z_lo).
Axes of the slice: x: 4, y: 4, z: 8 (z_hi: 2, z_lo: 4; z = z_hi * 4 + z_lo), core: 2. Of those that a mesh axis runs over, the one named last changes fastest.
Arguments:
- rows: bfloat16 [128, 256, 2048], P(('dp', 'fsdp'), 'role'), may hold values from -40 to 40
- cotangent: bfloat16 [128, 256, 2048], P(('dp', 'fsdp'), 'role'), may hold values from -6 to 6
- advantage: float32 [128, 256], P(('dp', 'fsdp'), 'role'), may hold values from -4 to 4
- action: int32 [128, 256], P(('dp', 'fsdp'), 'role'), may hold values 0 or 1
- norm_gain: float32 [2048], replicated, may hold values from 0.5 to 1.5
- q_gain: float32 [128], replicated, may hold values from 0.6 to 5.2
- k_gain: float32 [128], replicated, may hold values from 0.6 to 5.2
- w_q: bfloat16 [2048, 2048], P('fsdp', 'role'), may hold values from -0.1016466 to 0.1016466
- w_k: bfloat16 [2048, 512], P('fsdp', 'role'), may hold values from -0.1016466 to 0.1016466
- w_v: bfloat16 [2048, 512], P('fsdp', 'role'), may hold values from -0.125 to 0.125
- w_o: bfloat16 [2048, 2048], P('role', 'fsdp'), may hold values from -0.125 to 0.125
Outputs:
- out_rows: bfloat16 [128, 256, 2048], P(('dp', 'fsdp'), 'role')
- grad_rows: bfloat16 [128, 256, 2048], P(('dp', 'fsdp'), 'role')
- grad_w_q: float32 [2048, 2048], P('fsdp', 'role')
- grad_w_k: float32 [2048, 512], P('fsdp', 'role')
- grad_w_v: float32 [2048, 512], P('fsdp', 'role')
- grad_w_o: float32 [2048, 2048], P('role', 'fsdp')
All inputs are finite; a program needn't handle non-finite values. No bound on the sum of `action` on one device may be relied on, other than what follows from the above.
Results may differ from a plain program's by a relative error of at most 0.04.
The roundings to bfloat16 on the way count: a program that leaves them out, or rounds other values in their place, can miss the bound.
Values may be sent and summed in bfloat16 or wider, within the bound.
No kernel may reach another device: no remote copies, remote signals or barrier semaphores. Data moves between devices by JAX's collectives and lax.ppermute only.
A program may use at most 128 MiB of HBM per device.

v0:
```python
import jax
import jax.numpy as jnp
from jax import lax
from jax.experimental import pallas as pl
from jax.experimental.pallas import tpu as pltpu
from jax.sharding import PartitionSpec as P

HD = 128
TRAJ = 128
NX = 4
NC = 2
NY = 4
NZ = 4

eps_norm = 1e-06
theta_base = 1000000.0
f32 = jnp.float32
bf16 = jnp.bfloat16


def dims(a, b, left, right):
    return lax.dot_general(left, right, (((a,), (b,)), ((), ())), preferred_element_type=f32)


def dot(left, right):
    return dims(1, 0, left, right)


def dot_rows(left, right):
    return dims(1, 1, left, right)


def dot_cols(left, right):
    return dims(0, 0, left, right)


def call(kernel, outs, vmem, scalars=1, macs=0, **more):
    return pl.pallas_call(
        kernel,
        cost_estimate=pl.CostEstimate(
            flops=2 * macs,
            bytes_accessed=sum(shape[0] * shape[1] for shape, _ in outs) * 2,
            transcendentals=0,
        ),
        out_shape=[jax.ShapeDtypeStruct(shape, kind) for shape, kind in outs],
        in_specs=[pl.BlockSpec(memory_space=pltpu.SMEM)] * scalars
        + [pl.BlockSpec(memory_space=pltpu.VMEM)] * (vmem - scalars),
        out_specs=[pl.BlockSpec(memory_space=pltpu.VMEM)] * len(outs),
        compiler_params=pltpu.CompilerParams(vmem_limit_bytes=40 << 20),
        **more,
    )


def turned(place_ref, j):
    row = lax.rem(place_ref[0] + j // NZ, NY)
    col = lax.rem(place_ref[1] + j % NZ, NZ)
    return pl.ds(pl.multiple_of((row * NZ + col) * HD, HD), HD)


def norm_kernel(place_ref, rows_ref, gain_ref, normed_ref):
    x = rows_ref[...].astype(f32)
    inv = lax.rsqrt(jnp.mean(x * x, axis=-1, keepdims=True) + eps_norm)
    for j in range(NY * NZ):
        at = turned(place_ref, j)
        normed_ref[:, j * HD : (j + 1) * HD] = (
            rows_ref[:, at].astype(f32) * inv * gain_ref[:, at]
        ).astype(bf16)


def weigh_kernel(place_ref, cot_ref, weight_ref, grad_ref):
    weight = weight_ref[...]
    for j in range(NY * NZ):
        at = turned(place_ref, j)
        grad_ref[:, j * HD : (j + 1) * HD] = (cot_ref[:, at].astype(f32) * weight).astype(bf16)


def finish_kernel(
    place_ref, rows_ref, gain_ref, cot_ref, weight_ref, mixed_ref, back_ref, out_ref, grad_ref, scaled_ref
):
    for j in range(NY * NZ):
        at = turned(place_ref, j)
        cols = slice(j * HD, (j + 1) * HD)
        out_ref[:, at] = (rows_ref[:, at].astype(f32) + mixed_ref[:, cols].astype(f32)).astype(bf16)
        scaled_ref[:, at] = back_ref[:, cols].astype(f32) * gain_ref[:, at]
    x = rows_ref[...].astype(f32)
    inv = lax.rsqrt(jnp.mean(x * x, axis=-1, keepdims=True) + eps_norm)
    scaled = scaled_ref[...]
    unit = x * inv
    mean = jnp.mean(scaled * unit, axis=-1, keepdims=True)
    grad_out = (cot_ref[...].astype(f32) * weight_ref[...]).astype(bf16).astype(f32)
    grad_ref[...] = (grad_out + inv * (scaled - unit * mean)).astype(bf16)


def project_kernel(normed_ref, *refs):
    own, other, outs = refs[:NY], refs[NY : 2 * NY], refs[2 * NY :]
    for chunks, out_ref in zip((own, other), outs):
        total = None
        for j in range(NY):
            span = chunks[j].shape[0]
            term = dot(normed_ref[:, j * span : (j + 1) * span], chunks[j][...])
            total = term if total is None else total + term
        out_ref[...] = total.astype(out_ref.dtype)


def expand_kernel(left_own_ref, left_other_ref, *refs):
    own, other, out_ref = refs[:NY], refs[NY : 2 * NY], refs[2 * NY]
    for j in range(NY):
        span = own[j].shape[0]
        total = dot_rows(left_own_ref[...], own[j][...])
        total = total + dot_rows(left_other_ref[...], other[j][...])
        out_ref[:, j * span : (j + 1) * span] = total.astype(bf16)


def rotate(t, cos, sin):
    return t * cos + pltpu.roll(t, HD // 2, 1) * sin


def rotate_back(g, cos, sin):
    return g * cos + pltpu.roll(g * sin, HD // 2, 1)


def inv_norm(t):
    return lax.rsqrt(jnp.mean(t * t, axis=-1, keepdims=True) + eps_norm)


def norm_back(t, grad, gain):
    r = inv_norm(t)
    u = grad * gain
    return r * u - t * (r * r * r * jnp.mean(t * u, axis=-1, keepdims=True))


def stack_heads(own_ref, other_ref):
    return jnp.concatenate(
        [ref[:, k * HD : (k + 1) * HD] for ref in (own_ref, other_ref) for k in range(2)], axis=0
    )


def attend_kernel(
    first_ref, own_ref, other_ref, q_gain_ref, k_gain_ref, cos_ref, sin_ref,
    q_rot_ref, k_rot_ref, value_ref, probs_ref, mixed_own_ref, mixed_other_ref,
):
    cos, sin = cos_ref[...], sin_ref[...]
    cos4, sin4 = jnp.concatenate([cos] * 4, axis=0), jnp.concatenate([sin] * 4, axis=0)
    first = first_ref[0] == 1
    tail_own, tail_other = own_ref[:, 2 * HD :], other_ref[:, 2 * HD :]
    keys = jnp.where(first, tail_own, tail_other)
    value = jnp.where(first, tail_other, tail_own).astype(bf16)
    query = stack_heads(own_ref, other_ref)
    q_rot = rotate(query * inv_norm(query) * q_gain_ref[...], cos4, sin4).astype(bf16)
    k_rot = rotate(keys * inv_norm(keys) * k_gain_ref[...], cos, sin).astype(bf16)
    scores = dot_rows(q_rot, k_rot) * HD ** (-0.5)
    row = lax.broadcasted_iota(jnp.int32, scores.shape, 0) % TRAJ
    allowed = row >= lax.broadcasted_iota(jnp.int32, scores.shape, 1)
    scores = jnp.where(allowed, scores, -1e30)
    peak = jnp.max(scores, axis=-1, keepdims=True)
    weights = jnp.where(allowed, jnp.exp(scores - peak), 0.0)
    probs = weights / jnp.sum(weights, axis=-1, keepdims=True)
    mixed = dot(probs.astype(bf16), value).astype(bf16)
    q_rot_ref[...] = q_rot
    k_rot_ref[...] = k_rot
    value_ref[...] = value
    probs_ref[...] = probs
    for k in range(2):
        mixed_own_ref[:, k * HD : (k + 1) * HD] = mixed[k * TRAJ : (k + 1) * TRAJ]
        mixed_other_ref[:, k * HD : (k + 1) * HD] = mixed[(k + 2) * TRAJ : (k + 3) * TRAJ]


def attend_back_kernel(
    first_ref, own_ref, other_ref, q_gain_ref, k_gain_ref, cos_ref, sin_ref,
    q_rot_ref, k_rot_ref, value_ref, probs_ref, gm_own_ref, gm_other_ref,
    g_own_ref, g_other_ref,
):
    cos, sin = cos_ref[...], sin_ref[...]
    cos4, sin4 = jnp.concatenate([cos] * 4, axis=0), jnp.concatenate([sin] * 4, axis=0)
    first = first_ref[0] == 1
    keys = jnp.where(first, own_ref[:, 2 * HD :], other_ref[:, 2 * HD :])
    query = stack_heads(own_ref, other_ref)
    grad_mixed = stack_heads(gm_own_ref, gm_other_ref)
    q_rot, k_rot, value, probs = q_rot_ref[...], k_rot_ref[...], value_ref[...], probs_ref[...]
    grad_probs = dot_rows(grad_mixed, value)
    grad_value = dot_cols(probs.astype(bf16), grad_mixed).astype(bf16)
    inner = jnp.sum(grad_probs * probs, axis=-1, keepdims=True)
    grad_scores = (probs * (grad_probs - inner) * HD ** (-0.5)).astype(bf16)
    grad_q_rot = dot(grad_scores, k_rot)
    grad_k_rot = dot_cols(grad_scores, q_rot)
    grad_query = norm_back(query, rotate_back(grad_q_rot, cos4, sin4), q_gain_ref[...]).astype(bf16)
    grad_keys = norm_back(keys, rotate_back(grad_k_rot, cos, sin), k_gain_ref[...]).astype(bf16)
    for k in range(2):
        g_own_ref[:, k * HD : (k + 1) * HD] = grad_query[k * TRAJ : (k + 1) * TRAJ]
        g_other_ref[:, k * HD : (k + 1) * HD] = grad_query[(k + 2) * TRAJ : (k + 3) * TRAJ]
    g_own_ref[:, 2 * HD :] = jnp.where(first, grad_keys, grad_value)
    g_other_ref[:, 2 * HD :] = jnp.where(first, grad_value, grad_keys)


def by_trajectory(kernel, outs, ins):
    def spec(rows, cols):
        if rows == 0:
            return pl.BlockSpec(cols, lambda i: (0, 0))
        return pl.BlockSpec((rows, cols), lambda i: (i, 0))

    return pl.pallas_call(
        kernel,
        cost_estimate=pl.CostEstimate(
            flops=2 * 8 * NX * TRAJ * TRAJ * HD * 4, bytes_accessed=1 << 20, transcendentals=0
        ),
        grid=(NX,),
        out_shape=[jax.ShapeDtypeStruct((rows * NX, cols), kind) for rows, cols, kind in outs],
        in_specs=[pl.BlockSpec(memory_space=pltpu.SMEM)] + [spec(*entry) for entry in ins],
        out_specs=[spec(rows, cols) for rows, cols, _ in outs],
        compiler_params=pltpu.CompilerParams(vmem_limit_bytes=40 << 20),
    )


def weight_grad_kernel(left_ref, own_ref, other_ref, *refs):
    outs, other_out = refs[:NY], refs[NY]
    for j in range(NY):
        span = outs[j].shape[0]
        left = left_ref[:, j * span : (j + 1) * span]
        other_out[j * span : (j + 1) * span] = dot_cols(left, other_ref[...]).astype(bf16)
        outs[j][...] = dot_cols(left, own_ref[...]).astype(bf16)


def grad_o_kernel(place_ref, left_ref, own_ref, other_ref, own_out, other_out):
    span = NZ * HD
    for j in range(NY):
        left = left_ref[:, j * span : (j + 1) * span]
        at = pl.ds(pl.multiple_of(lax.rem(place_ref[0] + j, NY) * span, span), span)
        other_out[at] = dot_cols(left, other_ref[...]).astype(bf16)
        own_out[at] = dot_cols(left, own_ref[...]).astype(bf16)


def rope_tables():
    position = jnp.arange(TRAJ, dtype=jnp.int32).astype(f32)
    inverse = jnp.exp(
        jnp.arange(HD // 2, dtype=f32) * (-2.0 * jnp.log(jnp.float32(theta_base)) / HD)
    )
    angles = position[:, None] * inverse[None, :]
    cos, sin = jnp.cos(angles), jnp.sin(angles)
    return jnp.concatenate([cos, cos], axis=1), jnp.concatenate([-sin, sin], axis=1)


def after(values, *earlier):
    alone = not isinstance(values, (list, tuple))
    values = (values,) if alone else tuple(values)
    held = lax.optimization_barrier(values + earlier)[: len(values)]
    return held[0] if alone else list(held)


SAME_CORE = [[x * NC + c for x in range(NX)] for c in range(NC)]


def gather_x(value):
    return lax.all_gather(value, "dp", axis=0, tiled=True, axis_index_groups=SAME_CORE)


SAME_Z = [[y * NZ + z for y in range(NY)] for z in range(NZ)]


def scatter_y(value):
    return lax.psum_scatter(
        value, "fsdp", scatter_dimension=0, tiled=True, axis_index_groups=SAME_Z
    )


def scatter_x(value):
    return lax.psum_scatter(
        value, "dp", scatter_dimension=0, tiled=True, axis_index_groups=SAME_CORE
    )


def take_y(value, step):
    pairs = [(y * NZ + z, (y - step) % NY * NZ + z) for y in range(NY) for z in range(NZ)]
    return lax.ppermute(value, "fsdp", pairs)


def take_z(value, step):
    pairs = [(y * NZ + z, y * NZ + (z - step) % NZ) for y in range(NY) for z in range(NZ)]
    return lax.ppermute(value, "fsdp", pairs)


def other_core(value):
    return lax.ppermute(value, "dp", [(i, i ^ 1) for i in range(NX * NC)])


def owner_role(x):
    return x // (NX // 2)


def from_owner(value):
    n = NX * NC
    pairs = [(owner_role(d // NC) * n + d, (1 - owner_role(d // NC)) * n + d) for d in range(n)]
    return lax.ppermute(value, ("role", "dp"), pairs)


def to_owner(value):
    n = NX * NC
    pairs = [((1 - owner_role(d // NC)) * n + d, owner_role(d // NC) * n + d) for d in range(n)]
    return lax.ppermute(value, ("role", "dp"), pairs)


def spread_x(value, step):
    n = NX * NC
    pairs = [
        (owner_role(x) * n + x * NC + c, owner_role(x) * n + (x - step) % NX * NC + c)
        for x in range(NX)
        for c in range(NC)
    ]
    return lax.ppermute(value, ("role", "dp"), pairs)


def over_role(block, at_owner):
    return jnp.where(at_owner, block, from_owner(block))


def over_z(block):
    return jnp.concatenate([block] + [take_z(block, k) for k in range(1, NZ)], axis=0)


def over_y(plane):
    return [plane] + [take_y(plane, k) for k in range(1, NY)]


def add_core(own, theirs):
    span = own[0].shape[0]
    return [
        (own[k].astype(f32) + theirs[k * span : (k + 1) * span].astype(f32)).astype(bf16)
        for k in range(NY)
    ]


def add_y(terms):
    total = terms[0].astype(f32)
    for term in terms[1:]:
        total = total + term.astype(f32)
    span = total.shape[0] // NZ
    return [total[k * span : (k + 1) * span].astype(bf16) for k in range(NZ)]


def add_z(terms):
    total = terms[0].astype(f32)
    for k in range(1, NZ):
        total = total + take_z(terms[k], -k).astype(f32)
    return total.astype(bf16)


def add_role(term):
    return (term.astype(f32) + to_owner(term).astype(f32)).astype(bf16)


def share(total, x, role, *earlier):
    copies = [total] + after([spread_x(total, k) for k in range(1, NX)], *earlier)
    items = []
    for sub in range(2):
        source = role * 2 + sub
        item = copies[0]
        for k in range(1, NX):
            item = jnp.where((source - x) % NX == k, copies[k], item)
        items.append(item)
    mine = jnp.concatenate(items, axis=0)
    return mine, other_core(mine)


def on_device(rows, cotangent, advantage, action, norm_gain, q_gain, k_gain, w_q, w_k, w_v, w_o):
    role = lax.axis_index("role")
    dp = lax.axis_index("dp")
    fsdp = lax.axis_index("fsdp")
    x, core = dp // NC, dp % NC
    y, z = fsdp // NZ, fsdp % NZ
    at_owner = role == owner_role(x)
    sub = x % 2
    width = 4 * HD
    half = 2 * HD
    first = core == 0
    place = jnp.stack([y, z]).astype(jnp.int32)
    flag = first.astype(jnp.int32)[None]

    q_part = lax.dynamic_slice(w_q, (0, sub * width + core * half), (HD, half))
    k_part = lax.dynamic_slice(w_k, (0, sub * HD), (HD, HD))
    v_part = lax.dynamic_slice(w_v, (0, sub * HD), (HD, HD))
    o_part = lax.dynamic_slice(w_o, (sub * width + core * half, 0), (half, HD)).T
    wide = half + HD
    kv_part = jnp.where(first, k_part, v_part)
    block_part = jnp.concatenate([q_part, kv_part, o_part], axis=1)
    block = over_role(block_part, at_owner)
    qkv_plane = over_z(block[:, :wide])

    rows_own, cot_own = rows[0], cotangent[0]
    gain = norm_gain[None]
    weight = (advantage[0] * action[0].astype(f32))[:, None]
    flat = (TRAJ, rows_own.shape[1])
    normed_own = call(norm_kernel, [(flat, bf16)], 3)(place, after(rows_own, block_part), gain)[0]
    normed = gather_x(normed_own)
    cot_late = after(cot_own, block)
    grad_turned = call(weigh_kernel, [(flat, bf16)], 3)(place, cot_late, weight)[0]
    grad_all = gather_x(grad_turned)

    qkv_own = over_y(qkv_plane)
    qkv_first = other_core(qkv_plane)
    o_plane = over_z(after(block[:, wide:], qkv_first))
    o_first = other_core(o_plane)
    qkv_other = [qkv_first] + [other_core(after(piece, o_first)) for piece in qkv_own[1:]]
    o_late = after(o_plane, *qkv_own)
    o_near = [take_y(o_late, 1), take_y(o_late, 3)]

    tokens = normed.shape[0]
    cos_tab, sin_tab = rope_tables()
    proj_own, proj_other = call(
        project_kernel, [((tokens, wide), f32)] * 2, 1 + 2 * NY, scalars=0, macs=tokens * flat[1] * 2 * wide
    )(normed, *qkv_own, *qkv_other)
    o_own = [o_plane, o_near[0], take_y(after(o_plane, proj_own), 2), o_near[1]]
    o_other = [o_first] + [other_core(piece) for piece in o_own[1:]]
    proj_own, proj_other = after([proj_own, proj_other], *o_near)
    shared = [(0, (1, HD)), (0, (1, HD)), (0, (TRAJ, HD)), (0, (TRAJ, HD))]
    tables = (q_gain[None], k_gain[None], cos_tab, sin_tab)
    kept = [(width, HD, bf16), (TRAJ, HD, bf16), (TRAJ, HD, bf16), (width, HD, f32)]
    q_rot, k_rot, value, probs, mixed_own, mixed_other = by_trajectory(
        attend_kernel,
        kept + [(TRAJ, half, bf16)] * 2,
        [(TRAJ, wide)] * 2 + shared,
    )(flag, proj_own, proj_other, *tables)

    span = NZ * HD
    go_own, go_cross = call(
        grad_o_kernel, [((NY * span, half), bf16)] * 2, 4, macs=tokens * flat[1] * width
    )(place, after(grad_all, o_own[2], o_other[1], o_other[3]), mixed_own, mixed_other)
    gm_own, gm_other = call(
        project_kernel, [((tokens, half), bf16)] * 2, 1 + 2 * NY, scalars=0, macs=tokens * flat[1] * width
    )(after(grad_all, go_cross), *o_own, *o_other)
    go_theirs = after(other_core(go_cross), gm_own)
    go_terms = scatter_y((go_own.astype(f32) + go_theirs.astype(f32)).astype(bf16))
    g_own, g_other = by_trajectory(
        attend_back_kernel,
        [(TRAJ, wide, bf16)] * 2,
        [(TRAJ, wide)] * 2 + shared + [entry[:2] for entry in kept] + [(TRAJ, half)] * 2,
    )(flag, proj_own, proj_other, *tables, q_rot, k_rot, value, probs, *after([gm_own, gm_other], go_theirs))
    *gw_own, gw_cross = call(
        weight_grad_kernel,
        [((span, wide), bf16)] * NY + [((NY * span, wide), bf16)],
        3,
        scalars=0,
    )(normed, g_own, g_other)
    gw_theirs = other_core(gw_cross)
    spread = ((tokens, flat[1]), bf16)
    part_out = call(expand_kernel, [spread], 2 + 2 * NY, scalars=0, macs=tokens * flat[1] * width)(
        *after([mixed_own, mixed_other], gw_cross), *o_own, *o_other
    )[0]
    gw_terms = after(add_core(gw_own, gw_theirs), part_out)
    gw_near = [take_y(gw_terms[1], -1), take_y(gw_terms[3], -3)]
    back = call(expand_kernel, [spread], 2 + 2 * NY, scalars=0, macs=tokens * flat[1] * 2 * wide)(
        *after([g_own, g_other], *gw_near), *qkv_own, *qkv_other
    )[0]
    out_total = scatter_x(part_out)
    back_total = scatter_x(back)

    go_terms = after(go_terms, *gw_near)
    go_term = add_z([go_terms[k * HD : (k + 1) * HD] for k in range(NZ)])
    gw_far = take_y(after(gw_terms[2], *gw_near), -2)
    gw_terms = add_y([gw_terms[0], *gw_near, after(gw_far, go_term)])
    gw_term = add_z(gw_terms)
    out_rows, grad_rows = call(
        finish_kernel, [(flat, bf16)] * 2, 7, scratch_shapes=[pltpu.VMEM(flat, f32)]
    )(place, rows_own, gain, cot_own, weight, out_total, back_total)
    total = add_role(jnp.concatenate([gw_term, go_term], axis=1))
    mine, theirs = share(after(total, out_total), x, role, grad_rows)
    g_0, g_1 = jnp.where(first, mine, theirs), jnp.where(first, theirs, mine)

    def pick(value, item, lo, hi):
        return value[item * HD : (item + 1) * HD, lo:hi].astype(f32)

    grad_w_q = jnp.concatenate(
        [pick(g, item, 0, half) for item in range(2) for g in (g_0, g_1)], axis=1
    )
    grad_w_k = jnp.concatenate([pick(g_0, item, half, wide) for item in range(2)], axis=1)
    grad_w_v = jnp.concatenate([pick(g_1, item, half, wide) for item in range(2)], axis=1)
    grad_w_o = jnp.concatenate(
        [pick(g, item, wide, wide + half).T for item in range(2) for g in (g_0, g_1)], axis=0
    )
    return (out_rows[None], grad_rows[None], grad_w_q, grad_w_k, grad_w_v, grad_w_o)


def solution(mesh):
    in_specs = (
        P(("dp", "fsdp"), "role", None),
        P(("dp", "fsdp"), "role", None),
        P(("dp", "fsdp"), "role"),
        P(("dp", "fsdp"), "role"),
        P(),
        P(),
        P(),
        P("fsdp", "role"),
        P("fsdp", "role"),
        P("fsdp", "role"),
        P("role", "fsdp"),
    )
    out_specs = (
        P(("dp", "fsdp"), "role", None),
        P(("dp", "fsdp"), "role", None),
        P("fsdp", "role"),
        P("fsdp", "role"),
        P("fsdp", "role"),
        P("role", "fsdp"),
    )
    return jax.shard_map(
        on_device, mesh=mesh, in_specs=in_specs, out_specs=out_specs, check_vma=False
    )
```

profile of v0, /device:TPU:1, one launch (start us, length us, event | category | flops | bytes accessed | tf_op | source)
XLA Modules:
  0.0 237.3 jit_solution(67291449859786338)
XLA Ops:
  13.4 9.7 %collective-permute-start = (bf16[128,640]{1,0:T(8,128)(2,1)S(1)}, bf16[128,640]{1,0:T(8,128)(2,1)S(1)}, u32[]{:S(2)}, u32[]{:S(2)}) collective-permute-start(bf16[128,640]{1,0:T(8,128)(2,1)S(1)} %pad_maximum_fusion.2), channel_id=1, source_target_pairs={{0,128},{16,144},{32,160},{48,176},{192,64},{208,80},{224,96},{240... | collective-permute-start | bytes 491528 | tf_op jit(solution)/shard_map/ppermute | solution.py:292
  23.3 2.7 %collective-permute-done = bf16[128,640]{1,0:T(8,128)(2,1)S(1)} collective-permute-done((bf16[128,640]{1,0:T(8,128)(2,1)S(1)}, bf16[128,640]{1,0:T(8,128)(2,1)S(1)}, u32[]{:S(2)}, u32[]{:S(2)}) %collective-permute-start) | collective-permute-done | bytes 163872 | tf_op jit(solution)/shard_map/ppermute | solution.py:292
  27.7 4.5 %collective-permute-start.3 = (bf16[128,384]{1,0:T(8,128)(2,1)S(1)}, bf16[128,384]{1,0:T(8,128)(2,1)S(1)}, u32[]{:S(2)}, u32[]{:S(2)}) collective-permute-start(bf16[128,384]{1,0:T(8,128)(2,1)S(1)} %slice.108), channel_id=1, source_target_pairs={{0,1},{1,2},{2,3},{3,0},{4,5},{5,6},{6,7},{7,4},{8,9},{9,10},{10,1... | collective-permute-start | bytes 294920 | tf_op jit(solution)/shard_map/ppermute | solution.py:278
  35.0 3.0 %collective-permute-done.2 = bf16[128,384]{1,0:T(8,128)(2,1)S(1)} collective-permute-done((bf16[128,384]{1,0:T(8,128)(2,1)S(1)}, bf16[128,384]{1,0:T(8,128)(2,1)S(1)}, u32[]{:S(2)}, u32[]{:S(2)}) %collective-permute-start.2) | collective-permute-done | bytes 98336 | tf_op jit(solution)/shard_map/ppermute | solution.py:278
  38.0 3.5 %collective-permute-start.7 = (bf16[512,384]{1,0:T(8,128)(2,1)S(1)}, bf16[512,384]{1,0:T(8,128)(2,1)S(1)}, u32[]{:S(2)}, u32[]{:S(2)}) collective-permute-start(bf16[512,384]{1,0:T(8,128)(2,1)S(1)} %pad_maximum_fusion.refs_0_), channel_id=1, source_target_pairs={{0,16},{16,0},{32,48},{48,32},{64,80},{80,64},{96,112},{112,96},{1... | collective-permute-start | bytes 1179656 | tf_op jit(solution)/shard_map/ppermute | solution.py:282
  41.5 2.8 %collective-permute-start.4 = (bf16[512,384]{1,0:T(8,128)(2,1)S(1)}, bf16[512,384]{1,0:T(8,128)(2,1)S(1)}, u32[]{:S(2)}, u32[]{:S(2)}) collective-permute-start(bf16[512,384]{1,0:T(8,128)(2,1)S(1)} %pad_maximum_fusion.refs_0_), channel_id=1, source_target_pairs={{0,12},{1,13},{2,14},{3,15},{4,0},{5,1},{6,2},{7,3},{8,4},{9,5},{1... | collective-permute-start | bytes 1179656 | tf_op jit(solution)/shard_map/ppermute | solution.py:273
  45.3 3.6 %collective-permute-start.8 = (bf16[128,256]{1,0:T(8,128)(2,1)S(1)}, bf16[128,256]{1,0:T(8,128)(2,1)S(1)}, u32[]{:S(2)}, u32[]{:S(2)}) collective-permute-start(bf16[128,256]{1,0:T(8,128)(2,1)S(1)} %slice.109), channel_id=1, source_target_pairs={{0,3},{1,0},{2,1},{3,2},{4,7},{5,4},{6,5},{7,6},{8,11},{9,8},{10,9... | collective-permute-start | bytes 196616 | tf_op jit(solution)/shard_map/ppermute | solution.py:278
  50.3 3.4 %collective-permute-done.9 = bf16[128,256]{1,0:T(8,128)(2,1)S(1)} collective-permute-done((bf16[128,256]{1,0:T(8,128)(2,1)S(1)}, bf16[128,256]{1,0:T(8,128)(2,1)S(1)}, u32[]{:S(2)}, u32[]{:S(2)}) %collective-permute-start.9) | collective-permute-done | bytes 65568 | tf_op jit(solution)/shard_map/ppermute | solution.py:278
  56.1 3.1 %collective-permute-start.11 = (bf16[512,256]{1,0:T(8,128)(2,1)S(1)}, bf16[512,256]{1,0:T(8,128)(2,1)S(1)}, u32[]{:S(2)}, u32[]{:S(2)}) collective-permute-start(bf16[512,256]{1,0:T(8,128)(2,1)S(1)} %constant_dynamic-update-slice_fusion.refs_0_), channel_id=1, source_target_pairs={{0,16},{16,0},{32,48},{48,32},{64,80},{80,64},{96,112},{112,96},{1... | collective-permute-start | bytes 786440 | tf_op jit(solution)/shard_map/ppermute | solution.py:282
  68.8 5.8 %collective-permute-done.15.refs_1_ = bf16[512,256]{1,0:T(8,128)(2,1)S(1)} collective-permute-done((bf16[512,256]{1,0:T(8,128)(2,1)S(1)}, bf16[512,256]{1,0:T(8,128)(2,1)S(1)}, u32[]{:S(2)}, u32[]{:S(2)}) %collective-permute-start.15) | collective-permute-done | bytes 262176 | tf_op jit(solution)/shard_map/ppermute | solution.py:273
  96.0 3.9 %shard_map.156 = (bf16[2048,128]{1,0:T(8,128)(2,1)S(1)}, bf16[512,128]{1,0:T(8,128)(2,1)S(1)}, bf16[512,128]{1,0:T(8,128)(2,1)S(1)}, f32[2048,128]{1,0:T(8,128)S...) custom-call(s32[1]{0:T(128)} %bitcast.6.first_ref, f32[512,384]{1,0:T(8,128)S(1)} %copy-done.31, ...), custom_call_target="tpu_custom_call" | custom-call | flops 536870912 | bytes 1048576 | tf_op jit(solution)/shard_map/pallas_call | solution.py:416
  111.8 2.5 %collective-permute-done.20.refs_6_ = bf16[512,256]{1,0:T(8,128)(2,1)S(1)} collective-permute-done((bf16[512,256]{1,0:T(8,128)(2,1)S(1)}, bf16[512,256]{1,0:T(8,128)(2,1)S(1)}, u32[]{:S(2)}, u32[]{:S(2)}) %collective-permute-start.20) | collective-permute-done | bytes 262176 | tf_op jit(solution)/shard_map/ppermute | solution.py:282
  128.5 3.5 %shard_map.160 = (bf16[512,384]{1,0:T(8,128)(2,1)S(1)}, bf16[512,384]{1,0:T(8,128)(2,1)S(1)}) custom-call(s32[1]{0:T(128)} %bitcast.6.first_ref, f32[512,384]{1,0:T(8,128)S(1)} %copy-done.32, f32[512,384]{1,0:T(8,128)S(1)} %copy-done.35, f32[1,128]{1,0:T(1,128)S(1)} %bitcast.28, f32[1,128]{1,0:T(1,128)S(1)} %bitcast.30, f32[128,128]{1,0:T(8,128)S(1)} %copy-done.72, ...), custom_call_target="tpu_custom_call" | custom-call | flops 536870912 | bytes 1048576 | tf_op jit(solution)/shard_map/pallas_call | solution.py:431
  138.9 2.6 %shard_map.162 = bf16[512,2048]{1,0:T(8,128)(2,1)} custom-call(bf16[512,256]{1,0:T(8,128)(2,1)S(1)} %copy-done.77, bf16[512,256]{1,0:T(8,128)(2,1)S(1)} %copy-done.80, bf16[512,256]{1,0:T(8,128)(2,1)S(1)} %constant_dynamic-update-slice_fusion.refs_0_, bf16[512,256]{1,0:T(8,128)(2,1)S(1)} %copy-done.17, bf16[512,256]{1,0:T(8,128)(2,1)S(1)} %copy-done.27, ...), custom_call_target="tpu_custom_call" | custom-call | flops 1073741824 | bytes 2097152 | tf_op jit(solution)/shard_map/pallas_call | solution.py:444
  142.1 3.5 %collective-permute-done.22 = bf16[2048,384]{1,0:T(8,128)(2,1)S(1)} collective-permute-done((bf16[2048,384]{1,0:T(8,128)(2,1)}, bf16[2048,384]{1,0:T(8,128)(2,1)S(1)}, u32[]{:S(2)}, u32[]{:S(2)}) %collective-permute-start.22) | collective-permute-done | bytes 1572896 | tf_op jit(solution)/shard_map/ppermute | solution.py:282
  149.5 9.1 %collective-permute-done.23 = bf16[512,384]{1,0:T(8,128)(2,1)S(1)} collective-permute-done((bf16[512,384]{1,0:T(8,128)(2,1)S(1)}, bf16[512,384]{1,0:T(8,128)(2,1)S(1)}, u32[]{:S(2)}, u32[]{:S(2)}) %collective-permute-start.23) | collective-permute-done | bytes 393248 | tf_op jit(solution)/shard_map/ppermute | solution.py:273
  158.7 3.7 %shard_map.163 = bf16[512,2048]{1,0:T(8,128)(2,1)} custom-call(bf16[512,384]{1,0:T(8,128)(2,1)S(1)} %copy-done.9, bf16[512,384]{1,0:T(8,128)(2,1)S(1)} %copy-done.11, bf16[512,384]{1,0:T(8,128)(2,1)S(1)} %pad_maximum_fusion.refs_0_, bf16[512,384]{1,0:T(8,128)(2,1)S(1)} %copy-done.47, bf16[512,384]{1,0:T(8,128)(2,1)S(1)} %copy-done.50, ...), custom_call_target="tpu_custom_call" | custom-call | flops 1610612736 | bytes 2097152 | tf_op jit(solution)/shard_map/pallas_call | solution.py:449
  165.9 3.7 %collective-permute-start.28 = (bf16[128,256]{1,0:T(8,128)(2,1)S(1)}, bf16[128,256]{1,0:T(8,128)(2,1)S(1)}, u32[]{:S(2)}, u32[]{:S(2)}) collective-permute-start(bf16[128,256]{1,0:T(8,128)(2,1)S(1)} %get-tuple-element.138), channel_id=1, source_target_pairs={{0,3},{1,0},{2,1},{3,2},{4,7},{5,4},{6,5},{7,6},{8,11},{9,8},{10,9... | collective-permute-start | bytes 196616 | tf_op jit(solution)/shard_map/ppermute | solution.py:278
  171.0 4.4 %collective-permute-done.27 = bf16[128,256]{1,0:T(8,128)(2,1)S(1)} collective-permute-done((bf16[128,256]{1,0:T(8,128)(2,1)S(1)}, bf16[128,256]{1,0:T(8,128)(2,1)S(1)}, u32[]{:S(2)}, u32[]{:S(2)}) %collective-permute-start.27) | collective-permute-done | bytes 65568 | tf_op jit(solution)/shard_map/ppermute | solution.py:278
  181.3 4.1 %collective-permute-done.30 = bf16[128,384]{1,0:T(8,128)(2,1)S(1)} collective-permute-done((bf16[128,384]{1,0:T(8,128)(2,1)S(1)}, bf16[128,384]{1,0:T(8,128)(2,1)S(1)}, u32[]{:S(2)}, u32[]{:S(2)}) %collective-permute-start.30) | collective-permute-done | bytes 98336 | tf_op jit(solution)/shard_map/ppermute | solution.py:278
  188.2 8.8 %collective-permute-done.32 = bf16[128,640]{1,0:T(8,128)(2,1)S(1)} collective-permute-done((bf16[128,640]{1,0:T(8,128)(2,1)S(1)}, bf16[128,640]{1,0:T(8,128)(2,1)S(1)}, u32[]{:S(2)}, u32[]{:S(2)}) %collective-permute-start.32) | collective-permute-done | bytes 163872 | tf_op jit(solution)/shard_map/ppermute | solution.py:298
  200.3 3.4 %collective-permute-start.35 = (bf16[128,640]{1,0:T(8,128)(2,1)S(1)}, bf16[128,640]{1,0:T(8,128)(2,1)S(1)}, u32[]{:S(2)}, u32[]{:S(2)}) collective-permute-start(bf16[128,640]{1,0:T(8,128)(2,1)S(1)} %add_convert_fusion.6), channel_id=1, source_target_pairs={{0,32},{16,48},{32,64},{48,80},{192,224},{208,240},{224,128},{240,... | collective-permute-start | bytes 491528 | tf_op jit(solution)/shard_map/ppermute | solution.py:308
  203.8 16.9 %reduce-scatter.6.cloned.1.call-done.back_ref = bf16[128,2048]{1,0:T(8,128)(2,1)} async-done(((bf16[512,2048]{1,0:T(8,128)(2,1)}), bf16[128,2048]{1,0:T(8,128)(2,1)}) %reduce-scatter.6.cloned.1.call-update) | async-done | bytes 524304 | tf_op jit(solution)/shard_map/reduce_scatter | solution.py:266
  222.8 2.4 %shard_map.164 = (bf16[128,2048]{1,0:T(8,128)(2,1)}, bf16[128,2048]{1,0:T(8,128)(2,1)}) custom-call(s32[2]{0:T(128)S(1)} %pad_add_fusion.place_ref, bf16[128,2048]{1,0:T(8,128)(2,1)S(1)} %bitcast.24, f32[1,2048]{1,0:T(1,128)S(1)} %bitcast.26, bf16[128,2048]{1,0:T(8,128)(2,1)S(1)} %bitcast.22, f32[128,1]{1,0:T(8,128)S(1)} %copy-done.37, ...), custom_call_target="tpu_custom_call" | custom-call | bytes 1048576 | tf_op jit(solution)/shard_map/pallas_call | solution.py:460
  (313 shorter events, 107.8 us)
Async XLA Ops:
  7.2 73.3 %all-gather.3.cloned.1.call-start = ((), (), s32[]{:S(2)}) async-start(), calls=%async_computation.3 | async-start | bytes 2621440 | tf_op jit(solution)/shard_map/all_gather | solution.py:253
  13.4 91.8 %all-gather.5.cloned.1.call-start = ((), (), s32[]{:S(2)}) async-start(), calls=%async_computation.4 | async-start | bytes 2621440 | tf_op jit(solution)/shard_map/all_gather | solution.py:253
  13.4 12.5 %collective-permute-start = (bf16[128,640]{1,0:T(8,128)(2,1)S(1)}, bf16[128,640]{1,0:T(8,128)(2,1)S(1)}, u32[]{:S(2)}, u32[]{:S(2)}) collective-permute-start(bf16[128,640]{1,0:T(8,128)(2,1)S(1)} %pad_maximum_fusion.2), channel_id=1, source_target_pairs={{0,128},{16,144},{32,160},{48,176},{192,64},{208,80},{224,96},{240... | collective-permute-start | bytes 491528 | tf_op jit(solution)/shard_map/ppermute | solution.py:292
  27.6 137.4 %reduce-scatter.8.cloned.1.call-start = ((), (), s32[]{:S(2)}) async-start(), calls=%async_computation.7 | async-start | bytes 1310720 | tf_op jit(solution)/shard_map/reduce_scatter | solution.py:260
  41.5 19.5 %collective-permute-start.4 = (bf16[512,384]{1,0:T(8,128)(2,1)S(1)}, bf16[512,384]{1,0:T(8,128)(2,1)S(1)}, u32[]{:S(2)}, u32[]{:S(2)}) collective-permute-start(bf16[512,384]{1,0:T(8,128)(2,1)S(1)} %pad_maximum_fusion.refs_0_), channel_id=1, source_target_pairs={{0,12},{1,13},{2,14},{3,15},{4,0},{5,1},{6,2},{7,3},{8,4},{9,5},{1... | collective-permute-start | bytes 1179656 | tf_op jit(solution)/shard_map/ppermute | solution.py:273
  44.3 18.5 %collective-permute-start.5 = (bf16[512,384]{1,0:T(8,128)(2,1)S(1)}, bf16[512,384]{1,0:T(8,128)(2,1)S(1)}, u32[]{:S(2)}, u32[]{:S(2)}) collective-permute-start(bf16[512,384]{1,0:T(8,128)(2,1)S(1)} %pad_maximum_fusion.refs_0_), channel_id=1, source_target_pairs={{0,8},{1,9},{2,10},{3,11},{4,12},{5,13},{6,14},{7,15},{8,0},{9,1},... | collective-permute-start | bytes 1179656 | tf_op jit(solution)/shard_map/ppermute | solution.py:273
  44.6 20.6 %collective-permute-start.6 = (bf16[512,384]{1,0:T(8,128)(2,1)S(1)}, bf16[512,384]{1,0:T(8,128)(2,1)S(1)}, u32[]{:S(2)}, u32[]{:S(2)}) collective-permute-start(bf16[512,384]{1,0:T(8,128)(2,1)S(1)} %pad_maximum_fusion.refs_0_), channel_id=1, source_target_pairs={{0,4},{1,5},{2,6},{3,7},{4,8},{5,9},{6,10},{7,11},{8,12},{9,13},{1... | collective-permute-start | bytes 1179656 | tf_op jit(solution)/shard_map/ppermute | solution.py:273
  61.1 17.1 %collective-permute-start.12 = (bf16[512,384]{1,0:T(8,128)(2,1)S(1)}, bf16[512,384]{1,0:T(8,128)(2,1)S(1)}, u32[]{:S(2)}, u32[]{:S(2)}) collective-permute-start(bf16[512,384]{1,0:T(8,128)(2,1)S(1)} %collective-permute-done.4.refs_1_), channel_id=1, source_target_pairs={{0,16},{16,0},{32,48},{48,32},{64,80},{80,64},{96,112},{112,96},{1... | collective-permute-start | bytes 1179656 | tf_op jit(solution)/shard_map/ppermute | solution.py:282
  62.8 16.1 %collective-permute-start.13 = (bf16[512,384]{1,0:T(8,128)(2,1)S(1)}, bf16[512,384]{1,0:T(8,128)(2,1)S(1)}, u32[]{:S(2)}, u32[]{:S(2)}) collective-permute-start(bf16[512,384]{1,0:T(8,128)(2,1)S(1)} %collective-permute-done.5.refs_2_), channel_id=1, source_target_pairs={{0,16},{16,0},{32,48},{48,32},{64,80},{80,64},{96,112},{112,96},{1... | collective-permute-start | bytes 1179656 | tf_op jit(solution)/shard_map/ppermute | solution.py:282
  65.3 14.4 %collective-permute-start.14 = (bf16[512,384]{1,0:T(8,128)(2,1)S(1)}, bf16[512,384]{1,0:T(8,128)(2,1)S(1)}, u32[]{:S(2)}, u32[]{:S(2)}) collective-permute-start(bf16[512,384]{1,0:T(8,128)(2,1)S(1)} %collective-permute-done.6.refs_3_), channel_id=1, source_target_pairs={{0,16},{16,0},{32,48},{48,32},{64,80},{80,64},{96,112},{112,96},{1... | collective-permute-start | bytes 1179656 | tf_op jit(solution)/shard_map/ppermute | solution.py:282
  66.5 8.0 %collective-permute-start.15 = (bf16[512,256]{1,0:T(8,128)(2,1)S(1)}, bf16[512,256]{1,0:T(8,128)(2,1)S(1)}, u32[]{:S(2)}, u32[]{:S(2)}) collective-permute-start(bf16[512,256]{1,0:T(8,128)(2,1)S(1)} %constant_dynamic-update-slice_fusion.refs_0_), channel_id=1, source_target_pairs={{0,12},{1,13},{2,14},{3,15},{4,0},{5,1},{6,2},{7,3},{8,4},{9,5},{1... | collective-permute-start | bytes 786440 | tf_op jit(solution)/shard_map/ppermute | solution.py:273
  68.2 8.9 %collective-permute-start.16 = (bf16[512,256]{1,0:T(8,128)(2,1)S(1)}, bf16[512,256]{1,0:T(8,128)(2,1)S(1)}, u32[]{:S(2)}, u32[]{:S(2)}) collective-permute-start(bf16[512,256]{1,0:T(8,128)(2,1)S(1)} %constant_dynamic-update-slice_fusion.refs_0_), channel_id=1, source_target_pairs={{0,4},{1,5},{2,6},{3,7},{4,8},{5,9},{6,10},{7,11},{8,12},{9,13},{1... | collective-permute-start | bytes 786440 | tf_op jit(solution)/shard_map/ppermute | solution.py:273
  74.6 29.9 %collective-permute-start.18 = (bf16[512,256]{1,0:T(8,128)(2,1)S(1)}, bf16[512,256]{1,0:T(8,128)(2,1)S(1)}, u32[]{:S(2)}, u32[]{:S(2)}) collective-permute-start(bf16[512,256]{1,0:T(8,128)(2,1)S(1)} %collective-permute-done.15.refs_1_), channel_id=1, source_target_pairs={{0,16},{16,0},{32,48},{48,32},{64,80},{80,64},{96,112},{112,96},{1... | collective-permute-start | bytes 786440 | tf_op jit(solution)/shard_map/ppermute | solution.py:282
  77.1 27.3 %collective-permute-start.19 = (bf16[512,256]{1,0:T(8,128)(2,1)S(1)}, bf16[512,256]{1,0:T(8,128)(2,1)S(1)}, u32[]{:S(2)}, u32[]{:S(2)}) collective-permute-start(bf16[512,256]{1,0:T(8,128)(2,1)S(1)} %collective-permute-done.16.refs_3_), channel_id=1, source_target_pairs={{0,16},{16,0},{32,48},{48,32},{64,80},{80,64},{96,112},{112,96},{1... | collective-permute-start | bytes 786440 | tf_op jit(solution)/shard_map/ppermute | solution.py:282
  93.2 12.0 %collective-permute-start.17 = (bf16[512,256]{1,0:T(8,128)(2,1)S(1)}, bf16[512,256]{1,0:T(8,128)(2,1)S(1)}, u32[]{:S(2)}, u32[]{:S(2)}) collective-permute-start(bf16[512,256]{1,0:T(8,128)(2,1)S(1)} %constant_dynamic-update-slice_fusion.refs_0_), channel_id=1, source_target_pairs={{0,8},{1,9},{2,10},{3,11},{4,12},{5,13},{6,14},{7,15},{8,0},{9,1},... | collective-permute-start | bytes 786440 | tf_op jit(solution)/shard_map/ppermute | solution.py:273
  118.4 78.7 %reduce-scatter.4.cloned.1.call-start = ((), (), s32[]{:S(2)}) async-start(), calls=%async_computation.5 | async-start | bytes 2621440 | tf_op jit(solution)/shard_map/reduce_scatter | solution.py:266
  141.6 79.1 %reduce-scatter.6.cloned.1.call-start = ((), (), s32[]{:S(2)}) async-start(), calls=%async_computation.6 | async-start | bytes 2621440 | tf_op jit(solution)/shard_map/reduce_scatter | solution.py:266
  146.8 11.8 %collective-permute-start.23 = (bf16[512,384]{1,0:T(8,128)(2,1)S(1)}, bf16[512,384]{1,0:T(8,128)(2,1)S(1)}, u32[]{:S(2)}, u32[]{:S(2)}) collective-permute-start(bf16[512,384]{1,0:T(8,128)(2,1)S(1)} %get-tuple-element.92), channel_id=1, source_target_pairs={{0,4},{1,5},{2,6},{3,7},{4,8},{5,9},{6,10},{7,11},{8,12},{9,13},{1... | collective-permute-start | bytes 1179656 | tf_op jit(solution)/shard_map/ppermute | solution.py:273
  147.9 10.7 %collective-permute-start.24 = (bf16[512,384]{1,0:T(8,128)(2,1)S(1)}, bf16[512,384]{1,0:T(8,128)(2,1)S(1)}, u32[]{:S(2)}, u32[]{:S(2)}) collective-permute-start(bf16[512,384]{1,0:T(8,128)(2,1)S(1)} %get-tuple-element.93), channel_id=1, source_target_pairs={{0,12},{1,13},{2,14},{3,15},{4,0},{5,1},{6,2},{7,3},{8,4},{9,5},{1... | collective-permute-start | bytes 1179656 | tf_op jit(solution)/shard_map/ppermute | solution.py:273
  163.4 12.9 %collective-permute-start.25 = (bf16[512,384]{1,0:T(8,128)(2,1)S(1)}, bf16[512,384]{1,0:T(8,128)(2,1)}, u32[]{:S(2)}, u32[]{:S(2)}) collective-permute-start(bf16[512,384]{1,0:T(8,128)(2,1)S(1)} %copy-done.94), channel_id=1, source_target_pairs={{0,8},{1,9},{2,10},{3,11},{4,12},{5,13},{6,14},{7,15},{8,0},{9,1},... | collective-permute-start | bytes 1179656 | tf_op jit(solution)/shard_map/ppermute | solution.py:273
  186.9 10.1 %collective-permute-start.32 = (bf16[128,640]{1,0:T(8,128)(2,1)S(1)}, bf16[128,640]{1,0:T(8,128)(2,1)S(1)}, u32[]{:S(2)}, u32[]{:S(2)}) collective-permute-start(bf16[128,640]{1,0:T(8,128)(2,1)S(1)} %pad_maximum_fusion.3), channel_id=1, source_target_pairs={{128,0},{144,16},{160,32},{176,48},{64,192},{80,208},{96,224},{112... | collective-permute-start | bytes 491528 | tf_op jit(solution)/shard_map/ppermute | solution.py:298
  197.1 28.1 %collective-permute-start.33 = (bf16[128,640]{1,0:T(8,128)(2,1)S(1)}, bf16[128,640]{1,0:T(8,128)(2,1)S(1)}, u32[]{:S(2)}, u32[]{:S(2)}) collective-permute-start(bf16[128,640]{1,0:T(8,128)(2,1)S(1)} %add_convert_fusion.6), channel_id=1, source_target_pairs={{0,96},{16,112},{32,0},{48,16},{192,160},{208,176},{224,192},{240,... | collective-permute-start | bytes 491528 | tf_op jit(solution)/shard_map/ppermute | solution.py:308
  199.0 26.2 %collective-permute-start.34 = (bf16[128,640]{1,0:T(8,128)(2,1)S(1)}, bf16[128,640]{1,0:T(8,128)(2,1)S(1)}, u32[]{:S(2)}, u32[]{:S(2)}) collective-permute-start(bf16[128,640]{1,0:T(8,128)(2,1)S(1)} %add_convert_fusion.6), channel_id=1, source_target_pairs={{0,64},{16,80},{32,96},{48,112},{192,128},{208,144},{224,160},{240... | collective-permute-start | bytes 491528 | tf_op jit(solution)/shard_map/ppermute | solution.py:308
  200.3 24.9 %collective-permute-start.35 = (bf16[128,640]{1,0:T(8,128)(2,1)S(1)}, bf16[128,640]{1,0:T(8,128)(2,1)S(1)}, u32[]{:S(2)}, u32[]{:S(2)}) collective-permute-start(bf16[128,640]{1,0:T(8,128)(2,1)S(1)} %add_convert_fusion.6), channel_id=1, source_target_pairs={{0,32},{16,48},{32,64},{48,80},{192,224},{208,240},{224,128},{240,... | collective-permute-start | bytes 491528 | tf_op jit(solution)/shard_map/ppermute | solution.py:308
  (116 other events, 877.6 us)
Sparse Core Ops, SparseCore 0:
  13.5 37.1 all-gather.2
  53.1 33.4 all-gather.4
  118.5 25.9 reduce-scatter.7
  147.1 33.3 reduce-scatter.3
  182.9 37.7 reduce-scatter.5
where the time goes:
time: 239 us; the launch traced here: 237 us
  waiting for transfers between devices  77.1 us (32%)
  starting transfers between devices  57.9 us (24%)
  local copies, waits for them, and re-layouts  51.3 us (21%)
  Pallas kernels  27.2 us (11%)
  between operations  14.8 us (6%)
  other arithmetic  8.95 us (4%)
    unnamed x201, local copies, waits for them, and re-layouts  49.3 us
    ppermute x12, waiting for transfers between devices, take_z(): return lax.ppermute(value, 'fsdp', pairs)  21 us
    ppermute x9, waiting for transfers between devices, take_y(): return lax.ppermute(value, 'fsdp', pairs)  20.3 us
    ppermute x12, starting transfers between devices, take_z(): return lax.ppermute(value, 'fsdp', pairs)  18.8 us
    reduce_scatter x2, waiting for transfers between devices, scatter_x(): lax.psum_scatter(value, 'dp', scatter_dimension=0, tiled=True, axis_index...  17 us
    ppermute x11, starting transfers between devices, other_core(): return lax.ppermute(value, 'dp', [(i, i ^ 1) for i in range(NX * NC)])  11.7 us
    ppermute x9, starting transfers between devices, take_y(): return lax.ppermute(value, 'fsdp', pairs)  9.74 us
    ppermute x1, starting transfers between devices, from_owner(): return lax.ppermute(value, ('role', 'dp'), pairs)  9.65 us
  transfers between devices with their start and end apart: 42, of which 19 were waited for; matrix products, arithmetic and copies ran while one was open for 2% of the time, Pallas kernels for 10%

commit v1 on v0

--- a/solution.py
+++ b/solution.py
@@ -1,3 +1,5 @@
+from functools import partial
+
 import jax
 import jax.numpy as jnp
 from jax import lax
@@ -46,7 +48,7 @@
         in_specs=[pl.BlockSpec(memory_space=pltpu.SMEM)] * scalars
         + [pl.BlockSpec(memory_space=pltpu.VMEM)] * (vmem - scalars),
         out_specs=[pl.BlockSpec(memory_space=pltpu.VMEM)] * len(outs),
-        compiler_params=pltpu.CompilerParams(vmem_limit_bytes=40 << 20),
+        compiler_params=pltpu.CompilerParams(vmem_limit_bytes=16 << 20),
         **more,
     )
 
@@ -57,31 +59,31 @@
     return pl.ds(pl.multiple_of((row * NZ + col) * HD, HD), HD)
 
 
-def norm_kernel(place_ref, rows_ref, gain_ref, normed_ref):
+def rows_kernel(place_ref, rows_ref, gain_ref, cot_ref, weight_ref, out_ref):
     x = rows_ref[...].astype(f32)
     inv = lax.rsqrt(jnp.mean(x * x, axis=-1, keepdims=True) + eps_norm)
-    for j in range(NY * NZ):
-        at = turned(place_ref, j)
-        normed_ref[:, j * HD : (j + 1) * HD] = (
-            rows_ref[:, at].astype(f32) * inv * gain_ref[:, at]
-        ).astype(bf16)
-
-
-def weigh_kernel(place_ref, cot_ref, weight_ref, grad_ref):
     weight = weight_ref[...]
     for j in range(NY * NZ):
         at = turned(place_ref, j)
-        grad_ref[:, j * HD : (j + 1) * HD] = (cot_ref[:, at].astype(f32) * weight).astype(bf16)
+        cols = slice(j * HD, (j + 1) * HD)
+        out_ref[:TRAJ, cols] = (rows_ref[:, at].astype(f32) * inv * gain_ref[:, at]).astype(bf16)
+        out_ref[TRAJ:, cols] = (cot_ref[:, at].astype(f32) * weight).astype(bf16)
+
+
+def tokens_of(pair_ref, part, cols):
+    tops = [(2 * k + part) * TRAJ for k in range(NX)]
+    return jnp.concatenate([pair_ref[top : top + TRAJ, cols] for top in tops], axis=0)
 
 
 def finish_kernel(
-    place_ref, rows_ref, gain_ref, cot_ref, weight_ref, mixed_ref, back_ref, out_ref, grad_ref, scaled_ref
+    place_ref, rows_ref, gain_ref, cot_ref, weight_ref, total_ref, out_ref, grad_ref, scaled_ref
 ):
     for j in range(NY * NZ):
         at = turned(place_ref, j)
         cols = slice(j * HD, (j + 1) * HD)
-        out_ref[:, at] = (rows_ref[:, at].astype(f32) + mixed_ref[:, cols].astype(f32)).astype(bf16)
-        scaled_ref[:, at] = back_ref[:, cols].astype(f32) * gain_ref[:, at]
+        mixed, back = total_ref[:TRAJ, cols].astype(f32), total_ref[TRAJ:, cols].astype(f32)
+        out_ref[:, at] = (rows_ref[:, at].astype(f32) + mixed).astype(bf16)
+        scaled_ref[:, at] = back * gain_ref[:, at]
     x = rows_ref[...].astype(f32)
     inv = lax.rsqrt(jnp.mean(x * x, axis=-1, keepdims=True) + eps_norm)
     scaled = scaled_ref[...]
@@ -91,24 +93,34 @@
     grad_ref[...] = (grad_out + inv * (scaled - unit * mean)).astype(bf16)
 
 
-def project_kernel(normed_ref, *refs):
+def project_kernel(part, pair_ref, *refs):
     own, other, outs = refs[:NY], refs[NY : 2 * NY], refs[2 * NY :]
-    for chunks, out_ref in zip((own, other), outs):
-        total = None
-        for j in range(NY):
-            span = chunks[j].shape[0]
-            term = dot(normed_ref[:, j * span : (j + 1) * span], chunks[j][...])
-            total = term if total is None else total + term
-        out_ref[...] = total.astype(out_ref.dtype)
-
-
-def expand_kernel(left_own_ref, left_other_ref, *refs):
-    own, other, out_ref = refs[:NY], refs[NY : 2 * NY], refs[2 * NY]
+    totals = [None, None]
     for j in range(NY):
         span = own[j].shape[0]
-        total = dot_rows(left_own_ref[...], own[j][...])
-        total = total + dot_rows(left_other_ref[...], other[j][...])
-        out_ref[:, j * span : (j + 1) * span] = total.astype(bf16)
+        left = tokens_of(pair_ref, part, slice(j * span, (j + 1) * span))
+        for side, chunks in enumerate((own, other)):
+            term = dot(left, chunks[j][...])
+            totals[side] = term if totals[side] is None else totals[side] + term
+    for out_ref, total in zip(outs, totals):
+        out_ref[...] = total.astype(out_ref.dtype)
+
+
+def expand_kernel(mixed_own_ref, mixed_other_ref, g_own_ref, g_other_ref, *refs):
+    out_ref = refs[4 * NY]
+    lefts = ((mixed_own_ref, mixed_other_ref), (g_own_ref, g_other_ref))
+    for part, (left_own_ref, left_other_ref) in enumerate(lefts):
+        own = refs[2 * part * NY : (2 * part + 1) * NY]
+        other = refs[(2 * part + 1) * NY : (2 * part + 2) * NY]
+        for j in range(NY):
+            span = own[j].shape[0]
+            total = dot_rows(left_own_ref[...], own[j][...])
+            total = total + dot_rows(left_other_ref[...], other[j][...])
+            for k in range(NX):
+                top = (2 * k + part) * TRAJ
+                out_ref[top : top + TRAJ, j * span : (j + 1) * span] = total[
+                    k * TRAJ : (k + 1) * TRAJ
+                ].astype(bf16)
 
 
 def rotate(t, cos, sin):
@@ -207,23 +219,23 @@
         out_shape=[jax.ShapeDtypeStruct((rows * NX, cols), kind) for rows, cols, kind in outs],
         in_specs=[pl.BlockSpec(memory_space=pltpu.SMEM)] + [spec(*entry) for entry in ins],
         out_specs=[spec(rows, cols) for rows, cols, _ in outs],
-        compiler_params=pltpu.CompilerParams(vmem_limit_bytes=40 << 20),
-    )
-
-
-def weight_grad_kernel(left_ref, own_ref, other_ref, *refs):
+        compiler_params=pltpu.CompilerParams(vmem_limit_bytes=16 << 20),
+    )
+
+
+def weight_grad_kernel(pair_ref, own_ref, other_ref, *refs):
     outs, other_out = refs[:NY], refs[NY]
     for j in range(NY):
         span = outs[j].shape[0]
-        left = left_ref[:, j * span : (j + 1) * span]
+        left = tokens_of(pair_ref, 0, slice(j * span, (j + 1) * span))
         other_out[j * span : (j + 1) * span] = dot_cols(left, other_ref[...]).astype(bf16)
         outs[j][...] = dot_cols(left, own_ref[...]).astype(bf16)
 
 
-def grad_o_kernel(place_ref, left_ref, own_ref, other_ref, own_out, other_out):
+def grad_o_kernel(place_ref, pair_ref, own_ref, other_ref, own_out, other_out):
     span = NZ * HD
     for j in range(NY):
-        left = left_ref[:, j * span : (j + 1) * span]
+        left = tokens_of(pair_ref, 1, slice(j * span, (j + 1) * span))
         at = pl.ds(pl.multiple_of(lax.rem(place_ref[0] + j, NY) * span, span), span)
         other_out[at] = dot_cols(left, other_ref[...]).astype(bf16)
         own_out[at] = dot_cols(left, own_ref[...]).astype(bf16)
@@ -388,11 +400,10 @@
     gain = norm_gain[None]
     weight = (advantage[0] * action[0].astype(f32))[:, None]
     flat = (TRAJ, rows_own.shape[1])
-    normed_own = call(norm_kernel, [(flat, bf16)], 3)(place, after(rows_own, block_part), gain)[0]
-    normed = gather_x(normed_own)
-    cot_late = after(cot_own, block)
-    grad_turned = call(weigh_kernel, [(flat, bf16)], 3)(place, cot_late, weight)[0]
-    grad_all = gather_x(grad_turned)
+    pair_own = call(rows_kernel, [((2 * TRAJ, flat[1]), bf16)], 5)(
+        place, after(rows_own, block_part), gain, cot_own, weight
+    )[0]
+    pair = gather_x(pair_own)
 
     qkv_own = over_y(qkv_plane)
     qkv_first = other_core(qkv_plane)
@@ -402,13 +413,13 @@
     o_late = after(o_plane, *qkv_own)
     o_near = [take_y(o_late, 1), take_y(o_late, 3)]
 
-    tokens = normed.shape[0]
+    tokens = pair.shape[0] // 2
     cos_tab, sin_tab = rope_tables()
     proj_own, proj_other = call(
-        project_kernel, [((tokens, wide), f32)] * 2, 1 + 2 * NY, scalars=0, macs=tokens * flat[1] * 2 * wide
-    )(normed, *qkv_own, *qkv_other)
+        partial(project_kernel, 0), [((tokens, wide), f32)] * 2, 1 + 2 * NY, scalars=0, macs=tokens * flat[1] * 2 * wide
+    )(pair, *qkv_own, *qkv_other)
     o_own = [o_plane, o_near[0], take_y(after(o_plane, proj_own), 2), o_near[1]]
-    o_other = [o_first] + [other_core(piece) for piece in o_own[1:]]
+    o_other = [o_first] + [other_core(after(piece, proj_own)) for piece in o_own[1:]]
     proj_own, proj_other = after([proj_own, proj_other], *o_near)
     shared = [(0, (1, HD)), (0, (1, HD)), (0, (TRAJ, HD)), (0, (TRAJ, HD))]
     tables = (q_gain[None], k_gain[None], cos_tab, sin_tab)
@@ -422,10 +433,10 @@
     span = NZ * HD
     go_own, go_cross = call(
         grad_o_kernel, [((NY * span, half), bf16)] * 2, 4, macs=tokens * flat[1] * width
-    )(place, after(grad_all, o_own[2], o_other[1], o_other[3]), mixed_own, mixed_other)
+    )(place, after(pair, o_own[2], o_other[1], o_other[3]), mixed_own, mixed_other)
     gm_own, gm_other = call(
-        project_kernel, [((tokens, half), bf16)] * 2, 1 + 2 * NY, scalars=0, macs=tokens * flat[1] * width
-    )(after(grad_all, go_cross), *o_own, *o_other)
+        partial(project_kernel, 1), [((tokens, half), bf16)] * 2, 1 + 2 * NY, scalars=0, macs=tokens * flat[1] * width
+    )(after(pair, go_cross), *o_own, *o_other)
     go_theirs = after(other_core(go_cross), gm_own)
     go_terms = scatter_y((go_own.astype(f32) + go_theirs.astype(f32)).astype(bf16))
     g_own, g_other = by_trajectory(
@@ -438,30 +449,29 @@
         [((span, wide), bf16)] * NY + [((NY * span, wide), bf16)],
         3,
         scalars=0,
-    )(normed, g_own, g_other)
+    )(pair, g_own, g_other)
     gw_theirs = other_core(gw_cross)
-    spread = ((tokens, flat[1]), bf16)
-    part_out = call(expand_kernel, [spread], 2 + 2 * NY, scalars=0, macs=tokens * flat[1] * width)(
-        *after([mixed_own, mixed_other], gw_cross), *o_own, *o_other
-    )[0]
-    gw_terms = after(add_core(gw_own, gw_theirs), part_out)
+    terms = call(
+        expand_kernel,
+        [((2 * tokens, flat[1]), bf16)],
+        4 + 4 * NY,
+        scalars=0,
+        macs=tokens * flat[1] * (width + 2 * wide),
+    )(mixed_own, mixed_other, *after([g_own, g_other], gw_cross), *o_own, *o_other, *qkv_own, *qkv_other)[0]
+    row_total = scatter_x(terms)
+
+    gw_terms = after(add_core(gw_own, gw_theirs), terms)
     gw_near = [take_y(gw_terms[1], -1), take_y(gw_terms[3], -3)]
-    back = call(expand_kernel, [spread], 2 + 2 * NY, scalars=0, macs=tokens * flat[1] * 2 * wide)(
-        *after([g_own, g_other], *gw_near), *qkv_own, *qkv_other
-    )[0]
-    out_total = scatter_x(part_out)
-    back_total = scatter_x(back)
-
     go_terms = after(go_terms, *gw_near)
     go_term = add_z([go_terms[k * HD : (k + 1) * HD] for k in range(NZ)])
     gw_far = take_y(after(gw_terms[2], *gw_near), -2)
     gw_terms = add_y([gw_terms[0], *gw_near, after(gw_far, go_term)])
     gw_term = add_z(gw_terms)
     out_rows, grad_rows = call(
-        finish_kernel, [(flat, bf16)] * 2, 7, scratch_shapes=[pltpu.VMEM(flat, f32)]
-    )(place, rows_own, gain, cot_own, weight, out_total, back_total)
+        finish_kernel, [(flat, bf16)] * 2, 6, scratch_shapes=[pltpu.VMEM(flat, f32)]
+    )(place, rows_own, gain, cot_own, weight, row_total)
     total = add_role(jnp.concatenate([gw_term, go_term], axis=1))
-    mine, theirs = share(after(total, out_total), x, role, grad_rows)
+    mine, theirs = share(total, x, role, grad_rows)
     g_0, g_1 = jnp.where(first, mine, theirs), jnp.where(first, theirs, mine)
 
     def pick(value, item, lo, hi):

time: 239 us -> 215 us (0.90)
  the two profiles are of different devices: /device:TPU:1 before, /device:TPU:35 now
where the time goes in v1:
time: 215 us; the launch traced here: 214 us
  waiting for transfers between devices  68.8 us (32%)
  starting transfers between devices  51.5 us (24%)
  local copies, waits for them, and re-layouts  43.1 us (20%)
  Pallas kernels  25.9 us (12%)
  between operations  14.5 us (7%)
  other arithmetic  10 us (5%)
    unnamed x113, local copies, waits for them, and re-layouts  40.4 us
    ppermute x12, waiting for transfers between devices, take_z(): return lax.ppermute(value, 'fsdp', pairs)  21.4 us
    ppermute x9, waiting for transfers between devices, take_y(): return lax.ppermute(value, 'fsdp', pairs)  18.2 us
    ppermute x1, waiting for transfers between devices, to_owner(): return lax.ppermute(value, ('role', 'dp'), pairs)  14.4 us
    ppermute x12, starting transfers between devices, take_z(): return lax.ppermute(value, 'fsdp', pairs)  13.4 us
    ppermute x9, starting transfers between devices, take_y(): return lax.ppermute(value, 'fsdp', pairs)  12 us
    ppermute x11, starting transfers between devices, other_core(): return lax.ppermute(value, 'dp', [(i, i ^ 1) for i in range(NX * NC)])  11.2 us
    ppermute x1, starting transfers between devices, from_owner(): return lax.ppermute(value, ('role', 'dp'), pairs)  7.92 us
  transfers between devices with their start and end apart: 40, of which 20 were waited for; matrix products, arithmetic and copies ran while one was open for 4% of the time, Pallas kernels for 10%

profile of v1, /device:TPU:35, one launch (start us, length us, event | category | flops | bytes accessed | tf_op | source)
XLA Modules:
  0.0 213.8 jit_solution(2653351866096616791)
XLA Ops:
  15.6 7.9 %collective-permute-start = (bf16[128,640]{1,0:T(8,128)(2,1)S(1)}, bf16[128,640]{1,0:T(8,128)(2,1)S(1)}, u32[]{:S(2)}, u32[]{:S(2)}) collective-permute-start(bf16[128,640]{1,0:T(8,128)(2,1)S(1)} %pad_maximum_fusion.2), channel_id=1, source_target_pairs={{0,128},{16,144},{32,160},{48,176},{192,64},{208,80},{224,96},{240... | collective-permute-start | bytes 491528 | tf_op jit(solution)/shard_map/ppermute | solution.py:304
  23.6 6.4 %collective-permute-done = bf16[128,640]{1,0:T(8,128)(2,1)S(1)} collective-permute-done((bf16[128,640]{1,0:T(8,128)(2,1)S(1)}, bf16[128,640]{1,0:T(8,128)(2,1)S(1)}, u32[]{:S(2)}, u32[]{:S(2)}) %collective-permute-start) | collective-permute-done | bytes 163872 | tf_op jit(solution)/shard_map/ppermute | solution.py:304
  30.2 2.8 %collective-permute-start.2 = (bf16[128,384]{1,0:T(8,128)(2,1)S(1)}, bf16[128,384]{1,0:T(8,128)(2,1)S(1)}, u32[]{:S(2)}, u32[]{:S(2)}) collective-permute-start(bf16[128,384]{1,0:T(8,128)(2,1)S(1)} %slice.108), channel_id=1, source_target_pairs={{0,2},{1,3},{2,0},{3,1},{4,6},{5,7},{6,4},{7,5},{8,10},{9,11},{10,... | collective-permute-start | bytes 294920 | tf_op jit(solution)/shard_map/ppermute | solution.py:290
  37.0 4.0 %collective-permute-start.7 = (bf16[512,384]{1,0:T(8,128)(2,1)S(1)}, bf16[512,384]{1,0:T(8,128)(2,1)S(1)}, u32[]{:S(2)}, u32[]{:S(2)}) collective-permute-start(bf16[512,384]{1,0:T(8,128)(2,1)S(1)} %pad_maximum_fusion.refs_0_.refs_8_), channel_id=1, source_target_pairs={{0,16},{16,0},{32,48},{48,32},{64,80},{80,64},{96,112},{112,96},{1... | collective-permute-start | bytes 1179656 | tf_op jit(solution)/shard_map/ppermute | solution.py:294
  41.0 2.8 %collective-permute-start.4 = (bf16[512,384]{1,0:T(8,128)(2,1)S(1)}, bf16[512,384]{1,0:T(8,128)(2,1)S(1)}, u32[]{:S(2)}, u32[]{:S(2)}) collective-permute-start(bf16[512,384]{1,0:T(8,128)(2,1)S(1)} %pad_maximum_fusion.refs_0_.refs_8_), channel_id=1, source_target_pairs={{0,12},{1,13},{2,14},{3,15},{4,0},{5,1},{6,2},{7,3},{8,4},{9,5},{1... | collective-permute-start | bytes 1179656 | tf_op jit(solution)/shard_map/ppermute | solution.py:285
  44.8 2.4 %collective-permute-start.8 = (bf16[128,256]{1,0:T(8,128)(2,1)S(1)}, bf16[128,256]{1,0:T(8,128)(2,1)S(1)}, u32[]{:S(2)}, u32[]{:S(2)}) collective-permute-start(bf16[128,256]{1,0:T(8,128)(2,1)S(1)} %slice.109), channel_id=1, source_target_pairs={{0,3},{1,0},{2,1},{3,2},{4,7},{5,4},{6,5},{7,6},{8,11},{9,8},{10,9... | collective-permute-start | bytes 196616 | tf_op jit(solution)/shard_map/ppermute | solution.py:290
  53.4 2.4 %collective-permute-start.11 = (bf16[512,256]{1,0:T(8,128)(2,1)}, bf16[512,256]{1,0:T(8,128)(2,1)S(1)}, u32[]{:S(2)}, u32[]{:S(2)}) collective-permute-start(bf16[512,256]{1,0:T(8,128)(2,1)} %constant_dynamic-update-slice_fusion.refs_0_), channel_id=1, source_target_pairs={{0,16},{16,0},{32,48},{48,32},{64,80},{80,64},{96,112},{112,96},{1... | collective-permute-start | bytes 786440 | tf_op jit(solution)/shard_map/ppermute | solution.py:294
  55.8 8.9 %collective-permute-done.6.refs_3_.refs_11_ = bf16[512,384]{1,0:T(8,128)(2,1)S(1)} collective-permute-done((bf16[512,384]{1,0:T(8,128)(2,1)S(1)}, bf16[512,384]{1,0:T(8,128)(2,1)S(1)}, u32[]{:S(2)}, u32[]{:S(2)}) %collective-permute-start.6) | collective-permute-done | bytes 393248 | tf_op jit(solution)/shard_map/ppermute | solution.py:285
  66.4 2.7 %collective-permute-start.15 = (bf16[512,256]{1,0:T(8,128)(2,1)}, bf16[512,256]{1,0:T(8,128)(2,1)}, u32[]{:S(2)}, u32[]{:S(2)}) collective-permute-start(bf16[512,256]{1,0:T(8,128)(2,1)} %constant_dynamic-update-slice_fusion.refs_0_), channel_id=1, source_target_pairs={{0,12},{1,13},{2,14},{3,15},{4,0},{5,1},{6,2},{7,3},{8,4},{9,5},{1... | collective-permute-start | bytes 786440 | tf_op jit(solution)/shard_map/ppermute | solution.py:285
  82.7 3.9 %shard_map.156 = (bf16[2048,128]{1,0:T(8,128)(2,1)S(1)}, bf16[512,128]{1,0:T(8,128)(2,1)S(1)}, bf16[512,128]{1,0:T(8,128)(2,1)S(1)}, f32[2048,128]{1,0:T(8,128)S...) custom-call(s32[1]{0:T(128)} %bitcast.6.first_ref, f32[512,384]{1,0:T(8,128)S(1)} %copy-done.23, ...), custom_call_target="tpu_custom_call" | custom-call | flops 536870912 | bytes 1048576 | tf_op jit(solution)/shard_map/pallas_call | solution.py:427
  94.8 2.7 %collective-permute-done.20.refs_6_ = bf16[512,256]{1,0:T(8,128)(2,1)S(1)} collective-permute-done((bf16[512,256]{1,0:T(8,128)(2,1)}, bf16[512,256]{1,0:T(8,128)(2,1)S(1)}, u32[]{:S(2)}, u32[]{:S(2)}) %collective-permute-start.20) | collective-permute-done | bytes 262176 | tf_op jit(solution)/shard_map/ppermute | solution.py:294
  97.4 2.7 %shard_map.158 = (bf16[512,256]{1,0:T(8,128)(2,1)S(1)}, bf16[512,256]{1,0:T(8,128)(2,1)S(1)}) custom-call(bf16[1024,2048]{1,0:T(8,128)(2,1)S(1)} %copy-done.3, bf16[512,256]{1,0:T(8,128)(2,1)} %constant_dynamic-update-slice_fusion.refs_0_, bf16[512,256]{1,0:T(8,128)(2,1)} %collective-permute-done.15.refs_1_, ...), custom_call_target="tpu_custom_call" | custom-call | flops 1073741824 | bytes 524288 | tf_op jit(solution)/shard_map/pallas_call | solution.py:437
  112.2 3.5 %shard_map.159 = (bf16[512,384]{1,0:T(8,128)(2,1)S(1)}, bf16[512,384]{1,0:T(8,128)(2,1)S(1)}) custom-call(s32[1]{0:T(128)} %bitcast.6.first_ref, f32[512,384]{1,0:T(8,128)S(1)} %copy-done.24, f32[512,384]{1,0:T(8,128)S(1)} %copy-done.27, f32[1,128]{1,0:T(1,128)S(1)} %bitcast.28, f32[1,128]{1,0:T(1,128)S(1)} %bitcast.30, ...), custom_call_target="tpu_custom_call" | custom-call | flops 536870912 | bytes 1048576 | tf_op jit(solution)/shard_map/pallas_call | solution.py:442
  117.9 2.4 %shard_map.160 = (bf16[512,384]{1,0:T(8,128)(2,1)S(1)}, bf16[512,384]{1,0:T(8,128)(2,1)S(1)}, bf16[512,384]{1,0:T(8,128)(2,1)S(1)}, bf16[512,384]{1,0:T(8,128)(2,1)S(1)}, bf16[2048,384]{1,0:T(8,128)(2,1)S(1)}) custom-call(bf16[1024,2048]{1,0:T(8,128)(2,1)S(1)} %copy-done.4, bf16[512,384]{1,0:T(8,128)(2,1)S(1)} %get-tuple-element.87.own_ref.g_own_ref, ...), custom_call_target="tpu_custom_call" | custom-call | bytes 3145728 | tf_op jit(solution)/shard_map/pallas_call | solution.py:447
  124.5 4.8 %shard_map.161 = bf16[1024,2048]{1,0:T(8,128)(2,1)S(1)} custom-call(bf16[512,256]{1,0:T(8,128)(2,1)S(1)} %copy-done.17, bf16[512,256]{1,0:T(8,128)(2,1)S(1)} %copy-done.19, bf16[512,384]{1,0:T(8,128)(2,1)S(1)} %get-tuple-element.87.own_ref.g_own_ref, bf16[512,384]{1,0:T(8,128)(2,1)S(1)} %get-tuple-element.88.other_ref.g_other_ref, ...), custom_call_target="tpu_custom_call" | custom-call | flops 2684354560 | bytes 4194304 | tf_op jit(solution)/shard_map/pallas_call | solution.py:454
  133.1 3.0 %collective-permute-done.22 = bf16[2048,384]{1,0:T(8,128)(2,1)S(1)} collective-permute-done((bf16[2048,384]{1,0:T(8,128)(2,1)S(1)}, bf16[2048,384]{1,0:T(8,128)(2,1)S(1)}, u32[]{:S(2)}, u32[]{:S(2)}) %collective-permute-start.22) | collective-permute-done | bytes 1572896 | tf_op jit(solution)/shard_map/ppermute | solution.py:294
  139.3 9.0 %collective-permute-done.23 = bf16[512,384]{1,0:T(8,128)(2,1)} collective-permute-done((bf16[512,384]{1,0:T(8,128)(2,1)S(1)}, bf16[512,384]{1,0:T(8,128)(2,1)}, u32[]{:S(2)}, u32[]{:S(2)}) %collective-permute-start.23) | collective-permute-done | bytes 393248 | tf_op jit(solution)/shard_map/ppermute | solution.py:285
  151.4 3.2 %collective-permute-start.27 = (bf16[128,256]{1,0:T(8,128)(2,1)S(1)}, bf16[128,256]{1,0:T(8,128)(2,1)S(1)}, u32[]{:S(2)}, u32[]{:S(2)}) collective-permute-start(bf16[128,256]{1,0:T(8,128)(2,1)S(1)} %get-tuple-element.137), channel_id=1, source_target_pairs={{0,2},{1,3},{2,0},{3,1},{4,6},{5,7},{6,4},{7,5},{8,10},{9,11},{10,... | collective-permute-start | bytes 196616 | tf_op jit(solution)/shard_map/ppermute | solution.py:290
  154.7 2.6 %collective-permute-done.27 = bf16[128,256]{1,0:T(8,128)(2,1)S(1)} collective-permute-done((bf16[128,256]{1,0:T(8,128)(2,1)S(1)}, bf16[128,256]{1,0:T(8,128)(2,1)S(1)}, u32[]{:S(2)}, u32[]{:S(2)}) %collective-permute-start.27) | collective-permute-done | bytes 65568 | tf_op jit(solution)/shard_map/ppermute | solution.py:290
  157.3 3.0 %collective-permute-done.28 = bf16[128,256]{1,0:T(8,128)(2,1)S(1)} collective-permute-done((bf16[128,256]{1,0:T(8,128)(2,1)S(1)}, bf16[128,256]{1,0:T(8,128)(2,1)S(1)}, u32[]{:S(2)}, u32[]{:S(2)}) %collective-permute-start.28) | collective-permute-done | bytes 65568 | tf_op jit(solution)/shard_map/ppermute | solution.py:290
  166.5 5.2 %collective-permute-done.30 = bf16[128,384]{1,0:T(8,128)(2,1)S(1)} collective-permute-done((bf16[128,384]{1,0:T(8,128)(2,1)S(1)}, bf16[128,384]{1,0:T(8,128)(2,1)S(1)}, u32[]{:S(2)}, u32[]{:S(2)}) %collective-permute-start.30) | collective-permute-done | bytes 98336 | tf_op jit(solution)/shard_map/ppermute | solution.py:290
  171.6 2.9 %collective-permute-done.31 = bf16[128,384]{1,0:T(8,128)(2,1)S(1)} collective-permute-done((bf16[128,384]{1,0:T(8,128)(2,1)S(1)}, bf16[128,384]{1,0:T(8,128)(2,1)S(1)}, u32[]{:S(2)}, u32[]{:S(2)}) %collective-permute-start.31) | collective-permute-done | bytes 98336 | tf_op jit(solution)/shard_map/ppermute | solution.py:290
  175.9 14.4 %collective-permute-done.32 = bf16[128,640]{1,0:T(8,128)(2,1)S(1)} collective-permute-done((bf16[128,640]{1,0:T(8,128)(2,1)S(1)}, bf16[128,640]{1,0:T(8,128)(2,1)S(1)}, u32[]{:S(2)}, u32[]{:S(2)}) %collective-permute-start.32) | collective-permute-done | bytes 163872 | tf_op jit(solution)/shard_map/ppermute | solution.py:310
  197.0 2.4 %shard_map.162 = (bf16[128,2048]{1,0:T(8,128)(2,1)}, bf16[128,2048]{1,0:T(8,128)(2,1)}) custom-call(s32[2]{0:T(128)S(1)} %pad_add_fusion.place_ref, bf16[128,2048]{1,0:T(8,128)(2,1)S(1)} %bitcast.22, f32[1,2048]{1,0:T(1,128)S(1)} %bitcast.26, bf16[128,2048]{1,0:T(8,128)(2,1)S(1)} %bitcast.24, f32[128,1]{1,0:T(8,128)S(1)} %copy.19.weight_ref, ...), custom_call_target="tpu_custom_call" | custom-call | bytes 1048576 | tf_op jit(solution)/shard_map/pallas_call | solution.py:470
  (217 shorter events, 93.4 us)
Async XLA Ops:
  7.2 62.0 %all-gather.2.cloned.1.call-start = ((), (), s32[]{:S(2)}) async-start(), calls=%async_computation.2 | async-start | bytes 5242880 | tf_op jit(solution)/shard_map/all_gather | solution.py:265
  15.6 133.8 %reduce-scatter.5.cloned.1.call-start = ((), (), s32[]{:S(2)}) async-start(), calls=%async_computation.4 | async-start | bytes 1310720 | tf_op jit(solution)/shard_map/reduce_scatter | solution.py:272
  15.6 14.4 %collective-permute-start = (bf16[128,640]{1,0:T(8,128)(2,1)S(1)}, bf16[128,640]{1,0:T(8,128)(2,1)S(1)}, u32[]{:S(2)}, u32[]{:S(2)}) collective-permute-start(bf16[128,640]{1,0:T(8,128)(2,1)S(1)} %pad_maximum_fusion.2), channel_id=1, source_target_pairs={{0,128},{16,144},{32,160},{48,176},{192,64},{208,80},{224,96},{240... | collective-permute-start | bytes 491528 | tf_op jit(solution)/shard_map/ppermute | solution.py:304
  37.0 7.8 %collective-permute-start.7 = (bf16[512,384]{1,0:T(8,128)(2,1)S(1)}, bf16[512,384]{1,0:T(8,128)(2,1)S(1)}, u32[]{:S(2)}, u32[]{:S(2)}) collective-permute-start(bf16[512,384]{1,0:T(8,128)(2,1)S(1)} %pad_maximum_fusion.refs_0_.refs_8_), channel_id=1, source_target_pairs={{0,16},{16,0},{32,48},{48,32},{64,80},{80,64},{96,112},{112,96},{1... | collective-permute-start | bytes 1179656 | tf_op jit(solution)/shard_map/ppermute | solution.py:294
  41.0 25.0 %collective-permute-start.4 = (bf16[512,384]{1,0:T(8,128)(2,1)S(1)}, bf16[512,384]{1,0:T(8,128)(2,1)S(1)}, u32[]{:S(2)}, u32[]{:S(2)}) collective-permute-start(bf16[512,384]{1,0:T(8,128)(2,1)S(1)} %pad_maximum_fusion.refs_0_.refs_8_), channel_id=1, source_target_pairs={{0,12},{1,13},{2,14},{3,15},{4,0},{5,1},{6,2},{7,3},{8,4},{9,5},{1... | collective-permute-start | bytes 1179656 | tf_op jit(solution)/shard_map/ppermute | solution.py:285
  43.7 22.2 %collective-permute-start.5 = (bf16[512,384]{1,0:T(8,128)(2,1)S(1)}, bf16[512,384]{1,0:T(8,128)(2,1)S(1)}, u32[]{:S(2)}, u32[]{:S(2)}) collective-permute-start(bf16[512,384]{1,0:T(8,128)(2,1)S(1)} %pad_maximum_fusion.refs_0_.refs_8_), channel_id=1, source_target_pairs={{0,8},{1,9},{2,10},{3,11},{4,12},{5,13},{6,14},{7,15},{8,0},{9,1},... | collective-permute-start | bytes 1179656 | tf_op jit(solution)/shard_map/ppermute | solution.py:285
  44.1 20.6 %collective-permute-start.6 = (bf16[512,384]{1,0:T(8,128)(2,1)S(1)}, bf16[512,384]{1,0:T(8,128)(2,1)S(1)}, u32[]{:S(2)}, u32[]{:S(2)}) collective-permute-start(bf16[512,384]{1,0:T(8,128)(2,1)S(1)} %pad_maximum_fusion.refs_0_.refs_8_), channel_id=1, source_target_pairs={{0,4},{1,5},{2,6},{3,7},{4,8},{5,9},{6,10},{7,11},{8,12},{9,13},{1... | collective-permute-start | bytes 1179656 | tf_op jit(solution)/shard_map/ppermute | solution.py:285
  53.4 11.3 %collective-permute-start.11 = (bf16[512,256]{1,0:T(8,128)(2,1)}, bf16[512,256]{1,0:T(8,128)(2,1)S(1)}, u32[]{:S(2)}, u32[]{:S(2)}) collective-permute-start(bf16[512,256]{1,0:T(8,128)(2,1)} %constant_dynamic-update-slice_fusion.refs_0_), channel_id=1, source_target_pairs={{0,16},{16,0},{32,48},{48,32},{64,80},{80,64},{96,112},{112,96},{1... | collective-permute-start | bytes 786440 | tf_op jit(solution)/shard_map/ppermute | solution.py:294
  66.4 9.4 %collective-permute-start.16 = (bf16[512,256]{1,0:T(8,128)(2,1)}, bf16[512,256]{1,0:T(8,128)(2,1)}, u32[]{:S(2)}, u32[]{:S(2)}) collective-permute-start(bf16[512,256]{1,0:T(8,128)(2,1)} %constant_dynamic-update-slice_fusion.refs_0_), channel_id=1, source_target_pairs={{0,4},{1,5},{2,6},{3,7},{4,8},{5,9},{6,10},{7,11},{8,12},{9,13},{1... | collective-permute-start | bytes 786440 | tf_op jit(solution)/shard_map/ppermute | solution.py:285
  66.4 10.3 %collective-permute-start.15 = (bf16[512,256]{1,0:T(8,128)(2,1)}, bf16[512,256]{1,0:T(8,128)(2,1)}, u32[]{:S(2)}, u32[]{:S(2)}) collective-permute-start(bf16[512,256]{1,0:T(8,128)(2,1)} %constant_dynamic-update-slice_fusion.refs_0_), channel_id=1, source_target_pairs={{0,12},{1,13},{2,14},{3,15},{4,0},{5,1},{6,2},{7,3},{8,4},{9,5},{1... | collective-permute-start | bytes 786440 | tf_op jit(solution)/shard_map/ppermute | solution.py:285
  75.8 13.8 %collective-permute-start.19 = (bf16[512,256]{1,0:T(8,128)(2,1)}, bf16[512,256]{1,0:T(8,128)(2,1)}, u32[]{:S(2)}, u32[]{:S(2)}) collective-permute-start(bf16[512,256]{1,0:T(8,128)(2,1)} %collective-permute-done.16.refs_3_), channel_id=1, source_target_pairs={{0,16},{16,0},{32,48},{48,32},{64,80},{80,64},{96,112},{112,96},{1... | collective-permute-start | bytes 786440 | tf_op jit(solution)/shard_map/ppermute | solution.py:294
  76.7 12.9 %collective-permute-start.18 = (bf16[512,256]{1,0:T(8,128)(2,1)}, bf16[512,256]{1,0:T(8,128)(2,1)}, u32[]{:S(2)}, u32[]{:S(2)}) collective-permute-start(bf16[512,256]{1,0:T(8,128)(2,1)} %collective-permute-done.15.refs_1_), channel_id=1, source_target_pairs={{0,16},{16,0},{32,48},{48,32},{64,80},{80,64},{96,112},{112,96},{1... | collective-permute-start | bytes 786440 | tf_op jit(solution)/shard_map/ppermute | solution.py:294
  76.7 12.9 %collective-permute-start.17 = (bf16[512,256]{1,0:T(8,128)(2,1)}, bf16[512,256]{1,0:T(8,128)(2,1)}, u32[]{:S(2)}, u32[]{:S(2)}) collective-permute-start(bf16[512,256]{1,0:T(8,128)(2,1)} %constant_dynamic-update-slice_fusion.refs_0_), channel_id=1, source_target_pairs={{0,8},{1,9},{2,10},{3,11},{4,12},{5,13},{6,14},{7,15},{8,0},{9,1},... | collective-permute-start | bytes 786440 | tf_op jit(solution)/shard_map/ppermute | solution.py:285
  93.9 7.7 %collective-permute-start.21 = (bf16[2048,256]{1,0:T(8,128)(2,1)S(1)}, bf16[2048,256]{1,0:T(8,128)(2,1)S(1)}, u32[]{:S(2)}, u32[]{:S(2)}) collective-permute-start(bf16[2048,256]{1,0:T(8,128)(2,1)S(1)} %get-tuple-element.76), channel_id=1, source_target_pairs={{0,16},{16,0},{32,48},{48,32},{64,80},{80,64},{96,112},{112,96},{1... | collective-permute-start | bytes 3145736 | tf_op jit(solution)/shard_map/ppermute | solution.py:294
  102.8 92.9 %reduce-scatter.3.cloned.1.call-start = ((), (), s32[]{:S(2)}) async-start(), calls=%async_computation.3 | async-start | bytes 5242880 | tf_op jit(solution)/shard_map/reduce_scatter | solution.py:278
  136.5 11.7 %collective-permute-start.23 = (bf16[512,384]{1,0:T(8,128)(2,1)S(1)}, bf16[512,384]{1,0:T(8,128)(2,1)}, u32[]{:S(2)}, u32[]{:S(2)}) collective-permute-start(bf16[512,384]{1,0:T(8,128)(2,1)S(1)} %get-tuple-element.96), channel_id=1, source_target_pairs={{0,4},{1,5},{2,6},{3,7},{4,8},{5,9},{6,10},{7,11},{8,12},{9,13},{1... | collective-permute-start | bytes 1179656 | tf_op jit(solution)/shard_map/ppermute | solution.py:285
  138.0 10.2 %collective-permute-start.24 = (bf16[512,384]{1,0:T(8,128)(2,1)S(1)}, bf16[512,384]{1,0:T(8,128)(2,1)}, u32[]{:S(2)}, u32[]{:S(2)}) collective-permute-start(bf16[512,384]{1,0:T(8,128)(2,1)S(1)} %get-tuple-element.97), channel_id=1, source_target_pairs={{0,12},{1,13},{2,14},{3,15},{4,0},{5,1},{6,2},{7,3},{8,4},{9,5},{1... | collective-permute-start | bytes 1179656 | tf_op jit(solution)/shard_map/ppermute | solution.py:285
  148.2 12.9 %collective-permute-start.25 = (bf16[512,384]{1,0:T(8,128)(2,1)S(1)}, bf16[512,384]{1,0:T(8,128)(2,1)S(1)}, u32[]{:S(2)}, u32[]{:S(2)}) collective-permute-start(bf16[512,384]{1,0:T(8,128)(2,1)S(1)} %get-tuple-element.99), channel_id=1, source_target_pairs={{0,8},{1,9},{2,10},{3,11},{4,12},{5,13},{6,14},{7,15},{8,0},{9,1},... | collective-permute-start | bytes 1179656 | tf_op jit(solution)/shard_map/ppermute | solution.py:285
  162.6 9.0 %collective-permute-start.30 = (bf16[128,384]{1,0:T(8,128)(2,1)S(1)}, bf16[128,384]{1,0:T(8,128)(2,1)S(1)}, u32[]{:S(2)}, u32[]{:S(2)}) collective-permute-start(bf16[128,384]{1,0:T(8,128)(2,1)S(1)} %get-tuple-element.122), channel_id=1, source_target_pairs={{0,2},{1,3},{2,0},{3,1},{4,6},{5,7},{6,4},{7,5},{8,10},{9,11},{10,... | collective-permute-start | bytes 294920 | tf_op jit(solution)/shard_map/ppermute | solution.py:290
  164.8 9.7 %collective-permute-start.31 = (bf16[128,384]{1,0:T(8,128)(2,1)S(1)}, bf16[128,384]{1,0:T(8,128)(2,1)S(1)}, u32[]{:S(2)}, u32[]{:S(2)}) collective-permute-start(bf16[128,384]{1,0:T(8,128)(2,1)S(1)} %get-tuple-element.121), channel_id=1, source_target_pairs={{0,3},{1,0},{2,1},{3,2},{4,7},{5,4},{6,5},{7,6},{8,11},{9,8},{10,9... | collective-permute-start | bytes 294920 | tf_op jit(solution)/shard_map/ppermute | solution.py:290
  174.6 15.7 %collective-permute-start.32 = (bf16[128,640]{1,0:T(8,128)(2,1)S(1)}, bf16[128,640]{1,0:T(8,128)(2,1)S(1)}, u32[]{:S(2)}, u32[]{:S(2)}) collective-permute-start(bf16[128,640]{1,0:T(8,128)(2,1)S(1)} %pad_maximum_fusion.3), channel_id=1, source_target_pairs={{128,0},{144,16},{160,32},{176,48},{64,192},{80,208},{96,224},{112... | collective-permute-start | bytes 491528 | tf_op jit(solution)/shard_map/ppermute | solution.py:310
  190.3 9.2 %collective-permute-start.33 = (bf16[128,640]{1,0:T(8,128)(2,1)S(1)}, bf16[128,640]{1,0:T(8,128)(2,1)S(1)}, u32[]{:S(2)}, u32[]{:S(2)}) collective-permute-start(bf16[128,640]{1,0:T(8,128)(2,1)S(1)} %add_convert_fusion.6), channel_id=1, source_target_pairs={{0,96},{16,112},{32,0},{48,16},{192,160},{208,176},{224,192},{240,... | collective-permute-start | bytes 491528 | tf_op jit(solution)/shard_map/ppermute | solution.py:320
  192.4 7.0 %collective-permute-start.34 = (bf16[128,640]{1,0:T(8,128)(2,1)S(1)}, bf16[128,640]{1,0:T(8,128)(2,1)S(1)}, u32[]{:S(2)}, u32[]{:S(2)}) collective-permute-start(bf16[128,640]{1,0:T(8,128)(2,1)S(1)} %add_convert_fusion.6), channel_id=1, source_target_pairs={{0,64},{16,80},{32,96},{48,112},{192,128},{208,144},{224,160},{240... | collective-permute-start | bytes 491528 | tf_op jit(solution)/shard_map/ppermute | solution.py:320
  193.7 7.1 %collective-permute-start.35 = (bf16[128,640]{1,0:T(8,128)(2,1)S(1)}, bf16[128,640]{1,0:T(8,128)(2,1)S(1)}, u32[]{:S(2)}, u32[]{:S(2)}) collective-permute-start(bf16[128,640]{1,0:T(8,128)(2,1)S(1)} %add_convert_fusion.6), channel_id=1, source_target_pairs={{0,32},{16,48},{32,64},{48,80},{192,224},{208,240},{224,128},{240,... | collective-permute-start | bytes 491528 | tf_op jit(solution)/shard_map/ppermute | solution.py:320
  (70 other events, 325.6 us)
Sparse Core Ops, SparseCore 0:
  15.7 52.7 all-gather.1
  102.9 25.5 reduce-scatter.4
  131.4 49.4 reduce-scatter.2

commit v2 on v1

--- a/solution.py
+++ b/solution.py
@@ -46,9 +46,9 @@
         ),
         out_shape=[jax.ShapeDtypeStruct(shape, kind) for shape, kind in outs],
         in_specs=[pl.BlockSpec(memory_space=pltpu.SMEM)] * scalars
-        + [pl.BlockSpec(memory_space=pltpu.VMEM)] * (vmem - scalars),
-        out_specs=[pl.BlockSpec(memory_space=pltpu.VMEM)] * len(outs),
-        compiler_params=pltpu.CompilerParams(vmem_limit_bytes=16 << 20),
+        + [pl.BlockSpec()] * (vmem - scalars),
+        out_specs=[pl.BlockSpec()] * len(outs),
+        compiler_params=pltpu.CompilerParams(vmem_limit_bytes=56 << 20),
         **more,
     )
 
@@ -219,7 +219,7 @@
         out_shape=[jax.ShapeDtypeStruct((rows * NX, cols), kind) for rows, cols, kind in outs],
         in_specs=[pl.BlockSpec(memory_space=pltpu.SMEM)] + [spec(*entry) for entry in ins],
         out_specs=[spec(rows, cols) for rows, cols, _ in outs],
-        compiler_params=pltpu.CompilerParams(vmem_limit_bytes=16 << 20),
+        compiler_params=pltpu.CompilerParams(vmem_limit_bytes=56 << 20),
     )
 
 

time: 215 us -> 203 us (0.944)
  local copies, waits for them, and re-layouts: 43.1 us -> 8.73 us
  Pallas kernels: 25.9 us -> 48.9 us
    unnamed x113 -> x43, local copies, waits for them, and re-layouts: 40.4 us -> 5.5 us
    pallas_call x1, Pallas kernels: 2.32 us -> 6.29 us  [on_device(): call(partial(project_kernel, 0), [((tokens, wide), f32)] * 2, 1 + 2 * NY,...]
    pallas_call x1, Pallas kernels: 2.38 us -> 6.09 us  [on_device(): call(weight_grad_kernel, [((span, wide), bf16)] * NY + [((NY * span, wide...]
    pallas_call x1, Pallas kernels: 4.82 us -> 8.5 us  [on_device(): call(expand_kernel, [((2 * tokens, flat[1]), bf16)], 4 + 4 * NY, scalars=...]
    pallas_call x1, Pallas kernels: 1.83 us -> 5.04 us  [on_device(): call(grad_o_kernel, [((NY * span, half), bf16)] * 2, 4, macs=tokens * fla...]
    pallas_call x1, Pallas kernels: 3.53 us -> 6.18 us  [on_device(): by_trajectory(attend_back_kernel, [(TRAJ, wide, bf16)] * 2, [(TRAJ, wide)...]
  transfers between devices with their start and end apart: 40 -> 40, of which waited for: 20 -> 20; matrix products, arithmetic and copies ran while one was open for 4% -> 3% of each run, Pallas kernels for 10% -> 20%
where the time goes in v2:
time: 203 us; the launch traced here: 201 us
  waiting for transfers between devices  68.2 us (34%)
  starting transfers between devices  52.7 us (26%)
  Pallas kernels  48.9 us (24%)
  between operations  14.3 us (7%)
  local copies, waits for them, and re-layouts  8.73 us (4%)
  other arithmetic  8.56 us (4%)
    ppermute x12, waiting for transfers between devices, take_z(): return lax.ppermute(value, 'fsdp', pairs)  20.5 us
    ppermute x9, waiting for transfers between devices, take_y(): return lax.ppermute(value, 'fsdp', pairs)  18.4 us
    ppermute x1, waiting for transfers between devices, to_owner(): return lax.ppermute(value, ('role', 'dp'), pairs)  14.1 us
    ppermute x12, starting transfers between devices, take_z(): return lax.ppermute(value, 'fsdp', pairs)  13 us
    ppermute x9, starting transfers between devices, take_y(): return lax.ppermute(value, 'fsdp', pairs)  12.7 us
    ppermute x11, starting transfers between devices, other_core(): return lax.ppermute(value, 'dp', [(i, i ^ 1) for i in range(NX * NC)])  11.9 us
    pallas_call x1, Pallas kernels, on_device(): call(expand_kernel, [((2 * tokens, flat[1]), bf16)], 4 + 4 * NY, scalars=...  8.5 us
    ppermute x1, starting transfers between devices, from_owner(): return lax.ppermute(value, ('role', 'dp'), pairs)  7.92 us
  transfers between devices with their start and end apart: 40, of which 20 were waited for; matrix products, arithmetic and copies ran while one was open for 3% of the time, Pallas kernels for 20%

profile of v2, /device:TPU:35, one launch (start us, length us, event | category | flops | bytes accessed | tf_op | source)
XLA Modules:
  0.0 201.5 jit_solution(10398087406380084787)
XLA Ops:
  12.0 2.7 %shard_map.154 = bf16[256,2048]{1,0:T(8,128)(2,1)} custom-call(s32[2]{0:T(128)} %pad_add_fusion.place_ref, bf16[128,2048]{1,0:T(8,128)(2,1)} %bitcast.21, f32[1,2048]{1,0:T(1,128)} %bitcast.27, bf16[128,2048]{1,0:T(8,128)(2,1)} %bitcast.23, f32[128,1]{1,0:T(8,128)} %copy.19.weight_ref), custom_call_target="tpu_custom_call" | custom-call | bytes 1048576 | tf_op jit(solution)/shard_map/pallas_call | solution.py:403
  14.8 7.9 %collective-permute-start = (bf16[128,640]{1,0:T(8,128)(2,1)S(1)}, bf16[128,640]{1,0:T(8,128)(2,1)S(1)}, u32[]{:S(2)}, u32[]{:S(2)}) collective-permute-start(bf16[128,640]{1,0:T(8,128)(2,1)S(1)} %pad_maximum_fusion.2), channel_id=1, source_target_pairs={{0,128},{16,144},{32,160},{48,176},{192,64},{208,80},{224,96},{240... | collective-permute-start | bytes 491528 | tf_op jit(solution)/shard_map/ppermute | solution.py:304
  22.7 6.4 %collective-permute-done = bf16[128,640]{1,0:T(8,128)(2,1)S(1)} collective-permute-done((bf16[128,640]{1,0:T(8,128)(2,1)S(1)}, bf16[128,640]{1,0:T(8,128)(2,1)S(1)}, u32[]{:S(2)}, u32[]{:S(2)}) %collective-permute-start) | collective-permute-done | bytes 163872 | tf_op jit(solution)/shard_map/ppermute | solution.py:304
  29.3 2.8 %collective-permute-start.2 = (bf16[128,384]{1,0:T(8,128)(2,1)S(1)}, bf16[128,384]{1,0:T(8,128)(2,1)S(1)}, u32[]{:S(2)}, u32[]{:S(2)}) collective-permute-start(bf16[128,384]{1,0:T(8,128)(2,1)S(1)} %slice.108), channel_id=1, source_target_pairs={{0,2},{1,3},{2,0},{3,1},{4,6},{5,7},{6,4},{7,5},{8,10},{9,11},{10,... | collective-permute-start | bytes 294920 | tf_op jit(solution)/shard_map/ppermute | solution.py:290
  36.1 4.0 %collective-permute-start.7 = (bf16[512,384]{1,0:T(8,128)(2,1)S(1)}, bf16[512,384]{1,0:T(8,128)(2,1)S(1)}, u32[]{:S(2)}, u32[]{:S(2)}) collective-permute-start(bf16[512,384]{1,0:T(8,128)(2,1)S(1)} %pad_maximum_fusion.refs_0_.refs_8_), channel_id=1, source_target_pairs={{0,16},{16,0},{32,48},{48,32},{64,80},{80,64},{96,112},{112,96},{1... | collective-permute-start | bytes 1179656 | tf_op jit(solution)/shard_map/ppermute | solution.py:294
  40.1 2.8 %collective-permute-start.4 = (bf16[512,384]{1,0:T(8,128)(2,1)S(1)}, bf16[512,384]{1,0:T(8,128)(2,1)S(1)}, u32[]{:S(2)}, u32[]{:S(2)}) collective-permute-start(bf16[512,384]{1,0:T(8,128)(2,1)S(1)} %pad_maximum_fusion.refs_0_.refs_8_), channel_id=1, source_target_pairs={{0,12},{1,13},{2,14},{3,15},{4,0},{5,1},{6,2},{7,3},{8,4},{9,5},{1... | collective-permute-start | bytes 1179656 | tf_op jit(solution)/shard_map/ppermute | solution.py:285
  55.0 8.9 %collective-permute-done.6.refs_3_.refs_11_ = bf16[512,384]{1,0:T(8,128)(2,1)S(1)} collective-permute-done((bf16[512,384]{1,0:T(8,128)(2,1)S(1)}, bf16[512,384]{1,0:T(8,128)(2,1)S(1)}, u32[]{:S(2)}, u32[]{:S(2)}) %collective-permute-start.6) | collective-permute-done | bytes 393248 | tf_op jit(solution)/shard_map/ppermute | solution.py:285
  65.1 2.7 %collective-permute-start.15 = (bf16[512,256]{1,0:T(8,128)(2,1)}, bf16[512,256]{1,0:T(8,128)(2,1)}, u32[]{:S(2)}, u32[]{:S(2)}) collective-permute-start(bf16[512,256]{1,0:T(8,128)(2,1)} %constant_dynamic-update-slice_fusion.refs_0_), channel_id=1, source_target_pairs={{0,12},{1,13},{2,14},{3,15},{4,0},{5,1},{6,2},{7,3},{8,4},{9,5},{1... | collective-permute-start | bytes 786440 | tf_op jit(solution)/shard_map/ppermute | solution.py:285
  68.8 6.3 %shard_map.155 = (f32[512,384]{1,0:T(8,128)}, f32[512,384]{1,0:T(8,128)}) custom-call(bf16[1024,2048]{1,0:T(8,128)(2,1)} %all-gather.2.cloned.1.call-done.pair_ref, bf16[512,384]{1,0:T(8,128)(2,1)} %copy-done.1, bf16[512,384]{1,0:T(8,128)(2,1)} %copy-done.3, bf16[512,384]{1,0:T(8,128)(2,1)} %copy-done.4, bf16[512,384]{1,0:T(8,128)(2,1)} %copy-done.5, ...), custom_call_target="tpu_custom_call" | custom-call | flops 1610612736 | bytes 786432 | tf_op jit(solution)/shard_map/pallas_call | solution.py:418
  78.6 5.8 %shard_map.156 = (bf16[2048,128]{1,0:T(8,128)(2,1)}, bf16[512,128]{1,0:T(8,128)(2,1)}, bf16[512,128]{1,0:T(8,128)(2,1)}, f32[2048,128]{1,0:T(8,128)}, bf16[512,2...) custom-call(s32[1]{0:T(128)} %bitcast.6.first_ref, f32[512,384]{1,0:T(8,128)} %get-tuple-element.64.own_ref, ...), custom_call_target="tpu_custom_call" | custom-call | flops 536870912 | bytes 1048576 | tf_op jit(solution)/shard_map/pallas_call | solution.py:427
  85.1 5.0 %shard_map.157 = (bf16[2048,256]{1,0:T(8,128)(2,1)}, bf16[2048,256]{1,0:T(8,128)(2,1)}) custom-call(s32[2]{0:T(128)} %pad_add_fusion.place_ref, bf16[1024,2048]{1,0:T(8,128)(2,1)} %all-gather.2.cloned.1.call-done.pair_ref, bf16[512,256]{1,0:T(8,128)(2,1)} %get-tuple-element.66.own_ref.mixed_own_ref, bf16[512,256]{1,0:T(8,128)(2,1)} %get-tuple-element.67.other_ref.mixed_other_ref), custom_call_target="tpu_custom_call" | custom-call | flops 1073741824 | bytes 2097152 | tf_op jit(solution)/shard_map/pallas_call | solution.py:434
  94.8 4.8 %shard_map.158 = (bf16[512,256]{1,0:T(8,128)(2,1)}, bf16[512,256]{1,0:T(8,128)(2,1)}) custom-call(bf16[1024,2048]{1,0:T(8,128)(2,1)} %all-gather.2.cloned.1.call-done.pair_ref, bf16[512,256]{1,0:T(8,128)(2,1)} %constant_dynamic-update-slice_fusion.refs_0_, bf16[512,256]{1,0:T(8,128)(2,1)} %collective-permute-done.15.refs_1_, bf16[512,256]{1,0:T(8,128)(2,1)} %copy-done.13, ...), custom_call_target="tpu_custom_call" | custom-call | flops 1073741824 | bytes 524288 | tf_op jit(solution)/shard_map/pallas_call | solution.py:437
  101.1 6.2 %shard_map.159 = (bf16[512,384]{1,0:T(8,128)(2,1)}, bf16[512,384]{1,0:T(8,128)(2,1)}) custom-call(s32[1]{0:T(128)} %bitcast.6.first_ref, f32[512,384]{1,0:T(8,128)} %get-tuple-element.64.own_ref, f32[512,384]{1,0:T(8,128)} %get-tuple-element.65.other_ref, f32[1,128]{1,0:T(1,128)} %bitcast.30, f32[1,128]{1,0:T(1,128)} %bitcast.32, ...), custom_call_target="tpu_custom_call" | custom-call | flops 536870912 | bytes 1048576 | tf_op jit(solution)/shard_map/pallas_call | solution.py:442
  107.3 6.1 %shard_map.160 = (bf16[512,384]{1,0:T(8,128)(2,1)}, bf16[512,384]{1,0:T(8,128)(2,1)}, bf16[512,384]{1,0:T(8,128)(2,1)}, bf16[512,384]{1,0:T(8,128)(2,1)}, bf16[2048,384]{1,0:T(8,128)(2,1)}) custom-call(bf16[1024,2048]{1,0:T(8,128)(2,1)} %all-gather.2.cloned.1.call-done.pair_ref, bf16[512,384]{1,0:T(8,128)(2,1)} %get-tuple-element.87.own_ref.g_own_ref, ...), custom_call_target="tpu_custom_call" | custom-call | bytes 3145728 | tf_op jit(solution)/shard_map/pallas_call | solution.py:447
  113.4 8.5 %shard_map.161 = bf16[1024,2048]{1,0:T(8,128)(2,1)} custom-call(bf16[512,256]{1,0:T(8,128)(2,1)} %get-tuple-element.66.own_ref.mixed_own_ref, bf16[512,256]{1,0:T(8,128)(2,1)} %get-tuple-element.67.other_ref.mixed_other_ref, bf16[512,384]{1,0:T(8,128)(2,1)} %get-tuple-element.87.own_ref.g_own_ref, bf16[512,384]{1,0:T(8,128)(2,1)} %get-tuple-element.88.other_ref.g_other_ref, ...), custom_call_target="tpu_custom_call" | custom-call | flops 2684354560 | bytes 4194304 | tf_op jit(solution)/shard_map/pallas_call | solution.py:454
  122.4 3.2 %collective-permute-done.22 = bf16[2048,384]{1,0:T(8,128)(2,1)S(1)} collective-permute-done((bf16[2048,384]{1,0:T(8,128)(2,1)}, bf16[2048,384]{1,0:T(8,128)(2,1)S(1)}, u32[]{:S(2)}, u32[]{:S(2)}) %collective-permute-start.22) | collective-permute-done | bytes 1572896 | tf_op jit(solution)/shard_map/ppermute | solution.py:294
  126.3 2.6 %collective-permute-start.24 = (bf16[512,384]{1,0:T(8,128)(2,1)S(1)}, bf16[512,384]{1,0:T(8,128)(2,1)S(1)}, u32[]{:S(2)}, u32[]{:S(2)}) collective-permute-start(bf16[512,384]{1,0:T(8,128)(2,1)S(1)} %get-tuple-element.97), channel_id=1, source_target_pairs={{0,12},{1,13},{2,14},{3,15},{4,0},{5,1},{6,2},{7,3},{8,4},{9,5},{1... | collective-permute-start | bytes 1179656 | tf_op jit(solution)/shard_map/ppermute | solution.py:285
  128.8 8.9 %collective-permute-done.23 = bf16[512,384]{1,0:T(8,128)(2,1)S(1)} collective-permute-done((bf16[512,384]{1,0:T(8,128)(2,1)S(1)}, bf16[512,384]{1,0:T(8,128)(2,1)S(1)}, u32[]{:S(2)}, u32[]{:S(2)}) %collective-permute-start.23) | collective-permute-done | bytes 393248 | tf_op jit(solution)/shard_map/ppermute | solution.py:285
  141.9 2.9 %collective-permute-start.27 = (bf16[128,256]{1,0:T(8,128)(2,1)S(1)}, bf16[128,256]{1,0:T(8,128)(2,1)S(1)}, u32[]{:S(2)}, u32[]{:S(2)}) collective-permute-start(bf16[128,256]{1,0:T(8,128)(2,1)S(1)} %get-tuple-element.137), channel_id=1, source_target_pairs={{0,2},{1,3},{2,0},{3,1},{4,6},{5,7},{6,4},{7,5},{8,10},{9,11},{10,... | collective-permute-start | bytes 196616 | tf_op jit(solution)/shard_map/ppermute | solution.py:290
  144.8 2.6 %collective-permute-done.27 = bf16[128,256]{1,0:T(8,128)(2,1)S(1)} collective-permute-done((bf16[128,256]{1,0:T(8,128)(2,1)S(1)}, bf16[128,256]{1,0:T(8,128)(2,1)S(1)}, u32[]{:S(2)}, u32[]{:S(2)}) %collective-permute-start.27) | collective-permute-done | bytes 65568 | tf_op jit(solution)/shard_map/ppermute | solution.py:290
  147.5 2.9 %collective-permute-done.28 = bf16[128,256]{1,0:T(8,128)(2,1)S(1)} collective-permute-done((bf16[128,256]{1,0:T(8,128)(2,1)S(1)}, bf16[128,256]{1,0:T(8,128)(2,1)S(1)}, u32[]{:S(2)}, u32[]{:S(2)}) %collective-permute-start.28) | collective-permute-done | bytes 65568 | tf_op jit(solution)/shard_map/ppermute | solution.py:290
  155.5 4.4 %collective-permute-done.30 = bf16[128,384]{1,0:T(8,128)(2,1)S(1)} collective-permute-done((bf16[128,384]{1,0:T(8,128)(2,1)S(1)}, bf16[128,384]{1,0:T(8,128)(2,1)S(1)}, u32[]{:S(2)}, u32[]{:S(2)}) %collective-permute-start.30) | collective-permute-done | bytes 98336 | tf_op jit(solution)/shard_map/ppermute | solution.py:290
  163.6 14.1 %collective-permute-done.32 = bf16[128,640]{1,0:T(8,128)(2,1)S(1)} collective-permute-done((bf16[128,640]{1,0:T(8,128)(2,1)S(1)}, bf16[128,640]{1,0:T(8,128)(2,1)S(1)}, u32[]{:S(2)}, u32[]{:S(2)}) %collective-permute-start.32) | collective-permute-done | bytes 163872 | tf_op jit(solution)/shard_map/ppermute | solution.py:310
  183.5 3.5 %shard_map.162 = (bf16[128,2048]{1,0:T(8,128)(2,1)}, bf16[128,2048]{1,0:T(8,128)(2,1)}) custom-call(s32[2]{0:T(128)} %pad_add_fusion.place_ref, bf16[128,2048]{1,0:T(8,128)(2,1)} %bitcast.22, f32[1,2048]{1,0:T(1,128)} %bitcast.28, bf16[128,2048]{1,0:T(8,128)(2,1)} %bitcast.24, f32[128,1]{1,0:T(8,128)} %copy.19.weight_ref, ...), custom_call_target="tpu_custom_call" | custom-call | bytes 1048576 | tf_op jit(solution)/shard_map/pallas_call | solution.py:470
  (147 shorter events, 61.1 us)
Async XLA Ops:
  7.2 60.7 %all-gather.2.cloned.1.call-start = ((), (), s32[]{:S(2)}) async-start(), calls=%async_computation.2 | async-start | bytes 5242880 | tf_op jit(solution)/shard_map/all_gather | solution.py:265
  14.7 124.8 %reduce-scatter.5.cloned.1.call-start = ((), (), s32[]{:S(2)}) async-start(), calls=%async_computation.4 | async-start | bytes 1310720 | tf_op jit(solution)/shard_map/reduce_scatter | solution.py:272
  14.8 14.4 %collective-permute-start = (bf16[128,640]{1,0:T(8,128)(2,1)S(1)}, bf16[128,640]{1,0:T(8,128)(2,1)S(1)}, u32[]{:S(2)}, u32[]{:S(2)}) collective-permute-start(bf16[128,640]{1,0:T(8,128)(2,1)S(1)} %pad_maximum_fusion.2), channel_id=1, source_target_pairs={{0,128},{16,144},{32,160},{48,176},{192,64},{208,80},{224,96},{240... | collective-permute-start | bytes 491528 | tf_op jit(solution)/shard_map/ppermute | solution.py:304
  36.1 7.8 %collective-permute-start.7 = (bf16[512,384]{1,0:T(8,128)(2,1)S(1)}, bf16[512,384]{1,0:T(8,128)(2,1)S(1)}, u32[]{:S(2)}, u32[]{:S(2)}) collective-permute-start(bf16[512,384]{1,0:T(8,128)(2,1)S(1)} %pad_maximum_fusion.refs_0_.refs_8_), channel_id=1, source_target_pairs={{0,16},{16,0},{32,48},{48,32},{64,80},{80,64},{96,112},{112,96},{1... | collective-permute-start | bytes 1179656 | tf_op jit(solution)/shard_map/ppermute | solution.py:294
  40.1 24.4 %collective-permute-start.4 = (bf16[512,384]{1,0:T(8,128)(2,1)S(1)}, bf16[512,384]{1,0:T(8,128)(2,1)S(1)}, u32[]{:S(2)}, u32[]{:S(2)}) collective-permute-start(bf16[512,384]{1,0:T(8,128)(2,1)S(1)} %pad_maximum_fusion.refs_0_.refs_8_), channel_id=1, source_target_pairs={{0,12},{1,13},{2,14},{3,15},{4,0},{5,1},{6,2},{7,3},{8,4},{9,5},{1... | collective-permute-start | bytes 1179656 | tf_op jit(solution)/shard_map/ppermute | solution.py:285
  42.9 21.6 %collective-permute-start.5 = (bf16[512,384]{1,0:T(8,128)(2,1)S(1)}, bf16[512,384]{1,0:T(8,128)(2,1)S(1)}, u32[]{:S(2)}, u32[]{:S(2)}) collective-permute-start(bf16[512,384]{1,0:T(8,128)(2,1)S(1)} %pad_maximum_fusion.refs_0_.refs_8_), channel_id=1, source_target_pairs={{0,8},{1,9},{2,10},{3,11},{4,12},{5,13},{6,14},{7,15},{8,0},{9,1},... | collective-permute-start | bytes 1179656 | tf_op jit(solution)/shard_map/ppermute | solution.py:285
  43.2 20.6 %collective-permute-start.6 = (bf16[512,384]{1,0:T(8,128)(2,1)S(1)}, bf16[512,384]{1,0:T(8,128)(2,1)S(1)}, u32[]{:S(2)}, u32[]{:S(2)}) collective-permute-start(bf16[512,384]{1,0:T(8,128)(2,1)S(1)} %pad_maximum_fusion.refs_0_.refs_8_), channel_id=1, source_target_pairs={{0,4},{1,5},{2,6},{3,7},{4,8},{5,9},{6,10},{7,11},{8,12},{9,13},{1... | collective-permute-start | bytes 1179656 | tf_op jit(solution)/shard_map/ppermute | solution.py:285
  52.5 11.3 %collective-permute-start.11 = (bf16[512,256]{1,0:T(8,128)(2,1)}, bf16[512,256]{1,0:T(8,128)(2,1)S(1)}, u32[]{:S(2)}, u32[]{:S(2)}) collective-permute-start(bf16[512,256]{1,0:T(8,128)(2,1)} %constant_dynamic-update-slice_fusion.refs_0_), channel_id=1, source_target_pairs={{0,16},{16,0},{32,48},{48,32},{64,80},{80,64},{96,112},{112,96},{1... | collective-permute-start | bytes 786440 | tf_op jit(solution)/shard_map/ppermute | solution.py:294
  65.1 10.0 %collective-permute-start.16 = (bf16[512,256]{1,0:T(8,128)(2,1)}, bf16[512,256]{1,0:T(8,128)(2,1)}, u32[]{:S(2)}, u32[]{:S(2)}) collective-permute-start(bf16[512,256]{1,0:T(8,128)(2,1)} %constant_dynamic-update-slice_fusion.refs_0_), channel_id=1, source_target_pairs={{0,4},{1,5},{2,6},{3,7},{4,8},{5,9},{6,10},{7,11},{8,12},{9,13},{1... | collective-permute-start | bytes 786440 | tf_op jit(solution)/shard_map/ppermute | solution.py:285
  65.1 10.6 %collective-permute-start.15 = (bf16[512,256]{1,0:T(8,128)(2,1)}, bf16[512,256]{1,0:T(8,128)(2,1)}, u32[]{:S(2)}, u32[]{:S(2)}) collective-permute-start(bf16[512,256]{1,0:T(8,128)(2,1)} %constant_dynamic-update-slice_fusion.refs_0_), channel_id=1, source_target_pairs={{0,12},{1,13},{2,14},{3,15},{4,0},{5,1},{6,2},{7,3},{8,4},{9,5},{1... | collective-permute-start | bytes 786440 | tf_op jit(solution)/shard_map/ppermute | solution.py:285
  75.1 9.3 %collective-permute-start.19 = (bf16[512,256]{1,0:T(8,128)(2,1)}, bf16[512,256]{1,0:T(8,128)(2,1)S(1)}, u32[]{:S(2)}, u32[]{:S(2)}) collective-permute-start(bf16[512,256]{1,0:T(8,128)(2,1)} %collective-permute-done.16.refs_3_), channel_id=1, source_target_pairs={{0,16},{16,0},{32,48},{48,32},{64,80},{80,64},{96,112},{112,96},{1... | collective-permute-start | bytes 786440 | tf_op jit(solution)/shard_map/ppermute | solution.py:294
  75.8 8.7 %collective-permute-start.18 = (bf16[512,256]{1,0:T(8,128)(2,1)}, bf16[512,256]{1,0:T(8,128)(2,1)S(1)}, u32[]{:S(2)}, u32[]{:S(2)}) collective-permute-start(bf16[512,256]{1,0:T(8,128)(2,1)} %collective-permute-done.15.refs_1_), channel_id=1, source_target_pairs={{0,16},{16,0},{32,48},{48,32},{64,80},{80,64},{96,112},{112,96},{1... | collective-permute-start | bytes 786440 | tf_op jit(solution)/shard_map/ppermute | solution.py:294
  75.9 9.2 %collective-permute-start.17 = (bf16[512,256]{1,0:T(8,128)(2,1)}, bf16[512,256]{1,0:T(8,128)(2,1)S(1)}, u32[]{:S(2)}, u32[]{:S(2)}) collective-permute-start(bf16[512,256]{1,0:T(8,128)(2,1)} %constant_dynamic-update-slice_fusion.refs_0_), channel_id=1, source_target_pairs={{0,8},{1,9},{2,10},{3,11},{4,12},{5,13},{6,14},{7,15},{8,0},{9,1},... | collective-permute-start | bytes 786440 | tf_op jit(solution)/shard_map/ppermute | solution.py:285
  90.1 9.5 %collective-permute-start.21 = (bf16[2048,256]{1,0:T(8,128)(2,1)}, bf16[2048,256]{1,0:T(8,128)(2,1)S(1)}, u32[]{:S(2)}, u32[]{:S(2)}) collective-permute-start(bf16[2048,256]{1,0:T(8,128)(2,1)} %get-tuple-element.76), channel_id=1, source_target_pairs={{0,16},{16,0},{32,48},{48,32},{64,80},{80,64},{96,112},{112,96},{1... | collective-permute-start | bytes 3145736 | tf_op jit(solution)/shard_map/ppermute | solution.py:294
  100.9 82.6 %reduce-scatter.3.cloned.1.call-start = ((), (), s32[]{:S(2)}) async-start(), calls=%async_computation.3 | async-start | bytes 5242880 | tf_op jit(solution)/shard_map/reduce_scatter | solution.py:278
  126.1 11.6 %collective-permute-start.23 = (bf16[512,384]{1,0:T(8,128)(2,1)S(1)}, bf16[512,384]{1,0:T(8,128)(2,1)S(1)}, u32[]{:S(2)}, u32[]{:S(2)}) collective-permute-start(bf16[512,384]{1,0:T(8,128)(2,1)S(1)} %get-tuple-element.96), channel_id=1, source_target_pairs={{0,4},{1,5},{2,6},{3,7},{4,8},{5,9},{6,10},{7,11},{8,12},{9,13},{1... | collective-permute-start | bytes 1179656 | tf_op jit(solution)/shard_map/ppermute | solution.py:285
  126.3 11.4 %collective-permute-start.24 = (bf16[512,384]{1,0:T(8,128)(2,1)S(1)}, bf16[512,384]{1,0:T(8,128)(2,1)S(1)}, u32[]{:S(2)}, u32[]{:S(2)}) collective-permute-start(bf16[512,384]{1,0:T(8,128)(2,1)S(1)} %get-tuple-element.97), channel_id=1, source_target_pairs={{0,12},{1,13},{2,14},{3,15},{4,0},{5,1},{6,2},{7,3},{8,4},{9,5},{1... | collective-permute-start | bytes 1179656 | tf_op jit(solution)/shard_map/ppermute | solution.py:285
  137.7 13.6 %collective-permute-start.25 = (bf16[512,384]{1,0:T(8,128)(2,1)S(1)}, bf16[512,384]{1,0:T(8,128)(2,1)S(1)}, u32[]{:S(2)}, u32[]{:S(2)}) collective-permute-start(bf16[512,384]{1,0:T(8,128)(2,1)S(1)} %get-tuple-element.99), channel_id=1, source_target_pairs={{0,8},{1,9},{2,10},{3,11},{4,12},{5,13},{6,14},{7,15},{8,0},{9,1},... | collective-permute-start | bytes 1179656 | tf_op jit(solution)/shard_map/ppermute | solution.py:285
  151.6 8.3 %collective-permute-start.30 = (bf16[128,384]{1,0:T(8,128)(2,1)S(1)}, bf16[128,384]{1,0:T(8,128)(2,1)S(1)}, u32[]{:S(2)}, u32[]{:S(2)}) collective-permute-start(bf16[128,384]{1,0:T(8,128)(2,1)S(1)} %get-tuple-element.122), channel_id=1, source_target_pairs={{0,2},{1,3},{2,0},{3,1},{4,6},{5,7},{6,4},{7,5},{8,10},{9,11},{10,... | collective-permute-start | bytes 294920 | tf_op jit(solution)/shard_map/ppermute | solution.py:290
  153.2 9.0 %collective-permute-start.31 = (bf16[128,384]{1,0:T(8,128)(2,1)S(1)}, bf16[128,384]{1,0:T(8,128)(2,1)S(1)}, u32[]{:S(2)}, u32[]{:S(2)}) collective-permute-start(bf16[128,384]{1,0:T(8,128)(2,1)S(1)} %get-tuple-element.121), channel_id=1, source_target_pairs={{0,3},{1,0},{2,1},{3,2},{4,7},{5,4},{6,5},{7,6},{8,11},{9,8},{10,9... | collective-permute-start | bytes 294920 | tf_op jit(solution)/shard_map/ppermute | solution.py:290
  162.3 15.4 %collective-permute-start.32 = (bf16[128,640]{1,0:T(8,128)(2,1)S(1)}, bf16[128,640]{1,0:T(8,128)(2,1)S(1)}, u32[]{:S(2)}, u32[]{:S(2)}) collective-permute-start(bf16[128,640]{1,0:T(8,128)(2,1)S(1)} %pad_maximum_fusion.3), channel_id=1, source_target_pairs={{128,0},{144,16},{160,32},{176,48},{64,192},{80,208},{96,224},{112... | collective-permute-start | bytes 491528 | tf_op jit(solution)/shard_map/ppermute | solution.py:310
  177.8 9.2 %collective-permute-start.33 = (bf16[128,640]{1,0:T(8,128)(2,1)S(1)}, bf16[128,640]{1,0:T(8,128)(2,1)S(1)}, u32[]{:S(2)}, u32[]{:S(2)}) collective-permute-start(bf16[128,640]{1,0:T(8,128)(2,1)S(1)} %add_convert_fusion.6), channel_id=1, source_target_pairs={{0,96},{16,112},{32,0},{48,16},{192,160},{208,176},{224,192},{240,... | collective-permute-start | bytes 491528 | tf_op jit(solution)/shard_map/ppermute | solution.py:320
  180.1 6.8 %collective-permute-start.34 = (bf16[128,640]{1,0:T(8,128)(2,1)S(1)}, bf16[128,640]{1,0:T(8,128)(2,1)S(1)}, u32[]{:S(2)}, u32[]{:S(2)}) collective-permute-start(bf16[128,640]{1,0:T(8,128)(2,1)S(1)} %add_convert_fusion.6), channel_id=1, source_target_pairs={{0,64},{16,80},{32,96},{48,112},{192,128},{208,144},{224,160},{240... | collective-permute-start | bytes 491528 | tf_op jit(solution)/shard_map/ppermute | solution.py:320
  181.5 7.1 %collective-permute-start.35 = (bf16[128,640]{1,0:T(8,128)(2,1)S(1)}, bf16[128,640]{1,0:T(8,128)(2,1)S(1)}, u32[]{:S(2)}, u32[]{:S(2)}) collective-permute-start(bf16[128,640]{1,0:T(8,128)(2,1)S(1)} %add_convert_fusion.6), channel_id=1, source_target_pairs={{0,32},{16,48},{32,64},{48,80},{192,224},{208,240},{224,128},{240,... | collective-permute-start | bytes 491528 | tf_op jit(solution)/shard_map/ppermute | solution.py:320
  (35 other events, 179.2 us)
Sparse Core Ops, SparseCore 0:
  14.9 52.7 all-gather.1
  101.0 26.6 reduce-scatter.4
  130.4 49.3 reduce-scatter.2

commit v3 on v2

--- a/solution.py
+++ b/solution.py
@@ -1,5 +1,3 @@
-from functools import partial
-
 import jax
 import jax.numpy as jnp
 from jax import lax
@@ -36,9 +34,10 @@
     return dims(0, 0, left, right)
 
 
-def call(kernel, outs, vmem, scalars=1, macs=0, **more):
+def call(kernel, outs, vmem, scalars=1, macs=0, parts=(), **more):
     return pl.pallas_call(
         kernel,
+        grid=(1,) if parts else (),
         cost_estimate=pl.CostEstimate(
             flops=2 * macs,
             bytes_accessed=sum(shape[0] * shape[1] for shape, _ in outs) * 2,
@@ -46,7 +45,8 @@
         ),
         out_shape=[jax.ShapeDtypeStruct(shape, kind) for shape, kind in outs],
         in_specs=[pl.BlockSpec(memory_space=pltpu.SMEM)] * scalars
-        + [pl.BlockSpec()] * (vmem - scalars),
+        + [part_spec(*entry) for entry in parts]
+        + [pl.BlockSpec()] * (vmem - scalars - len(parts)),
         out_specs=[pl.BlockSpec()] * len(outs),
         compiler_params=pltpu.CompilerParams(vmem_limit_bytes=56 << 20),
         **more,
@@ -70,9 +70,12 @@
         out_ref[TRAJ:, cols] = (cot_ref[:, at].astype(f32) * weight).astype(bf16)
 
 
-def tokens_of(pair_ref, part, cols):
-    tops = [(2 * k + part) * TRAJ for k in range(NX)]
-    return jnp.concatenate([pair_ref[top : top + TRAJ, cols] for top in tops], axis=0)
+def part_spec(part, columns):
+    return pl.BlockSpec((NX, 1, TRAJ, columns), lambda i: (0, part, 0, 0))
+
+
+def tokens_of(part_ref, cols):
+    return jnp.concatenate([part_ref[k, 0, :, cols] for k in range(NX)], axis=0)
 
 
 def finish_kernel(
@@ -93,12 +96,12 @@
     grad_ref[...] = (grad_out + inv * (scaled - unit * mean)).astype(bf16)
 
 
-def project_kernel(part, pair_ref, *refs):
+def project_kernel(part_ref, *refs):
     own, other, outs = refs[:NY], refs[NY : 2 * NY], refs[2 * NY :]
     totals = [None, None]
     for j in range(NY):
         span = own[j].shape[0]
-        left = tokens_of(pair_ref, part, slice(j * span, (j + 1) * span))
+        left = tokens_of(part_ref, slice(j * span, (j + 1) * span))
         for side, chunks in enumerate((own, other)):
             term = dot(left, chunks[j][...])
             totals[side] = term if totals[side] is None else totals[side] + term
@@ -141,9 +144,9 @@
     return r * u - t * (r * r * r * jnp.mean(t * u, axis=-1, keepdims=True))
 
 
-def stack_heads(own_ref, other_ref):
+def stack_heads(own_ref, other_ref, rows=slice(None)):
     return jnp.concatenate(
-        [ref[:, k * HD : (k + 1) * HD] for ref in (own_ref, other_ref) for k in range(2)], axis=0
+        [ref[rows, k * HD : (k + 1) * HD] for ref in (own_ref, other_ref) for k in range(2)], axis=0
     )
 
 
@@ -177,31 +180,42 @@
         mixed_other_ref[:, k * HD : (k + 1) * HD] = mixed[(k + 2) * TRAJ : (k + 3) * TRAJ]
 
 
-def attend_back_kernel(
-    first_ref, own_ref, other_ref, q_gain_ref, k_gain_ref, cos_ref, sin_ref,
-    q_rot_ref, k_rot_ref, value_ref, probs_ref, gm_own_ref, gm_other_ref,
-    g_own_ref, g_other_ref,
+def back_kernel(
+    first_ref, normed_ref, grad_ref, own_ref, other_ref, q_gain_ref, k_gain_ref, cos_ref, sin_ref,
+    q_rot_ref, k_rot_ref, value_ref, probs_ref, *refs,
 ):
+    o_own, o_other, refs = refs[:NY], refs[NY : 2 * NY], refs[2 * NY :]
+    g_own_ref, g_other_ref, outs, other_out = refs[0], refs[1], refs[2 : 2 + NY], refs[2 + NY]
+    gm_own_ref, gm_other_ref = refs[3 + NY :]
+    project_kernel(grad_ref, *o_own, *o_other, gm_own_ref, gm_other_ref)
     cos, sin = cos_ref[...], sin_ref[...]
     cos4, sin4 = jnp.concatenate([cos] * 4, axis=0), jnp.concatenate([sin] * 4, axis=0)
     first = first_ref[0] == 1
-    keys = jnp.where(first, own_ref[:, 2 * HD :], other_ref[:, 2 * HD :])
-    query = stack_heads(own_ref, other_ref)
-    grad_mixed = stack_heads(gm_own_ref, gm_other_ref)
-    q_rot, k_rot, value, probs = q_rot_ref[...], k_rot_ref[...], value_ref[...], probs_ref[...]
-    grad_probs = dot_rows(grad_mixed, value)
-    grad_value = dot_cols(probs.astype(bf16), grad_mixed).astype(bf16)
-    inner = jnp.sum(grad_probs * probs, axis=-1, keepdims=True)
-    grad_scores = (probs * (grad_probs - inner) * HD ** (-0.5)).astype(bf16)
-    grad_q_rot = dot(grad_scores, k_rot)
-    grad_k_rot = dot_cols(grad_scores, q_rot)
-    grad_query = norm_back(query, rotate_back(grad_q_rot, cos4, sin4), q_gain_ref[...]).astype(bf16)
-    grad_keys = norm_back(keys, rotate_back(grad_k_rot, cos, sin), k_gain_ref[...]).astype(bf16)
-    for k in range(2):
-        g_own_ref[:, k * HD : (k + 1) * HD] = grad_query[k * TRAJ : (k + 1) * TRAJ]
-        g_other_ref[:, k * HD : (k + 1) * HD] = grad_query[(k + 2) * TRAJ : (k + 3) * TRAJ]
-    g_own_ref[:, 2 * HD :] = jnp.where(first, grad_keys, grad_value)
-    g_other_ref[:, 2 * HD :] = jnp.where(first, grad_value, grad_keys)
+    for i in range(NX):
+        at = slice(i * TRAJ, (i + 1) * TRAJ)
+        at4 = slice(i * 4 * TRAJ, (i + 1) * 4 * TRAJ)
+        keys = jnp.where(first, own_ref[at, 2 * HD :], other_ref[at, 2 * HD :])
+        query = stack_heads(own_ref, other_ref, at)
+        grad_mixed = stack_heads(gm_own_ref, gm_other_ref, at)
+        q_rot, k_rot, value, probs = q_rot_ref[at4], k_rot_ref[at], value_ref[at], probs_ref[at4]
+        grad_probs = dot_rows(grad_mixed, value)
+        grad_value = dot_cols(probs.astype(bf16), grad_mixed).astype(bf16)
+        inner = jnp.sum(grad_probs * probs, axis=-1, keepdims=True)
+        grad_scores = (probs * (grad_probs - inner) * HD ** (-0.5)).astype(bf16)
+        grad_q_rot = rotate_back(dot(grad_scores, k_rot), cos4, sin4)
+        grad_k_rot = rotate_back(dot_cols(grad_scores, q_rot), cos, sin)
+        grad_query = norm_back(query, grad_q_rot, q_gain_ref[...]).astype(bf16)
+        grad_keys = norm_back(keys, grad_k_rot, k_gain_ref[...]).astype(bf16)
+        for k in range(2):
+            g_own_ref[at, k * HD : (k + 1) * HD] = grad_query[k * TRAJ : (k + 1) * TRAJ]
+            g_other_ref[at, k * HD : (k + 1) * HD] = grad_query[(k + 2) * TRAJ : (k + 3) * TRAJ]
+        g_own_ref[at, 2 * HD :] = jnp.where(first, grad_keys, grad_value)
+        g_other_ref[at, 2 * HD :] = jnp.where(first, grad_value, grad_keys)
+    for j in range(NY):
+        span = outs[j].shape[0]
+        left = tokens_of(normed_ref, slice(j * span, (j + 1) * span))
+        other_out[j * span : (j + 1) * span] = dot_cols(left, g_other_ref[...]).astype(bf16)
+        outs[j][...] = dot_cols(left, g_own_ref[...]).astype(bf16)
 
 
 def by_trajectory(kernel, outs, ins):
@@ -223,19 +237,10 @@
     )
 
 
-def weight_grad_kernel(pair_ref, own_ref, other_ref, *refs):
-    outs, other_out = refs[:NY], refs[NY]
-    for j in range(NY):
-        span = outs[j].shape[0]
-        left = tokens_of(pair_ref, 0, slice(j * span, (j + 1) * span))
-        other_out[j * span : (j + 1) * span] = dot_cols(left, other_ref[...]).astype(bf16)
-        outs[j][...] = dot_cols(left, own_ref[...]).astype(bf16)
-
-
-def grad_o_kernel(place_ref, pair_ref, own_ref, other_ref, own_out, other_out):
+def grad_o_kernel(place_ref, part_ref, own_ref, other_ref, own_out, other_out):
     span = NZ * HD
     for j in range(NY):
-        left = tokens_of(pair_ref, 1, slice(j * span, (j + 1) * span))
+        left = tokens_of(part_ref, slice(j * span, (j + 1) * span))
         at = pl.ds(pl.multiple_of(lax.rem(place_ref[0] + j, NY) * span, span), span)
         other_out[at] = dot_cols(left, other_ref[...]).astype(bf16)
         own_out[at] = dot_cols(left, own_ref[...]).astype(bf16)
@@ -414,9 +419,15 @@
     o_near = [take_y(o_late, 1), take_y(o_late, 3)]
 
     tokens = pair.shape[0] // 2
+    pair = pair.reshape(NX, 2, TRAJ, flat[1])
     cos_tab, sin_tab = rope_tables()
     proj_own, proj_other = call(
-        partial(project_kernel, 0), [((tokens, wide), f32)] * 2, 1 + 2 * NY, scalars=0, macs=tokens * flat[1] * 2 * wide
+        project_kernel,
+        [((tokens, wide), f32)] * 2,
+        1 + 2 * NY,
+        scalars=0,
+        macs=tokens * flat[1] * 2 * wide,
+        parts=[(0, flat[1])],
     )(pair, *qkv_own, *qkv_other)
     o_own = [o_plane, o_near[0], take_y(after(o_plane, proj_own), 2), o_near[1]]
     o_other = [o_first] + [other_core(after(piece, proj_own)) for piece in o_own[1:]]
@@ -432,24 +443,36 @@
 
     span = NZ * HD
     go_own, go_cross = call(
-        grad_o_kernel, [((NY * span, half), bf16)] * 2, 4, macs=tokens * flat[1] * width
+        grad_o_kernel,
+        [((NY * span, half), bf16)] * 2,
+        4,
+        macs=tokens * flat[1] * width,
+        parts=[(1, flat[1])],
     )(place, after(pair, o_own[2], o_other[1], o_other[3]), mixed_own, mixed_other)
-    gm_own, gm_other = call(
-        partial(project_kernel, 1), [((tokens, half), bf16)] * 2, 1 + 2 * NY, scalars=0, macs=tokens * flat[1] * width
-    )(after(pair, go_cross), *o_own, *o_other)
-    go_theirs = after(other_core(go_cross), gm_own)
+    go_theirs = after(other_core(go_cross), o_other[2])
     go_terms = scatter_y((go_own.astype(f32) + go_theirs.astype(f32)).astype(bf16))
-    g_own, g_other = by_trajectory(
-        attend_back_kernel,
-        [(TRAJ, wide, bf16)] * 2,
-        [(TRAJ, wide)] * 2 + shared + [entry[:2] for entry in kept] + [(TRAJ, half)] * 2,
-    )(flag, proj_own, proj_other, *tables, q_rot, k_rot, value, probs, *after([gm_own, gm_other], go_theirs))
-    *gw_own, gw_cross = call(
-        weight_grad_kernel,
-        [((span, wide), bf16)] * NY + [((NY * span, wide), bf16)],
-        3,
-        scalars=0,
-    )(pair, g_own, g_other)
+    g_own, g_other, *gw_own, gw_cross = call(
+        back_kernel,
+        [((tokens, wide), bf16)] * 2
+        + [((span, wide), bf16)] * NY
+        + [((NY * span, wide), bf16)],
+        13 + 2 * NY,
+        macs=tokens * flat[1] * (width + 2 * wide),
+        parts=[(0, flat[1]), (1, flat[1])],
+        scratch_shapes=[pltpu.VMEM((tokens, half), bf16)] * 2,
+    )(
+        flag,
+        *after([pair, pair], go_theirs),
+        proj_own,
+        proj_other,
+        *tables,
+        q_rot,
+        k_rot,
+        value,
+        probs,
+        *o_own,
+        *o_other,
+    )
     gw_theirs = other_core(gw_cross)
     terms = call(
         expand_kernel,

time: 203 us -> 192 us (0.946)
  waiting for transfers between devices: 68.2 us -> 59.4 us
  Pallas kernels: 48.9 us -> 41.6 us
  starting transfers between devices: 52.7 us -> 58.7 us
  local copies, waits for them, and re-layouts: 8.73 us -> 6.32 us
    ppermute x9, waiting for transfers between devices: 18.4 us -> 10.3 us  [take_y(): return lax.ppermute(value, 'fsdp', pairs)]
    pallas_call x4 -> x2, Pallas kernels: 23.4 us -> 16.6 us  [the longest x1 10.9 us: on_device(): call(back_kernel, [((tokens, wide), bf16)] * 2 + [((span, wide), bf16)] *...]
    ppermute x1, waiting for transfers between devices: 14.1 us -> 8.67 us  [to_owner(): return lax.ppermute(value, ('role', 'dp'), pairs)]
    reduce_scatter x1, waiting for transfers between devices: 0.02 us -> 2.86 us  [scatter_x(): lax.psum_scatter(value, 'dp', scatter_dimension=0, tiled=True, axis_index...]
    unnamed x43 -> x41, local copies, waits for them, and re-layouts: 5.5 us -> 3.08 us
    ppermute x11, starting transfers between devices: 11.9 us -> 14.1 us  [other_core(): return lax.ppermute(value, 'dp', [(i, i ^ 1) for i in range(NX * NC)])]
    ppermute x9, starting transfers between devices: 12.7 us -> 14.8 us  [take_y(): return lax.ppermute(value, 'fsdp', pairs)]
  transfers between devices with their start and end apart: 40 -> 40, of which waited for: 20 -> 20; matrix products, arithmetic and copies ran while one was open for 3% -> 3% of each run, Pallas kernels for 20% -> 18%
where the time goes in v3:
time: 192 us; the launch traced here: 190 us
  waiting for transfers between devices  59.4 us (31%)
  starting transfers between devices  58.7 us (31%)
  Pallas kernels  41.6 us (22%)
  between operations  14.4 us (8%)
  other arithmetic  9.77 us (5%)
  local copies, waits for them, and re-layouts  6.32 us (3%)
    ppermute x12, waiting for transfers between devices, take_z(): return lax.ppermute(value, 'fsdp', pairs)  20 us
    ppermute x9, starting transfers between devices, take_y(): return lax.ppermute(value, 'fsdp', pairs)  14.8 us
    ppermute x11, starting transfers between devices, other_core(): return lax.ppermute(value, 'dp', [(i, i ^ 1) for i in range(NX * NC)])  14.1 us
    ppermute x12, starting transfers between devices, take_z(): return lax.ppermute(value, 'fsdp', pairs)  13.9 us
    pallas_call x1, Pallas kernels, on_device(): call(back_kernel, [((tokens, wide), bf16)] * 2 + [((span, wide), bf16)] *...  10.9 us
    ppermute x9, waiting for transfers between devices, take_y(): return lax.ppermute(value, 'fsdp', pairs)  10.3 us
    ppermute x1, waiting for transfers between devices, to_owner(): return lax.ppermute(value, ('role', 'dp'), pairs)  8.67 us
    ppermute x11, waiting for transfers between devices, other_core(): return lax.ppermute(value, 'dp', [(i, i ^ 1) for i in range(NX * NC)])  8.66 us
  transfers between devices with their start and end apart: 40, of which 20 were waited for; matrix products, arithmetic and copies ran while one was open for 3% of the time, Pallas kernels for 18%

profile of v3, /device:TPU:35, one launch (start us, length us, event | category | flops | bytes accessed | tf_op | source)
XLA Modules:
  0.0 190.1 jit_solution(6072258426795598754)
XLA Ops:
  11.1 2.7 %shard_map.154 = bf16[256,2048]{1,0:T(8,128)(2,1)} custom-call(s32[2]{0:T(128)} %pad_add_fusion.place_ref, bf16[128,2048]{1,0:T(8,128)(2,1)} %bitcast.26, f32[1,2048]{1,0:T(1,128)} %bitcast.32, bf16[128,2048]{1,0:T(8,128)(2,1)} %bitcast.28, f32[128,1]{1,0:T(8,128)} %copy.19.weight_ref), custom_call_target="tpu_custom_call" | custom-call | bytes 1048576 | tf_op jit(solution)/shard_map/pallas_call | solution.py:408
  13.9 7.9 %collective-permute-start = (bf16[128,640]{1,0:T(8,128)(2,1)S(1)}, bf16[128,640]{1,0:T(8,128)(2,1)S(1)}, u32[]{:S(2)}, u32[]{:S(2)}) collective-permute-start(bf16[128,640]{1,0:T(8,128)(2,1)S(1)} %pad_maximum_fusion.2), channel_id=1, source_target_pairs={{0,128},{16,144},{32,160},{48,176},{192,64},{208,80},{224,96},{240... | collective-permute-start | bytes 491528 | tf_op jit(solution)/shard_map/ppermute | solution.py:309
  21.8 7.4 %collective-permute-done = bf16[128,640]{1,0:T(8,128)(2,1)S(1)} collective-permute-done((bf16[128,640]{1,0:T(8,128)(2,1)S(1)}, bf16[128,640]{1,0:T(8,128)(2,1)S(1)}, u32[]{:S(2)}, u32[]{:S(2)}) %collective-permute-start) | collective-permute-done | bytes 163872 | tf_op jit(solution)/shard_map/ppermute | solution.py:309
  33.9 2.4 %collective-permute-done.1 = bf16[128,384]{1,0:T(8,128)(2,1)S(1)} collective-permute-done((bf16[128,384]{1,0:T(8,128)(2,1)S(1)}, bf16[128,384]{1,0:T(8,128)(2,1)S(1)}, u32[]{:S(2)}, u32[]{:S(2)}) %collective-permute-start.1) | collective-permute-done | bytes 98336 | tf_op jit(solution)/shard_map/ppermute | solution.py:295
  36.4 3.5 %collective-permute-start.7 = (bf16[512,384]{1,0:T(8,128)(2,1)S(1)}, bf16[512,384]{1,0:T(8,128)(2,1)S(1)}, u32[]{:S(2)}, u32[]{:S(2)}) collective-permute-start(bf16[512,384]{1,0:T(8,128)(2,1)S(1)} %pad_maximum_fusion.refs_0_.refs_8_), channel_id=1, source_target_pairs={{0,16},{16,0},{32,48},{48,32},{64,80},{80,64},{96,112},{112,96},{1... | collective-permute-start | bytes 1179656 | tf_op jit(solution)/shard_map/ppermute | solution.py:299
  47.0 2.9 %collective-permute-done.8 = bf16[128,256]{1,0:T(8,128)(2,1)S(1)} collective-permute-done((bf16[128,256]{1,0:T(8,128)(2,1)S(1)}, bf16[128,256]{1,0:T(8,128)(2,1)S(1)}, u32[]{:S(2)}, u32[]{:S(2)}) %collective-permute-start.8) | collective-permute-done | bytes 65568 | tf_op jit(solution)/shard_map/ppermute | solution.py:295
  55.5 2.8 %collective-permute-start.11 = (bf16[512,256]{1,0:T(8,128)(2,1)}, bf16[512,256]{1,0:T(8,128)(2,1)S(1)}, u32[]{:S(2)}, u32[]{:S(2)}) collective-permute-start(bf16[512,256]{1,0:T(8,128)(2,1)} %constant_dynamic-update-slice_fusion.refs_0_), channel_id=1, source_target_pairs={{0,16},{16,0},{32,48},{48,32},{64,80},{80,64},{96,112},{112,96},{1... | collective-permute-start | bytes 786440 | tf_op jit(solution)/shard_map/ppermute | solution.py:299
  66.8 5.7 %shard_map.155 = (f32[512,384]{1,0:T(8,128)}, f32[512,384]{1,0:T(8,128)}) custom-call(bf16[4,2,128,2048]{3,2,1,0:T(8,128)(2,1)} %bitcast.22, bf16[512,384]{1,0:T(8,128)(2,1)} %copy-done.1, bf16[512,384]{1,0:T(8,128)(2,1)} %copy-done.5, bf16[512,384]{1,0:T(8,128)(2,1)} %copy-done.4, bf16[512,384]{1,0:T(8,128)(2,1)} %copy-done.3, bf16[512,384]{1,0:T(8,128)(2,1)} %copy-done.2, ...), custom_call_target="tpu_custom_call" | custom-call | flops 1610612736 | bytes 786432 | tf_op jit(solution)/shard_map/pallas_call | solution.py:424
  72.5 2.8 %collective-permute-start.17 = (bf16[512,256]{1,0:T(8,128)(2,1)}, bf16[512,256]{1,0:T(8,128)(2,1)S(1)}, u32[]{:S(2)}, u32[]{:S(2)}) collective-permute-start(bf16[512,256]{1,0:T(8,128)(2,1)} %constant_dynamic-update-slice_fusion.refs_0_), channel_id=1, source_target_pairs={{0,8},{1,9},{2,10},{3,11},{4,12},{5,13},{6,14},{7,15},{8,0},{9,1},... | collective-permute-start | bytes 786440 | tf_op jit(solution)/shard_map/ppermute | solution.py:290
  77.3 5.8 %shard_map.156 = (bf16[2048,128]{1,0:T(8,128)(2,1)}, bf16[512,128]{1,0:T(8,128)(2,1)}, bf16[512,128]{1,0:T(8,128)(2,1)}, f32[2048,128]{1,0:T(8,128)}, bf16[512,2...) custom-call(s32[1]{0:T(128)} %bitcast.6.first_ref, f32[512,384]{1,0:T(8,128)} %get-tuple-element.61.own_ref, ...), custom_call_target="tpu_custom_call" | custom-call | flops 536870912 | bytes 1048576 | tf_op jit(solution)/shard_map/pallas_call | solution.py:438
  83.2 4.5 %shard_map.157 = (bf16[2048,256]{1,0:T(8,128)(2,1)}, bf16[2048,256]{1,0:T(8,128)(2,1)}) custom-call(s32[2]{0:T(128)} %pad_add_fusion.place_ref, bf16[4,2,128,2048]{3,2,1,0:T(8,128)(2,1)} %bitcast.23, bf16[512,256]{1,0:T(8,128)(2,1)} %get-tuple-element.63.own_ref.mixed_own_ref, bf16[512,256]{1,0:T(8,128)(2,1)} %get-tuple-element.64.other_ref.mixed_other_ref), custom_call_target="tpu_custom_call" | custom-call | flops 1073741824 | bytes 2097152 | tf_op jit(solution)/shard_map/pallas_call | solution.py:445
  88.4 2.5 %collective-permute-done.21.refs_6_ = bf16[512,256]{1,0:T(8,128)(2,1)S(1)} collective-permute-done((bf16[512,256]{1,0:T(8,128)(2,1)S(1)}, bf16[512,256]{1,0:T(8,128)(2,1)S(1)}, u32[]{:S(2)}, u32[]{:S(2)}) %collective-permute-start.21) | collective-permute-done | bytes 262176 | tf_op jit(solution)/shard_map/ppermute | solution.py:299
  91.1 2.5 %add_convert_fusion = bf16[2048,256]{1,0:T(8,128)(2,1)} fusion(bf16[2048,256]{1,0:T(8,128)(2,1)S(1)} %collective-permute-done.20, bf16[2048,256]{1,0:T(8,128)(2,1)} %get-tuple-element.94), kind=kLoop, calls=%fused_computation | loop fusion | flops 2097152 | bytes 3145728 | tf_op jit(solution)/shard_map/convert_element_type | solution.py:453
  93.8 10.9 %shard_map.158 = (bf16[512,384]{1,0:T(8,128)(2,1)}, bf16[512,384]{1,0:T(8,128)(2,1)}, bf16[512,384]{1,0:T(8,128)(2,1)}, bf16[512,384]{1,0:T(8,128)(2,1)}, bf16[5...) custom-call(s32[1]{0:T(128)} %bitcast.6.first_ref, bf16[4,2,128,2048]{3,2,1,0:T(8,128)(2,1)} %bitcast.24, ...), custom_call_target="tpu_custom_call" | custom-call | flops 2684354560 | bytes 3932160 | tf_op jit(solution)/shard_map/pallas_call | solution.py:454
  104.7 8.5 %shard_map.159 = bf16[1024,2048]{1,0:T(8,128)(2,1)} custom-call(bf16[512,256]{1,0:T(8,128)(2,1)} %get-tuple-element.63.own_ref.mixed_own_ref, bf16[512,256]{1,0:T(8,128)(2,1)} %get-tuple-element.64.other_ref.mixed_other_ref, bf16[512,384]{1,0:T(8,128)(2,1)} %get-tuple-element.81.g_own_ref, bf16[512,384]{1,0:T(8,128)(2,1)} %get-tuple-element.82.g_other_ref, ...), custom_call_target="tpu_custom_call" | custom-call | flops 2684354560 | bytes 4194304 | tf_op jit(solution)/shard_map/pallas_call | solution.py:477
  113.7 3.3 %collective-permute-done.22 = bf16[2048,384]{1,0:T(8,128)(2,1)S(1)} collective-permute-done((bf16[2048,384]{1,0:T(8,128)(2,1)}, bf16[2048,384]{1,0:T(8,128)(2,1)S(1)}, u32[]{:S(2)}, u32[]{:S(2)}) %collective-permute-start.22) | collective-permute-done | bytes 1572896 | tf_op jit(solution)/shard_map/ppermute | solution.py:299
  120.1 8.9 %collective-permute-done.23 = bf16[512,384]{1,0:T(8,128)(2,1)S(1)} collective-permute-done((bf16[512,384]{1,0:T(8,128)(2,1)S(1)}, bf16[512,384]{1,0:T(8,128)(2,1)S(1)}, u32[]{:S(2)}, u32[]{:S(2)}) %collective-permute-start.23) | collective-permute-done | bytes 393248 | tf_op jit(solution)/shard_map/ppermute | solution.py:290
  136.4 3.0 %collective-permute-done.27 = bf16[128,256]{1,0:T(8,128)(2,1)S(1)} collective-permute-done((bf16[128,256]{1,0:T(8,128)(2,1)S(1)}, bf16[128,256]{1,0:T(8,128)(2,1)S(1)}, u32[]{:S(2)}, u32[]{:S(2)}) %collective-permute-start.27) | collective-permute-done | bytes 65568 | tf_op jit(solution)/shard_map/ppermute | solution.py:295
  147.6 3.7 %collective-permute-done.30 = bf16[128,384]{1,0:T(8,128)(2,1)S(1)} collective-permute-done((bf16[128,384]{1,0:T(8,128)(2,1)S(1)}, bf16[128,384]{1,0:T(8,128)(2,1)S(1)}, u32[]{:S(2)}, u32[]{:S(2)}) %collective-permute-start.30) | collective-permute-done | bytes 98336 | tf_op jit(solution)/shard_map/ppermute | solution.py:295
  152.7 8.7 %collective-permute-done.32 = bf16[128,640]{1,0:T(8,128)(2,1)S(1)} collective-permute-done((bf16[128,640]{1,0:T(8,128)(2,1)S(1)}, bf16[128,640]{1,0:T(8,128)(2,1)S(1)}, u32[]{:S(2)}, u32[]{:S(2)}) %collective-permute-start.32) | collective-permute-done | bytes 163872 | tf_op jit(solution)/shard_map/ppermute | solution.py:315
  164.6 3.4 %collective-permute-start.33 = (bf16[128,640]{1,0:T(8,128)(2,1)S(1)}, bf16[128,640]{1,0:T(8,128)(2,1)S(1)}, u32[]{:S(2)}, u32[]{:S(2)}) collective-permute-start(bf16[128,640]{1,0:T(8,128)(2,1)S(1)} %add_convert_fusion.6), channel_id=1, source_target_pairs={{0,96},{16,112},{32,0},{48,16},{192,160},{208,176},{224,192},{240,... | collective-permute-start | bytes 491528 | tf_op jit(solution)/shard_map/ppermute | solution.py:325
  168.0 2.9 %reduce-scatter.3.cloned.1.call-done.total_ref = bf16[256,2048]{1,0:T(8,128)(2,1)} async-done(((bf16[1024,2048]{1,0:T(8,128)(2,1)}), bf16[256,2048]{1,0:T(8,128)(2,1)}) %reduce-scatter.3.cloned.1.call-update) | async-done | bytes 1048592 | tf_op jit(solution)/shard_map/reduce_scatter | solution.py:283
  170.9 3.5 %shard_map.160 = (bf16[128,2048]{1,0:T(8,128)(2,1)}, bf16[128,2048]{1,0:T(8,128)(2,1)}) custom-call(s32[2]{0:T(128)} %pad_add_fusion.place_ref, bf16[128,2048]{1,0:T(8,128)(2,1)} %bitcast.27, f32[1,2048]{1,0:T(1,128)} %bitcast.33, bf16[128,2048]{1,0:T(8,128)(2,1)} %bitcast.29, f32[128,1]{1,0:T(8,128)} %copy.19.weight_ref, ...), custom_call_target="tpu_custom_call" | custom-call | bytes 1048576 | tf_op jit(solution)/shard_map/pallas_call | solution.py:493
  174.5 4.4 %collective-permute-start.36 = (bf16[256,640]{1,0:T(8,128)(2,1)S(1)}, bf16[256,640]{1,0:T(8,128)(2,1)S(1)}, u32[]{:S(2)}, u32[]{:S(2)}) collective-permute-start(bf16[256,640]{1,0:T(8,128)(2,1)S(1)} %pad_maximum_fusion.1), channel_id=1, source_target_pairs={{0,16},{16,0},{32,48},{48,32},{64,80},{80,64},{96,112},{112,96},{1... | collective-permute-start | bytes 983048 | tf_op jit(solution)/shard_map/ppermute | solution.py:299
  (143 shorter events, 61.2 us)
Async XLA Ops:
  7.2 59.6 %all-gather.2.cloned.1.call-start = ((), (), s32[]{:S(2)}) async-start(), calls=%async_computation.2 | async-start | bytes 5242880 | tf_op jit(solution)/shard_map/all_gather | solution.py:270
  13.8 116.6 %reduce-scatter.5.cloned.1.call-start = ((), (), s32[]{:S(2)}) async-start(), calls=%async_computation.4 | async-start | bytes 1310720 | tf_op jit(solution)/shard_map/reduce_scatter | solution.py:277
  13.9 15.3 %collective-permute-start = (bf16[128,640]{1,0:T(8,128)(2,1)S(1)}, bf16[128,640]{1,0:T(8,128)(2,1)S(1)}, u32[]{:S(2)}, u32[]{:S(2)}) collective-permute-start(bf16[128,640]{1,0:T(8,128)(2,1)S(1)} %pad_maximum_fusion.2), channel_id=1, source_target_pairs={{0,128},{16,144},{32,160},{48,176},{192,64},{208,80},{224,96},{240... | collective-permute-start | bytes 491528 | tf_op jit(solution)/shard_map/ppermute | solution.py:309
  29.5 6.9 %collective-permute-start.1 = (bf16[128,384]{1,0:T(8,128)(2,1)S(1)}, bf16[128,384]{1,0:T(8,128)(2,1)S(1)}, u32[]{:S(2)}, u32[]{:S(2)}) collective-permute-start(bf16[128,384]{1,0:T(8,128)(2,1)S(1)} %slice.108), channel_id=1, source_target_pairs={{0,3},{1,0},{2,1},{3,2},{4,7},{5,4},{6,5},{7,6},{8,11},{9,8},{10,9... | collective-permute-start | bytes 294920 | tf_op jit(solution)/shard_map/ppermute | solution.py:295
  36.4 8.5 %collective-permute-start.7 = (bf16[512,384]{1,0:T(8,128)(2,1)S(1)}, bf16[512,384]{1,0:T(8,128)(2,1)S(1)}, u32[]{:S(2)}, u32[]{:S(2)}) collective-permute-start(bf16[512,384]{1,0:T(8,128)(2,1)S(1)} %pad_maximum_fusion.refs_0_.refs_8_), channel_id=1, source_target_pairs={{0,16},{16,0},{32,48},{48,32},{64,80},{80,64},{96,112},{112,96},{1... | collective-permute-start | bytes 1179656 | tf_op jit(solution)/shard_map/ppermute | solution.py:299
  39.9 18.4 %collective-permute-start.6 = (bf16[512,384]{1,0:T(8,128)(2,1)S(1)}, bf16[512,384]{1,0:T(8,128)(2,1)S(1)}, u32[]{:S(2)}, u32[]{:S(2)}) collective-permute-start(bf16[512,384]{1,0:T(8,128)(2,1)S(1)} %pad_maximum_fusion.refs_0_.refs_8_), channel_id=1, source_target_pairs={{0,4},{1,5},{2,6},{3,7},{4,8},{5,9},{6,10},{7,11},{8,12},{9,13},{1... | collective-permute-start | bytes 1179656 | tf_op jit(solution)/shard_map/ppermute | solution.py:290
  42.1 19.4 %collective-permute-start.5 = (bf16[512,384]{1,0:T(8,128)(2,1)S(1)}, bf16[512,384]{1,0:T(8,128)(2,1)S(1)}, u32[]{:S(2)}, u32[]{:S(2)}) collective-permute-start(bf16[512,384]{1,0:T(8,128)(2,1)S(1)} %pad_maximum_fusion.refs_0_.refs_8_), channel_id=1, source_target_pairs={{0,8},{1,9},{2,10},{3,11},{4,12},{5,13},{6,14},{7,15},{8,0},{9,1},... | collective-permute-start | bytes 1179656 | tf_op jit(solution)/shard_map/ppermute | solution.py:290
  43.8 18.5 %collective-permute-start.4 = (bf16[512,384]{1,0:T(8,128)(2,1)S(1)}, bf16[512,384]{1,0:T(8,128)(2,1)S(1)}, u32[]{:S(2)}, u32[]{:S(2)}) collective-permute-start(bf16[512,384]{1,0:T(8,128)(2,1)S(1)} %pad_maximum_fusion.refs_0_.refs_8_), channel_id=1, source_target_pairs={{0,12},{1,13},{2,14},{3,15},{4,0},{5,1},{6,2},{7,3},{8,4},{9,5},{1... | collective-permute-start | bytes 1179656 | tf_op jit(solution)/shard_map/ppermute | solution.py:290
  44.9 9.9 %collective-permute-start.10 = (bf16[128,256]{1,0:T(8,128)(2,1)S(1)}, bf16[128,256]{1,0:T(8,128)(2,1)S(1)}, u32[]{:S(2)}, u32[]{:S(2)}) collective-permute-start(bf16[128,256]{1,0:T(8,128)(2,1)S(1)} %slice.109), channel_id=1, source_target_pairs={{0,1},{1,2},{2,3},{3,0},{4,5},{5,6},{6,7},{7,4},{8,9},{9,10},{10,1... | collective-permute-start | bytes 196616 | tf_op jit(solution)/shard_map/ppermute | solution.py:295
  62.5 10.0 %collective-permute-start.16 = (bf16[512,256]{1,0:T(8,128)(2,1)}, bf16[512,256]{1,0:T(8,128)(2,1)}, u32[]{:S(2)}, u32[]{:S(2)}) collective-permute-start(bf16[512,256]{1,0:T(8,128)(2,1)} %constant_dynamic-update-slice_fusion.refs_0_), channel_id=1, source_target_pairs={{0,4},{1,5},{2,6},{3,7},{4,8},{5,9},{6,10},{7,11},{8,12},{9,13},{1... | collective-permute-start | bytes 786440 | tf_op jit(solution)/shard_map/ppermute | solution.py:290
  63.3 9.2 %collective-permute-start.15 = (bf16[512,256]{1,0:T(8,128)(2,1)}, bf16[512,256]{1,0:T(8,128)(2,1)}, u32[]{:S(2)}, u32[]{:S(2)}) collective-permute-start(bf16[512,256]{1,0:T(8,128)(2,1)} %constant_dynamic-update-slice_fusion.refs_0_), channel_id=1, source_target_pairs={{0,12},{1,13},{2,14},{3,15},{4,0},{5,1},{6,2},{7,3},{8,4},{9,5},{1... | collective-permute-start | bytes 786440 | tf_op jit(solution)/shard_map/ppermute | solution.py:290
  72.5 10.7 %collective-permute-start.17 = (bf16[512,256]{1,0:T(8,128)(2,1)}, bf16[512,256]{1,0:T(8,128)(2,1)S(1)}, u32[]{:S(2)}, u32[]{:S(2)}) collective-permute-start(bf16[512,256]{1,0:T(8,128)(2,1)} %constant_dynamic-update-slice_fusion.refs_0_), channel_id=1, source_target_pairs={{0,8},{1,9},{2,10},{3,11},{4,12},{5,13},{6,14},{7,15},{8,0},{9,1},... | collective-permute-start | bytes 786440 | tf_op jit(solution)/shard_map/ppermute | solution.py:290
  75.3 7.9 %collective-permute-start.18 = (bf16[512,256]{1,0:T(8,128)(2,1)}, bf16[512,256]{1,0:T(8,128)(2,1)S(1)}, u32[]{:S(2)}, u32[]{:S(2)}) collective-permute-start(bf16[512,256]{1,0:T(8,128)(2,1)} %collective-permute-done.15.refs_1_), channel_id=1, source_target_pairs={{0,16},{16,0},{32,48},{48,32},{64,80},{80,64},{96,112},{112,96},{1... | collective-permute-start | bytes 786440 | tf_op jit(solution)/shard_map/ppermute | solution.py:299
  76.3 6.9 %collective-permute-start.19 = (bf16[512,256]{1,0:T(8,128)(2,1)}, bf16[512,256]{1,0:T(8,128)(2,1)S(1)}, u32[]{:S(2)}, u32[]{:S(2)}) collective-permute-start(bf16[512,256]{1,0:T(8,128)(2,1)} %collective-permute-done.16.refs_3_), channel_id=1, source_target_pairs={{0,16},{16,0},{32,48},{48,32},{64,80},{80,64},{96,112},{112,96},{1... | collective-permute-start | bytes 786440 | tf_op jit(solution)/shard_map/ppermute | solution.py:299
  93.7 77.2 %reduce-scatter.3.cloned.1.call-start = ((), (), s32[]{:S(2)}) async-start(), calls=%async_computation.3 | async-start | bytes 5242880 | tf_op jit(solution)/shard_map/reduce_scatter | solution.py:283
  117.3 11.6 %collective-permute-start.23 = (bf16[512,384]{1,0:T(8,128)(2,1)S(1)}, bf16[512,384]{1,0:T(8,128)(2,1)S(1)}, u32[]{:S(2)}, u32[]{:S(2)}) collective-permute-start(bf16[512,384]{1,0:T(8,128)(2,1)S(1)} %get-tuple-element.90), channel_id=1, source_target_pairs={{0,4},{1,5},{2,6},{3,7},{4,8},{5,9},{6,10},{7,11},{8,12},{9,13},{1... | collective-permute-start | bytes 1179656 | tf_op jit(solution)/shard_map/ppermute | solution.py:290
  118.0 11.0 %collective-permute-start.24 = (bf16[512,384]{1,0:T(8,128)(2,1)S(1)}, bf16[512,384]{1,0:T(8,128)(2,1)S(1)}, u32[]{:S(2)}, u32[]{:S(2)}) collective-permute-start(bf16[512,384]{1,0:T(8,128)(2,1)S(1)} %get-tuple-element.91), channel_id=1, source_target_pairs={{0,12},{1,13},{2,14},{3,15},{4,0},{5,1},{6,2},{7,3},{8,4},{9,5},{1... | collective-permute-start | bytes 1179656 | tf_op jit(solution)/shard_map/ppermute | solution.py:290
  129.0 11.4 %collective-permute-start.25 = (bf16[512,384]{1,0:T(8,128)(2,1)S(1)}, bf16[512,384]{1,0:T(8,128)(2,1)S(1)}, u32[]{:S(2)}, u32[]{:S(2)}) collective-permute-start(bf16[512,384]{1,0:T(8,128)(2,1)S(1)} %get-tuple-element.93), channel_id=1, source_target_pairs={{0,8},{1,9},{2,10},{3,11},{4,12},{5,13},{6,14},{7,15},{8,0},{9,1},... | collective-permute-start | bytes 1179656 | tf_op jit(solution)/shard_map/ppermute | solution.py:290
  132.9 6.6 %collective-permute-start.27 = (bf16[128,256]{1,0:T(8,128)(2,1)S(1)}, bf16[128,256]{1,0:T(8,128)(2,1)S(1)}, u32[]{:S(2)}, u32[]{:S(2)}) collective-permute-start(bf16[128,256]{1,0:T(8,128)(2,1)S(1)} %get-tuple-element.131), channel_id=1, source_target_pairs={{0,2},{1,3},{2,0},{3,1},{4,6},{5,7},{6,4},{7,5},{8,10},{9,11},{10,... | collective-permute-start | bytes 196616 | tf_op jit(solution)/shard_map/ppermute | solution.py:295
  143.0 8.2 %collective-permute-start.30 = (bf16[128,384]{1,0:T(8,128)(2,1)S(1)}, bf16[128,384]{1,0:T(8,128)(2,1)S(1)}, u32[]{:S(2)}, u32[]{:S(2)}) collective-permute-start(bf16[128,384]{1,0:T(8,128)(2,1)S(1)} %get-tuple-element.116), channel_id=1, source_target_pairs={{0,2},{1,3},{2,0},{3,1},{4,6},{5,7},{6,4},{7,5},{8,10},{9,11},{10,... | collective-permute-start | bytes 294920 | tf_op jit(solution)/shard_map/ppermute | solution.py:295
  151.4 10.0 %collective-permute-start.32 = (bf16[128,640]{1,0:T(8,128)(2,1)S(1)}, bf16[128,640]{1,0:T(8,128)(2,1)S(1)}, u32[]{:S(2)}, u32[]{:S(2)}) collective-permute-start(bf16[128,640]{1,0:T(8,128)(2,1)S(1)} %pad_maximum_fusion.3), channel_id=1, source_target_pairs={{128,0},{144,16},{160,32},{176,48},{64,192},{80,208},{96,224},{112... | collective-permute-start | bytes 491528 | tf_op jit(solution)/shard_map/ppermute | solution.py:315
  161.4 13.0 %collective-permute-start.35 = (bf16[128,640]{1,0:T(8,128)(2,1)S(1)}, bf16[128,640]{1,0:T(8,128)(2,1)S(1)}, u32[]{:S(2)}, u32[]{:S(2)}) collective-permute-start(bf16[128,640]{1,0:T(8,128)(2,1)S(1)} %add_convert_fusion.6), channel_id=1, source_target_pairs={{0,32},{16,48},{32,64},{48,80},{192,224},{208,240},{224,128},{240,... | collective-permute-start | bytes 491528 | tf_op jit(solution)/shard_map/ppermute | solution.py:325
  163.3 11.1 %collective-permute-start.34 = (bf16[128,640]{1,0:T(8,128)(2,1)S(1)}, bf16[128,640]{1,0:T(8,128)(2,1)S(1)}, u32[]{:S(2)}, u32[]{:S(2)}) collective-permute-start(bf16[128,640]{1,0:T(8,128)(2,1)S(1)} %add_convert_fusion.6), channel_id=1, source_target_pairs={{0,64},{16,80},{32,96},{48,112},{192,128},{208,144},{224,160},{240... | collective-permute-start | bytes 491528 | tf_op jit(solution)/shard_map/ppermute | solution.py:325
  164.6 9.8 %collective-permute-start.33 = (bf16[128,640]{1,0:T(8,128)(2,1)S(1)}, bf16[128,640]{1,0:T(8,128)(2,1)S(1)}, u32[]{:S(2)}, u32[]{:S(2)}) collective-permute-start(bf16[128,640]{1,0:T(8,128)(2,1)S(1)} %add_convert_fusion.6), channel_id=1, source_target_pairs={{0,96},{16,112},{32,0},{48,16},{192,160},{208,176},{224,192},{240,... | collective-permute-start | bytes 491528 | tf_op jit(solution)/shard_map/ppermute | solution.py:325
  (34 other events, 179.2 us)
Sparse Core Ops, SparseCore 0:
  13.9 52.7 all-gather.1
  93.8 24.0 reduce-scatter.4
  120.6 50.2 reduce-scatter.2

commit v4 on v3

--- a/solution.py
+++ b/solution.py
@@ -364,8 +364,8 @@
     return (term.astype(f32) + to_owner(term).astype(f32)).astype(bf16)
 
 
-def share(total, x, role, *earlier):
-    copies = [total] + after([spread_x(total, k) for k in range(1, NX)], *earlier)
+def share(total, x, role):
+    copies = [total] + [spread_x(total, k) for k in range(1, NX)]
     items = []
     for sub in range(2):
         source = role * 2 + sub
@@ -428,7 +428,7 @@
         scalars=0,
         macs=tokens * flat[1] * 2 * wide,
         parts=[(0, flat[1])],
-    )(pair, *qkv_own, *qkv_other)
+    )(after(pair, cos_tab, sin_tab), *qkv_own, *qkv_other)
     o_own = [o_plane, o_near[0], take_y(after(o_plane, proj_own), 2), o_near[1]]
     o_other = [o_first] + [other_core(after(piece, proj_own)) for piece in o_own[1:]]
     proj_own, proj_other = after([proj_own, proj_other], *o_near)
@@ -494,7 +494,7 @@
         finish_kernel, [(flat, bf16)] * 2, 6, scratch_shapes=[pltpu.VMEM(flat, f32)]
     )(place, rows_own, gain, cot_own, weight, row_total)
     total = add_role(jnp.concatenate([gw_term, go_term], axis=1))
-    mine, theirs = share(total, x, role, grad_rows)
+    mine, theirs = share(total, x, role)
     g_0, g_1 = jnp.where(first, mine, theirs), jnp.where(first, theirs, mine)
 
     def pick(value, item, lo, hi):

time: 192 us -> 197 us (1.026)
  starting transfers between devices: 58.7 us -> 62.4 us
    ppermute x3, waiting for transfers between devices: 0.01 us -> 4.26 us  [spread_x(): return lax.ppermute(value, ('role', 'dp'), pairs)]
    ppermute x11, starting transfers between devices: 14.1 us -> 18 us  [other_core(): return lax.ppermute(value, 'dp', [(i, i ^ 1) for i in range(NX * NC)])]
    reduce_scatter x1, waiting for transfers between devices: 2.86 us -> 0.01 us  [scatter_x(): lax.psum_scatter(value, 'dp', scatter_dimension=0, tiled=True, axis_index...]
  transfers between devices with their start and end apart: 40 -> 40, of which waited for: 20 -> 22; matrix products, arithmetic and copies ran while one was open for 3% -> 5% of each run, Pallas kernels for 18% -> 16%
where the time goes in v4:
time: 197 us; the launch traced here: 196 us
  starting transfers between devices  62.4 us (32%)
  waiting for transfers between devices  60.1 us (31%)
  Pallas kernels  41.6 us (21%)
  between operations  14.3 us (7%)
  other arithmetic  9.78 us (5%)
  local copies, waits for them, and re-layouts  7.87 us (4%)
    ppermute x12, waiting for transfers between devices, take_z(): return lax.ppermute(value, 'fsdp', pairs)  20.4 us
    ppermute x11, starting transfers between devices, other_core(): return lax.ppermute(value, 'dp', [(i, i ^ 1) for i in range(NX * NC)])  18 us
    ppermute x9, starting transfers between devices, take_y(): return lax.ppermute(value, 'fsdp', pairs)  15.5 us
    ppermute x12, starting transfers between devices, take_z(): return lax.ppermute(value, 'fsdp', pairs)  13.9 us
    pallas_call x1, Pallas kernels, on_device(): call(back_kernel, [((tokens, wide), bf16)] * 2 + [((span, wide), bf16)] *...  10.9 us
    ppermute x9, waiting for transfers between devices, take_y(): return lax.ppermute(value, 'fsdp', pairs)  10.3 us
    ppermute x1, waiting for transfers between devices, to_owner(): return lax.ppermute(value, ('role', 'dp'), pairs)  8.67 us
    ppermute x11, waiting for transfers between devices, other_core(): return lax.ppermute(value, 'dp', [(i, i ^ 1) for i in range(NX * NC)])  8.65 us
  transfers between devices with their start and end apart: 40, of which 22 were waited for; matrix products, arithmetic and copies ran while one was open for 5% of the time, Pallas kernels for 16%

profile of v4, /device:TPU:35, one launch (start us, length us, event | category | flops | bytes accessed | tf_op | source)
XLA Modules:
  0.0 196.1 jit_solution(8933574582167697072)
XLA Ops:
  11.1 2.7 %shard_map.154 = bf16[256,2048]{1,0:T(8,128)(2,1)} custom-call(s32[2]{0:T(128)} %pad_add_fusion.place_ref, bf16[128,2048]{1,0:T(8,128)(2,1)} %bitcast.26, f32[1,2048]{1,0:T(1,128)} %bitcast.32, bf16[128,2048]{1,0:T(8,128)(2,1)} %bitcast.28, f32[128,1]{1,0:T(8,128)} %copy.19.weight_ref), custom_call_target="tpu_custom_call" | custom-call | bytes 1048576 | tf_op jit(solution)/shard_map/pallas_call | solution.py:408
  13.9 7.9 %collective-permute-start = (bf16[128,640]{1,0:T(8,128)(2,1)S(1)}, bf16[128,640]{1,0:T(8,128)(2,1)S(1)}, u32[]{:S(2)}, u32[]{:S(2)}) collective-permute-start(bf16[128,640]{1,0:T(8,128)(2,1)S(1)} %pad_maximum_fusion.2), channel_id=1, source_target_pairs={{0,128},{16,144},{32,160},{48,176},{192,64},{208,80},{224,96},{240... | collective-permute-start | bytes 491528 | tf_op jit(solution)/shard_map/ppermute | solution.py:309
  21.8 7.4 %collective-permute-done = bf16[128,640]{1,0:T(8,128)(2,1)S(1)} collective-permute-done((bf16[128,640]{1,0:T(8,128)(2,1)S(1)}, bf16[128,640]{1,0:T(8,128)(2,1)S(1)}, u32[]{:S(2)}, u32[]{:S(2)}) %collective-permute-start) | collective-permute-done | bytes 163872 | tf_op jit(solution)/shard_map/ppermute | solution.py:309
  36.4 3.5 %collective-permute-start.7 = (bf16[512,384]{1,0:T(8,128)(2,1)S(1)}, bf16[512,384]{1,0:T(8,128)(2,1)S(1)}, u32[]{:S(2)}, u32[]{:S(2)}) collective-permute-start(bf16[512,384]{1,0:T(8,128)(2,1)S(1)} %pad_maximum_fusion.refs_0_.refs_8_), channel_id=1, source_target_pairs={{0,16},{16,0},{32,48},{48,32},{64,80},{80,64},{96,112},{112,96},{1... | collective-permute-start | bytes 1179656 | tf_op jit(solution)/shard_map/ppermute | solution.py:299
  47.0 2.9 %collective-permute-done.8 = bf16[128,256]{1,0:T(8,128)(2,1)S(1)} collective-permute-done((bf16[128,256]{1,0:T(8,128)(2,1)S(1)}, bf16[128,256]{1,0:T(8,128)(2,1)S(1)}, u32[]{:S(2)}, u32[]{:S(2)}) %collective-permute-start.8) | collective-permute-done | bytes 65568 | tf_op jit(solution)/shard_map/ppermute | solution.py:295
  55.5 2.8 %collective-permute-start.11 = (bf16[512,256]{1,0:T(8,128)(2,1)}, bf16[512,256]{1,0:T(8,128)(2,1)S(1)}, u32[]{:S(2)}, u32[]{:S(2)}) collective-permute-start(bf16[512,256]{1,0:T(8,128)(2,1)} %constant_dynamic-update-slice_fusion.refs_0_), channel_id=1, source_target_pairs={{0,16},{16,0},{32,48},{48,32},{64,80},{80,64},{96,112},{112,96},{1... | collective-permute-start | bytes 786440 | tf_op jit(solution)/shard_map/ppermute | solution.py:299
  68.4 5.7 %shard_map.155 = (f32[512,384]{1,0:T(8,128)}, f32[512,384]{1,0:T(8,128)}) custom-call(bf16[4,2,128,2048]{3,2,1,0:T(8,128)(2,1)} %bitcast.22, bf16[512,384]{1,0:T(8,128)(2,1)} %copy-done.1, bf16[512,384]{1,0:T(8,128)(2,1)} %copy-done.5, bf16[512,384]{1,0:T(8,128)(2,1)} %copy-done.4, bf16[512,384]{1,0:T(8,128)(2,1)} %copy-done.3, bf16[512,384]{1,0:T(8,128)(2,1)} %copy-done.2, ...), custom_call_target="tpu_custom_call" | custom-call | flops 1610612736 | bytes 786432 | tf_op jit(solution)/shard_map/pallas_call | solution.py:424
  74.1 2.8 %collective-permute-start.17 = (bf16[512,256]{1,0:T(8,128)(2,1)}, bf16[512,256]{1,0:T(8,128)(2,1)S(1)}, u32[]{:S(2)}, u32[]{:S(2)}) collective-permute-start(bf16[512,256]{1,0:T(8,128)(2,1)} %constant_dynamic-update-slice_fusion.refs_0_), channel_id=1, source_target_pairs={{0,8},{1,9},{2,10},{3,11},{4,12},{5,13},{6,14},{7,15},{8,0},{9,1},... | collective-permute-start | bytes 786440 | tf_op jit(solution)/shard_map/ppermute | solution.py:290
  77.8 5.8 %shard_map.156 = (bf16[2048,128]{1,0:T(8,128)(2,1)}, bf16[512,128]{1,0:T(8,128)(2,1)}, bf16[512,128]{1,0:T(8,128)(2,1)}, f32[2048,128]{1,0:T(8,128)}, bf16[512,2...) custom-call(s32[1]{0:T(128)} %bitcast.6.first_ref, f32[512,384]{1,0:T(8,128)} %get-tuple-element.60.own_ref, ...), custom_call_target="tpu_custom_call" | custom-call | flops 536870912 | bytes 1048576 | tf_op jit(solution)/shard_map/pallas_call | solution.py:438
  83.7 4.5 %shard_map.157 = (bf16[2048,256]{1,0:T(8,128)(2,1)}, bf16[2048,256]{1,0:T(8,128)(2,1)}) custom-call(s32[2]{0:T(128)} %pad_add_fusion.place_ref, bf16[4,2,128,2048]{3,2,1,0:T(8,128)(2,1)} %bitcast.23, bf16[512,256]{1,0:T(8,128)(2,1)} %get-tuple-element.62.own_ref.mixed_own_ref, bf16[512,256]{1,0:T(8,128)(2,1)} %get-tuple-element.63.other_ref.mixed_other_ref), custom_call_target="tpu_custom_call" | custom-call | flops 1073741824 | bytes 2097152 | tf_op jit(solution)/shard_map/pallas_call | solution.py:445
  89.3 2.5 %collective-permute-done.21.refs_6_ = bf16[512,256]{1,0:T(8,128)(2,1)S(1)} collective-permute-done((bf16[512,256]{1,0:T(8,128)(2,1)S(1)}, bf16[512,256]{1,0:T(8,128)(2,1)S(1)}, u32[]{:S(2)}, u32[]{:S(2)}) %collective-permute-start.21) | collective-permute-done | bytes 262176 | tf_op jit(solution)/shard_map/ppermute | solution.py:299
  92.1 2.5 %add_convert_fusion = bf16[2048,256]{1,0:T(8,128)(2,1)} fusion(bf16[2048,256]{1,0:T(8,128)(2,1)S(1)} %collective-permute-done.20, bf16[2048,256]{1,0:T(8,128)(2,1)} %get-tuple-element.93), kind=kLoop, calls=%fused_computation | loop fusion | flops 2097152 | bytes 3145728 | tf_op jit(solution)/shard_map/convert_element_type | solution.py:453
  94.7 10.9 %shard_map.158 = (bf16[512,384]{1,0:T(8,128)(2,1)}, bf16[512,384]{1,0:T(8,128)(2,1)}, bf16[512,384]{1,0:T(8,128)(2,1)}, bf16[512,384]{1,0:T(8,128)(2,1)}, bf16[5...) custom-call(s32[1]{0:T(128)} %bitcast.6.first_ref, bf16[4,2,128,2048]{3,2,1,0:T(8,128)(2,1)} %bitcast.24, ...), custom_call_target="tpu_custom_call" | custom-call | flops 2684354560 | bytes 3932160 | tf_op jit(solution)/shard_map/pallas_call | solution.py:454
  105.6 8.5 %shard_map.159 = bf16[1024,2048]{1,0:T(8,128)(2,1)} custom-call(bf16[512,256]{1,0:T(8,128)(2,1)} %get-tuple-element.62.own_ref.mixed_own_ref, bf16[512,256]{1,0:T(8,128)(2,1)} %get-tuple-element.63.other_ref.mixed_other_ref, bf16[512,384]{1,0:T(8,128)(2,1)} %get-tuple-element.80.g_own_ref, bf16[512,384]{1,0:T(8,128)(2,1)} %get-tuple-element.81.g_other_ref, ...), custom_call_target="tpu_custom_call" | custom-call | flops 2684354560 | bytes 4194304 | tf_op jit(solution)/shard_map/pallas_call | solution.py:477
  114.6 3.2 %collective-permute-done.22 = bf16[2048,384]{1,0:T(8,128)(2,1)S(1)} collective-permute-done((bf16[2048,384]{1,0:T(8,128)(2,1)}, bf16[2048,384]{1,0:T(8,128)(2,1)S(1)}, u32[]{:S(2)}, u32[]{:S(2)}) %collective-permute-start.22) | collective-permute-done | bytes 1572896 | tf_op jit(solution)/shard_map/ppermute | solution.py:299
  121.0 8.9 %collective-permute-done.23 = bf16[512,384]{1,0:T(8,128)(2,1)S(1)} collective-permute-done((bf16[512,384]{1,0:T(8,128)(2,1)S(1)}, bf16[512,384]{1,0:T(8,128)(2,1)S(1)}, u32[]{:S(2)}, u32[]{:S(2)}) %collective-permute-start.23) | collective-permute-done | bytes 393248 | tf_op jit(solution)/shard_map/ppermute | solution.py:290
  138.0 3.0 %collective-permute-done.27 = bf16[128,256]{1,0:T(8,128)(2,1)S(1)} collective-permute-done((bf16[128,256]{1,0:T(8,128)(2,1)S(1)}, bf16[128,256]{1,0:T(8,128)(2,1)S(1)}, u32[]{:S(2)}, u32[]{:S(2)}) %collective-permute-start.27) | collective-permute-done | bytes 65568 | tf_op jit(solution)/shard_map/ppermute | solution.py:295
  144.4 2.5 %collective-permute-start.30 = (bf16[128,384]{1,0:T(8,128)(2,1)S(1)}, bf16[128,384]{1,0:T(8,128)(2,1)S(1)}, u32[]{:S(2)}, u32[]{:S(2)}) collective-permute-start(bf16[128,384]{1,0:T(8,128)(2,1)S(1)} %get-tuple-element.112), channel_id=1, source_target_pairs={{0,2},{1,3},{2,0},{3,1},{4,6},{5,7},{6,4},{7,5},{8,10},{9,11},{10,... | collective-permute-start | bytes 294920 | tf_op jit(solution)/shard_map/ppermute | solution.py:295
  146.9 2.5 %collective-permute-done.31 = bf16[128,384]{1,0:T(8,128)(2,1)S(1)} collective-permute-done((bf16[128,384]{1,0:T(8,128)(2,1)S(1)}, bf16[128,384]{1,0:T(8,128)(2,1)S(1)}, u32[]{:S(2)}, u32[]{:S(2)}) %collective-permute-start.31) | collective-permute-done | bytes 98336 | tf_op jit(solution)/shard_map/ppermute | solution.py:295
  149.4 3.8 %collective-permute-done.30 = bf16[128,384]{1,0:T(8,128)(2,1)S(1)} collective-permute-done((bf16[128,384]{1,0:T(8,128)(2,1)S(1)}, bf16[128,384]{1,0:T(8,128)(2,1)S(1)}, u32[]{:S(2)}, u32[]{:S(2)}) %collective-permute-start.30) | collective-permute-done | bytes 98336 | tf_op jit(solution)/shard_map/ppermute | solution.py:295
  154.6 8.7 %collective-permute-done.32 = bf16[128,640]{1,0:T(8,128)(2,1)S(1)} collective-permute-done((bf16[128,640]{1,0:T(8,128)(2,1)S(1)}, bf16[128,640]{1,0:T(8,128)(2,1)S(1)}, u32[]{:S(2)}, u32[]{:S(2)}) %collective-permute-start.32) | collective-permute-done | bytes 163872 | tf_op jit(solution)/shard_map/ppermute | solution.py:315
  163.3 2.5 %collective-permute-start.35 = (bf16[128,640]{1,0:T(8,128)(2,1)S(1)}, bf16[128,640]{1,0:T(8,128)(2,1)S(1)}, u32[]{:S(2)}, u32[]{:S(2)}) collective-permute-start(bf16[128,640]{1,0:T(8,128)(2,1)S(1)} %add_convert_fusion.6), channel_id=1, source_target_pairs={{0,96},{16,112},{32,0},{48,16},{192,160},{208,176},{224,192},{240,... | collective-permute-start | bytes 491528 | tf_op jit(solution)/shard_map/ppermute | solution.py:325
  173.5 7.9 %collective-permute-start.36 = (bf16[256,640]{1,0:T(8,128)(2,1)S(1)}, bf16[256,640]{1,0:T(8,128)(2,1)S(1)}, u32[]{:S(2)}, u32[]{:S(2)}) collective-permute-start(bf16[256,640]{1,0:T(8,128)(2,1)S(1)} %pad_maximum_fusion.1), channel_id=1, source_target_pairs={{0,16},{16,0},{32,48},{48,32},{64,80},{80,64},{96,112},{112,96},{1... | collective-permute-start | bytes 983048 | tf_op jit(solution)/shard_map/ppermute | solution.py:299
  186.1 3.5 %shard_map.160 = (bf16[128,2048]{1,0:T(8,128)(2,1)}, bf16[128,2048]{1,0:T(8,128)(2,1)}) custom-call(s32[2]{0:T(128)} %pad_add_fusion.place_ref, bf16[128,2048]{1,0:T(8,128)(2,1)} %bitcast.27, f32[1,2048]{1,0:T(1,128)} %bitcast.33, bf16[128,2048]{1,0:T(8,128)(2,1)} %bitcast.29, f32[128,1]{1,0:T(8,128)} %copy.19.weight_ref, ...), custom_call_target="tpu_custom_call" | custom-call | bytes 1048576 | tf_op jit(solution)/shard_map/pallas_call | solution.py:493
  (143 shorter events, 64.7 us)
Async XLA Ops:
  7.2 59.6 %all-gather.2.cloned.1.call-start = ((), (), s32[]{:S(2)}) async-start(), calls=%async_computation.2 | async-start | bytes 5242880 | tf_op jit(solution)/shard_map/all_gather | solution.py:270
  13.8 118.2 %reduce-scatter.5.cloned.1.call-start = ((), (), s32[]{:S(2)}) async-start(), calls=%async_computation.4 | async-start | bytes 1310720 | tf_op jit(solution)/shard_map/reduce_scatter | solution.py:277
  13.9 15.3 %collective-permute-start = (bf16[128,640]{1,0:T(8,128)(2,1)S(1)}, bf16[128,640]{1,0:T(8,128)(2,1)S(1)}, u32[]{:S(2)}, u32[]{:S(2)}) collective-permute-start(bf16[128,640]{1,0:T(8,128)(2,1)S(1)} %pad_maximum_fusion.2), channel_id=1, source_target_pairs={{0,128},{16,144},{32,160},{48,176},{192,64},{208,80},{224,96},{240... | collective-permute-start | bytes 491528 | tf_op jit(solution)/shard_map/ppermute | solution.py:309
  29.5 6.9 %collective-permute-start.1 = (bf16[128,384]{1,0:T(8,128)(2,1)S(1)}, bf16[128,384]{1,0:T(8,128)(2,1)S(1)}, u32[]{:S(2)}, u32[]{:S(2)}) collective-permute-start(bf16[128,384]{1,0:T(8,128)(2,1)S(1)} %slice.108), channel_id=1, source_target_pairs={{0,3},{1,0},{2,1},{3,2},{4,7},{5,4},{6,5},{7,6},{8,11},{9,8},{10,9... | collective-permute-start | bytes 294920 | tf_op jit(solution)/shard_map/ppermute | solution.py:295
  36.4 8.5 %collective-permute-start.7 = (bf16[512,384]{1,0:T(8,128)(2,1)S(1)}, bf16[512,384]{1,0:T(8,128)(2,1)S(1)}, u32[]{:S(2)}, u32[]{:S(2)}) collective-permute-start(bf16[512,384]{1,0:T(8,128)(2,1)S(1)} %pad_maximum_fusion.refs_0_.refs_8_), channel_id=1, source_target_pairs={{0,16},{16,0},{32,48},{48,32},{64,80},{80,64},{96,112},{112,96},{1... | collective-permute-start | bytes 1179656 | tf_op jit(solution)/shard_map/ppermute | solution.py:299
  39.9 18.4 %collective-permute-start.6 = (bf16[512,384]{1,0:T(8,128)(2,1)S(1)}, bf16[512,384]{1,0:T(8,128)(2,1)S(1)}, u32[]{:S(2)}, u32[]{:S(2)}) collective-permute-start(bf16[512,384]{1,0:T(8,128)(2,1)S(1)} %pad_maximum_fusion.refs_0_.refs_8_), channel_id=1, source_target_pairs={{0,4},{1,5},{2,6},{3,7},{4,8},{5,9},{6,10},{7,11},{8,12},{9,13},{1... | collective-permute-start | bytes 1179656 | tf_op jit(solution)/shard_map/ppermute | solution.py:290
  42.1 19.4 %collective-permute-start.5 = (bf16[512,384]{1,0:T(8,128)(2,1)S(1)}, bf16[512,384]{1,0:T(8,128)(2,1)S(1)}, u32[]{:S(2)}, u32[]{:S(2)}) collective-permute-start(bf16[512,384]{1,0:T(8,128)(2,1)S(1)} %pad_maximum_fusion.refs_0_.refs_8_), channel_id=1, source_target_pairs={{0,8},{1,9},{2,10},{3,11},{4,12},{5,13},{6,14},{7,15},{8,0},{9,1},... | collective-permute-start | bytes 1179656 | tf_op jit(solution)/shard_map/ppermute | solution.py:290
  43.8 18.5 %collective-permute-start.4 = (bf16[512,384]{1,0:T(8,128)(2,1)S(1)}, bf16[512,384]{1,0:T(8,128)(2,1)S(1)}, u32[]{:S(2)}, u32[]{:S(2)}) collective-permute-start(bf16[512,384]{1,0:T(8,128)(2,1)S(1)} %pad_maximum_fusion.refs_0_.refs_8_), channel_id=1, source_target_pairs={{0,12},{1,13},{2,14},{3,15},{4,0},{5,1},{6,2},{7,3},{8,4},{9,5},{1... | collective-permute-start | bytes 1179656 | tf_op jit(solution)/shard_map/ppermute | solution.py:290
  44.9 9.9 %collective-permute-start.10 = (bf16[128,256]{1,0:T(8,128)(2,1)S(1)}, bf16[128,256]{1,0:T(8,128)(2,1)S(1)}, u32[]{:S(2)}, u32[]{:S(2)}) collective-permute-start(bf16[128,256]{1,0:T(8,128)(2,1)S(1)} %slice.109), channel_id=1, source_target_pairs={{0,1},{1,2},{2,3},{3,0},{4,5},{5,6},{6,7},{7,4},{8,9},{9,10},{10,1... | collective-permute-start | bytes 196616 | tf_op jit(solution)/shard_map/ppermute | solution.py:295
  59.7 7.1 %collective-permute-start.14 = (bf16[512,384]{1,0:T(8,128)(2,1)S(1)}, bf16[512,384]{1,0:T(8,128)(2,1)S(1)}, u32[]{:S(2)}, u32[]{:S(2)}) collective-permute-start(bf16[512,384]{1,0:T(8,128)(2,1)S(1)} %collective-permute-done.6.refs_3_.refs_11_), channel_id=1, source_target_pairs={{0,16},{16,0},{32,48},{48,32},{64,80},{80,64},{96,112},{112,96},{1... | collective-permute-start | bytes 1179656 | tf_op jit(solution)/shard_map/ppermute | solution.py:299
  62.8 11.3 %collective-permute-start.16 = (bf16[512,256]{1,0:T(8,128)(2,1)}, bf16[512,256]{1,0:T(8,128)(2,1)}, u32[]{:S(2)}, u32[]{:S(2)}) collective-permute-start(bf16[512,256]{1,0:T(8,128)(2,1)} %constant_dynamic-update-slice_fusion.refs_0_), channel_id=1, source_target_pairs={{0,4},{1,5},{2,6},{3,7},{4,8},{5,9},{6,10},{7,11},{8,12},{9,13},{1... | collective-permute-start | bytes 786440 | tf_op jit(solution)/shard_map/ppermute | solution.py:290
  63.7 10.4 %collective-permute-start.15 = (bf16[512,256]{1,0:T(8,128)(2,1)}, bf16[512,256]{1,0:T(8,128)(2,1)}, u32[]{:S(2)}, u32[]{:S(2)}) collective-permute-start(bf16[512,256]{1,0:T(8,128)(2,1)} %constant_dynamic-update-slice_fusion.refs_0_), channel_id=1, source_target_pairs={{0,12},{1,13},{2,14},{3,15},{4,0},{5,1},{6,2},{7,3},{8,4},{9,5},{1... | collective-permute-start | bytes 786440 | tf_op jit(solution)/shard_map/ppermute | solution.py:290
  74.1 9.6 %collective-permute-start.17 = (bf16[512,256]{1,0:T(8,128)(2,1)}, bf16[512,256]{1,0:T(8,128)(2,1)S(1)}, u32[]{:S(2)}, u32[]{:S(2)}) collective-permute-start(bf16[512,256]{1,0:T(8,128)(2,1)} %constant_dynamic-update-slice_fusion.refs_0_), channel_id=1, source_target_pairs={{0,8},{1,9},{2,10},{3,11},{4,12},{5,13},{6,14},{7,15},{8,0},{9,1},... | collective-permute-start | bytes 786440 | tf_op jit(solution)/shard_map/ppermute | solution.py:290
  76.9 6.8 %collective-permute-start.18 = (bf16[512,256]{1,0:T(8,128)(2,1)}, bf16[512,256]{1,0:T(8,128)(2,1)S(1)}, u32[]{:S(2)}, u32[]{:S(2)}) collective-permute-start(bf16[512,256]{1,0:T(8,128)(2,1)} %collective-permute-done.15.refs_1_), channel_id=1, source_target_pairs={{0,16},{16,0},{32,48},{48,32},{64,80},{80,64},{96,112},{112,96},{1... | collective-permute-start | bytes 786440 | tf_op jit(solution)/shard_map/ppermute | solution.py:299
  94.6 91.4 %reduce-scatter.3.cloned.1.call-start = ((), (), s32[]{:S(2)}) async-start(), calls=%async_computation.3 | async-start | bytes 5242880 | tf_op jit(solution)/shard_map/reduce_scatter | solution.py:283
  118.3 11.6 %collective-permute-start.23 = (bf16[512,384]{1,0:T(8,128)(2,1)S(1)}, bf16[512,384]{1,0:T(8,128)(2,1)S(1)}, u32[]{:S(2)}, u32[]{:S(2)}) collective-permute-start(bf16[512,384]{1,0:T(8,128)(2,1)S(1)} %get-tuple-element.89), channel_id=1, source_target_pairs={{0,4},{1,5},{2,6},{3,7},{4,8},{5,9},{6,10},{7,11},{8,12},{9,13},{1... | collective-permute-start | bytes 1179656 | tf_op jit(solution)/shard_map/ppermute | solution.py:290
  119.5 10.3 %collective-permute-start.24 = (bf16[512,384]{1,0:T(8,128)(2,1)S(1)}, bf16[512,384]{1,0:T(8,128)(2,1)S(1)}, u32[]{:S(2)}, u32[]{:S(2)}) collective-permute-start(bf16[512,384]{1,0:T(8,128)(2,1)S(1)} %get-tuple-element.90), channel_id=1, source_target_pairs={{0,12},{1,13},{2,14},{3,15},{4,0},{5,1},{6,2},{7,3},{8,4},{9,5},{1... | collective-permute-start | bytes 1179656 | tf_op jit(solution)/shard_map/ppermute | solution.py:290
  129.9 12.0 %collective-permute-start.25 = (bf16[512,384]{1,0:T(8,128)(2,1)S(1)}, bf16[512,384]{1,0:T(8,128)(2,1)S(1)}, u32[]{:S(2)}, u32[]{:S(2)}) collective-permute-start(bf16[512,384]{1,0:T(8,128)(2,1)S(1)} %get-tuple-element.92), channel_id=1, source_target_pairs={{0,8},{1,9},{2,10},{3,11},{4,12},{5,13},{6,14},{7,15},{8,0},{9,1},... | collective-permute-start | bytes 1179656 | tf_op jit(solution)/shard_map/ppermute | solution.py:290
  142.4 7.0 %collective-permute-start.31 = (bf16[128,384]{1,0:T(8,128)(2,1)S(1)}, bf16[128,384]{1,0:T(8,128)(2,1)S(1)}, u32[]{:S(2)}, u32[]{:S(2)}) collective-permute-start(bf16[128,384]{1,0:T(8,128)(2,1)S(1)} %get-tuple-element.111), channel_id=1, source_target_pairs={{0,3},{1,0},{2,1},{3,2},{4,7},{5,4},{6,5},{7,6},{8,11},{9,8},{10,9... | collective-permute-start | bytes 294920 | tf_op jit(solution)/shard_map/ppermute | solution.py:295
  144.4 8.9 %collective-permute-start.30 = (bf16[128,384]{1,0:T(8,128)(2,1)S(1)}, bf16[128,384]{1,0:T(8,128)(2,1)S(1)}, u32[]{:S(2)}, u32[]{:S(2)}) collective-permute-start(bf16[128,384]{1,0:T(8,128)(2,1)S(1)} %get-tuple-element.112), channel_id=1, source_target_pairs={{0,2},{1,3},{2,0},{3,1},{4,6},{5,7},{6,4},{7,5},{8,10},{9,11},{10,... | collective-permute-start | bytes 294920 | tf_op jit(solution)/shard_map/ppermute | solution.py:295
  153.3 10.0 %collective-permute-start.32 = (bf16[128,640]{1,0:T(8,128)(2,1)S(1)}, bf16[128,640]{1,0:T(8,128)(2,1)S(1)}, u32[]{:S(2)}, u32[]{:S(2)}) collective-permute-start(bf16[128,640]{1,0:T(8,128)(2,1)S(1)} %pad_maximum_fusion.3), channel_id=1, source_target_pairs={{128,0},{144,16},{160,32},{176,48},{64,192},{80,208},{96,224},{112... | collective-permute-start | bytes 491528 | tf_op jit(solution)/shard_map/ppermute | solution.py:315
  163.3 7.6 %collective-permute-start.35 = (bf16[128,640]{1,0:T(8,128)(2,1)S(1)}, bf16[128,640]{1,0:T(8,128)(2,1)S(1)}, u32[]{:S(2)}, u32[]{:S(2)}) collective-permute-start(bf16[128,640]{1,0:T(8,128)(2,1)S(1)} %add_convert_fusion.6), channel_id=1, source_target_pairs={{0,96},{16,112},{32,0},{48,16},{192,160},{208,176},{224,192},{240,... | collective-permute-start | bytes 491528 | tf_op jit(solution)/shard_map/ppermute | solution.py:325
  165.8 6.8 %collective-permute-start.34 = (bf16[128,640]{1,0:T(8,128)(2,1)S(1)}, bf16[128,640]{1,0:T(8,128)(2,1)S(1)}, u32[]{:S(2)}, u32[]{:S(2)}) collective-permute-start(bf16[128,640]{1,0:T(8,128)(2,1)S(1)} %add_convert_fusion.6), channel_id=1, source_target_pairs={{0,64},{16,80},{32,96},{48,112},{192,128},{208,144},{224,160},{240... | collective-permute-start | bytes 491528 | tf_op jit(solution)/shard_map/ppermute | solution.py:325
  173.5 9.2 %collective-permute-start.36 = (bf16[256,640]{1,0:T(8,128)(2,1)S(1)}, bf16[256,640]{1,0:T(8,128)(2,1)S(1)}, u32[]{:S(2)}, u32[]{:S(2)}) collective-permute-start(bf16[256,640]{1,0:T(8,128)(2,1)S(1)} %pad_maximum_fusion.1), channel_id=1, source_target_pairs={{0,16},{16,0},{32,48},{48,32},{64,80},{80,64},{96,112},{112,96},{1... | collective-permute-start | bytes 983048 | tf_op jit(solution)/shard_map/ppermute | solution.py:299
  (34 other events, 182.4 us)
Sparse Core Ops, SparseCore 0:
  13.9 52.7 all-gather.1
  94.7 25.3 reduce-scatter.4
  122.9 49.3 reduce-scatter.2
